TPU v7x, 256 devices: a whole 4x4x8 slice. The times are simulated.
256 devices in a mesh: inner: 8 (over y_hi, x), outer: 16 (over y_lo, z), head: 2 (over core).
Axes of the slice: x: 4, y: 4 (y_hi: 2, y_lo: 2; y = y_hi * 2 + y_lo), z: 8, core: 2. Of those that a mesh axis runs over, the one named last changes fastest.
Arguments:
- queries: bfloat16 [16384, 4096], P(('inner', 'outer'), 'head'), may hold values from -6 to 6
- out_grad: bfloat16 [16384, 4096], P(('inner', 'outer'), 'head'), may hold values from -6 to 6
- outputs: bfloat16 [16384, 4096], P(('inner', 'outer'), 'head'), may hold values from -4 to 4
- log_norm: float32 [32, 16384], P('head', ('inner', 'outer')), may hold values from 4 to 6
- kv_held: bfloat16 [16384, 2, 512], P(('inner', 'outer'), None, 'head'), may hold values from -6 to 6
- span_order: int32 [256], replicated, may hold values from 0 to 255, each once
- dq_acc: float32 [16384, 4096], P(('inner', 'outer'), 'head'), may hold values from -6 to 6
- dkv_acc: float32 [16384, 2, 512], P(('inner', 'outer'), None, 'head'), may hold values from -6 to 6
- kv_weight: bfloat16 [8192, 2, 512], P(('inner', 'outer'), None, 'head'), may hold values from -0.1875 to 0.1875
Outputs:
- dq: float32 [16384, 4096], P(('inner', 'outer'), 'head')
- dkv: float32 [16384, 2, 512], P(('inner', 'outer'), None, 'head')
- dx: bfloat16 [16384, 8192], P(('inner', 'outer'), 'head')
Inputs may be any that keep to these rules, and one draw needn't show every extreme that they name: `span_order`: every block number appears exactly once.
All inputs are finite; a program needn't handle non-finite values.
Results may differ from a plain program's by a relative error of at most 0.0056.
Values may be sent and summed in bfloat16 or wider, within the bound.
No kernel may reach another device: no remote copies, remote signals or barrier semaphores. Data moves between devices by JAX's collectives and lax.ppermute only.
A program may use at most 128 MiB of HBM per device.

v0:
```python
import math

import jax
import jax.numpy as jnp
from jax import lax
from jax.sharding import PartitionSpec as P

HD = 128
SPAN = 64


def from_behind(value, axis, steps):
    count = lax.axis_size(axis)
    pairs = [(source, (source + steps) % count) for source in range(count)]
    return lax.ppermute(value, axis, pairs)


def shards(queries, out_grad, outputs, log_norm, kv_held, span_order, dq_acc, dkv_acc, kv_weight):
    rows = queries.shape[0]
    kv_dev = kv_held.shape[2] // HD
    q_dev = queries.shape[1] // HD
    group_size = q_dev // kv_dev
    scale = 1.0 / math.sqrt(HD)
    n_inner = lax.axis_size("inner")
    n_outer = lax.axis_size("outer")
    inner_at = lax.axis_index("inner")
    outer_at = lax.axis_index("outer")
    key_outer = (outer_at + 1) % n_outer
    offsets = jnp.arange(SPAN, dtype=jnp.int32)

    def block_positions(block):
        spans = lax.dynamic_slice(span_order, (2 * block,), (2,))
        return (spans[:, None] * SPAN + offsets[None, :]).reshape(-1)

    q_pos = block_positions(inner_at * n_outer + outer_at)
    q4 = queries.reshape(rows, kv_dev, group_size, HD)
    do4 = out_grad.reshape(rows, kv_dev, group_size, HD)
    o4 = outputs.reshape(rows, kv_dev, group_size, HD)
    delta = jnp.einsum("tkgc,tkgc->kgt", do4, o4, preferred_element_type=jnp.float32)
    lse3 = log_norm.reshape(kv_dev, group_size, rows)
    held = kv_held
    carried = jnp.zeros(kv_held.shape, jnp.float32)
    dq_sum = jnp.zeros(queries.shape, jnp.float32)
    for step in range(n_inner):
        source = (inner_at - step) % n_inner
        k_pos = block_positions(source * n_outer + key_outer)
        width = held.shape[0]
        keys = held[:, 0].reshape(width, kv_dev, HD)
        values = held[:, 1].reshape(width, kv_dev, HD)
        allowed = k_pos[None, :] <= q_pos[:, None]
        scores = jnp.einsum("tkgc,ukc->kgtu", q4, keys, preferred_element_type=jnp.float32) * scale
        prob = jnp.where(allowed[None, None], jnp.exp(scores - lse3[..., None]), 0.0)
        dprob = jnp.einsum("tkgc,ukc->kgtu", do4, values, preferred_element_type=jnp.float32)
        dscore = (prob * (dprob - delta[..., None])).astype(jnp.bfloat16)
        probb = prob.astype(jnp.bfloat16)
        dq_term = (
            jnp.einsum("kgtu,ukc->tkgc", dscore, keys, preferred_element_type=jnp.float32) * scale
        )
        dk_term = (
            jnp.einsum("kgtu,tkgc->ukc", dscore, q4, preferred_element_type=jnp.float32) * scale
        )
        dv_term = jnp.einsum("kgtu,tkgc->ukc", probb, do4, preferred_element_type=jnp.float32)
        dkv_term = jnp.stack(
            [dk_term.reshape(width, kv_dev * HD), dv_term.reshape(width, kv_dev * HD)], axis=1
        )
        dq_term, dkv_term = (dq_term.reshape(rows, q_dev * HD), dkv_term)
        dq_sum = dq_sum + dq_term
        carried = from_behind(carried + dkv_term, "inner", 1)
        if step + 1 < n_inner:
            held = from_behind(held, "inner", 1)
    arrived = from_behind(carried, "outer", 1)
    dkv = dkv_acc + arrived
    dq = dq_acc + dq_sum
    dkv_rounded = dkv.astype(jnp.bfloat16)
    dkvb = dkv_rounded.reshape(rows, 2 * kv_dev * HD)
    piece = lax.all_gather(kv_weight, ("inner", "outer"), axis=0, tiled=True)
    flat = piece.reshape(piece.shape[0], 2 * kv_dev * HD)
    partial_dx = jnp.einsum("ts,ds->td", dkvb, flat, preferred_element_type=jnp.float32)
    dx = lax.psum_scatter(partial_dx, "head", scatter_dimension=1, tiled=True).astype(jnp.bfloat16)
    return (dq, dkv, dx)


def solution(mesh):
    return jax.shard_map(
        shards,
        mesh=mesh,
        in_specs=(
            P(("inner", "outer"), "head"),
            P(("inner", "outer"), "head"),
            P(("inner", "outer"), "head"),
            P("head", ("inner", "outer")),
            P(("inner", "outer"), None, "head"),
            P(),
            P(("inner", "outer"), "head"),
            P(("inner", "outer"), None, "head"),
            P(("inner", "outer"), None, "head"),
        ),
        out_specs=(
            P(("inner", "outer"), "head"),
            P(("inner", "outer"), None, "head"),
            P(("inner", "outer"), "head"),
        ),
        check_vma=False,
    )
```

profile of v0, /device:TPU:1, one launch (start us, length us, event | category | flops | bytes accessed | tf_op | source)
XLA Modules:
  0.0 712.8 jit_solution(16785417713915998784)
XLA Ops:
  9.8 2.1 collective-permute-start
  26.1 6.6 collective-permute-done.7
  33.7 2.9 collective-permute-done.1
  41.0 8.5 %collective-permute-done.2 = bf16[128,2,256]{0,2,1:T(8,128)(2,1)} collective-permute-done((bf16[128,2,256]{0,2,1:T(8,128)(2,1)}, bf16[128,2,256]{0,2,1:T(8,128)(2,1)}, u32[]{:S(2)}, u32[]{:S(2)}) %collective-permute-start.2) | collective-permute-done | bytes 131104 | tf_op jit(solution)/shard_map/ppermute | solution.py:15
  53.9 1.9 maximum_add_fusion.1
  55.9 6.1 collective-permute-done.3
  64.7 1.7 copy.168
  68.6 6.0 collective-permute-done.4
  79.1 1.9 maximum_add_fusion.2
  81.0 6.2 collective-permute-done.5
  92.5 1.7 copy.179
  94.1 3.3 collective-permute-done.6
  100.9 8.3 %collective-permute-done.11 = f32[128,2,256]{2,1,0:T(2,128)S(1)} collective-permute-done((f32[128,2,256]{2,1,0:T(2,128)S(1)}, f32[128,2,256]{2,1,0:T(2,128)S(1)}, u32[]{:S(2)}, u32[]{:S(2)}) %collective-permute-start.11) | collective-permute-done | bytes 262176 | tf_op jit(solution)/shard_map/ppermute | solution.py:15
  111.8 10.1 %collective-permute-done.12 = f32[128,2,256]{2,1,0:T(2,128)S(1)} collective-permute-done((f32[128,2,256]{2,1,0:T(2,128)S(1)}, f32[128,2,256]{2,1,0:T(2,128)S(1)}, u32[]{:S(2)}, u32[]{:S(2)}) %collective-permute-start.12) | collective-permute-done | bytes 262176 | tf_op jit(solution)/shard_map/ppermute | solution.py:15
  121.8 2.0 maximum_add_fusion.5
  127.2 8.0 %collective-permute-done.13 = f32[128,2,256]{2,1,0:T(2,128)} collective-permute-done((f32[128,2,256]{2,1,0:T(2,128)}, f32[128,2,256]{2,1,0:T(2,128)}, u32[]{:S(2)}, u32[]{:S(2)}) %collective-permute-start.13) | collective-permute-done | bytes 262176 | tf_op jit(solution)/shard_map/ppermute | solution.py:15
  136.8 12.4 %collective-permute-done.14 = f32[128,2,256]{2,1,0:T(2,128)S(1)} collective-permute-done((f32[128,2,256]{2,1,0:T(2,128)S(1)}, f32[128,2,256]{2,1,0:T(2,128)S(1)}, u32[]{:S(2)}, u32[]{:S(2)}) %collective-permute-start.14) | collective-permute-done | bytes 262176 | tf_op jit(solution)/shard_map/ppermute | solution.py:15
  149.2 10.0 %collective-permute-done.15 = f32[128,2,256]{2,1,0:T(2,128)S(1)} collective-permute-done((f32[128,2,256]{2,1,0:T(2,128)S(1)}, f32[128,2,256]{2,1,0:T(2,128)S(1)}, u32[]{:S(2)}, u32[]{:S(2)}) %collective-permute-start.15) | collective-permute-done | bytes 262176 | tf_op jit(solution)/shard_map/ppermute | solution.py:15
  159.2 1.8 fusion.83
  161.1 432.3 %all-gather.2.cloned.1.call-done = bf16[8192,2,256]{2,0,1:T(8,128)(2,1)} async-done(((bf16[64,2,256]{2,0,1:T(8,128)(2,1)}), bf16[8192,2,256]{2,0,1:T(8,128)(2,1)}) %all-gather.2.cloned.1.call-update) | async-done | bytes 8388624 | tf_op jit(solution)/shard_map/all_gather | solution.py:76
  593.3 8.3 %convolution_bitcast_fusion = f32[128,8192]{1,0:T(8,128)} fusion(bf16[8192,2,256]{2,0,1:T(8,128)(2,1)} %all-gather.2.cloned.1.call-done, bf16[128,2,256]{2,1,0:T(2,128)(2,1)S(1)} %get-tuple-element.3), kind=kOutput, calls=%fused_computation | convolution fusion | flops 1073741824 | bytes 12713984 | tf_op jit(solution)/shard_map/ts,ds->td/dot_general | solution.py:78
  604.5 2.3 add.406
  606.9 96.4 %reduce-scatter.2.cloned.1.call-done = f32[128,4096]{1,0:T(8,128)} async-done(((f32[128,8192]{1,0:T(8,128)}), f32[128,4096]{1,0:T(8,128)}) %reduce-scatter.2.cloned.1.call-update) | async-done | bytes 2097168 | tf_op jit(solution)/shard_map/reduce_scatter | solution.py:79
  703.2 2.7 convert_element_type.71
  (155 shorter events, 54.6 us)
Async XLA Ops:
  7.2 16.3 %copy-start.13 = (f32[16,128]{1,0:T(8,128)S(1)}, f32[16,128]{1,0:T(8,128)}, u32[]{:S(2)}) copy-start(f32[16,128]{1,0:T(8,128)} %param.12) | copy-start | bytes 24580
  7.2 586.2 %all-gather.2.cloned.1.call-start = ((), (), s32[]{:S(2)}) async-start(), calls=%async_computation.1 | async-start | bytes 8454144 | tf_op jit(solution)/shard_map/all_gather | solution.py:76
  8.7 694.5 %reduce-scatter.2.cloned.1.call-start = ((), (), s32[]{:S(2)}) async-start(), calls=%async_computation.2 | async-start | bytes 6291456 | tf_op jit(solution)/shard_map/reduce_scatter | solution.py:79
  9.8 13.7 %collective-permute-start = (bf16[128,2,256]{0,2,1:T(8,128)(2,1)S(1)}, bf16[128,2,256]{0,2,1:T(8,128)(2,1)S(1)}, u32[]{:S(2)}, u32[]{:S(2)}) collective-permute-start(bf16[128,2,256]{0,2,1:T(8,128)(2,1)S(1)} %copy.95), channel_id=1, source_target_pairs={{0,32},{32,64},{64,96},{96,128},{128,160},{160,192},{192,224},{224... | collective-permute-start | bytes 393224 | tf_op jit(solution)/shard_map/ppermute | solution.py:15
  22.2 10.5 %collective-permute-start.7 = (f32[128,2,256]{2,1,0:T(2,128)S(1)}, f32[128,2,256]{2,1,0:T(2,128)S(1)}, u32[]{:S(2)}, u32[]{:S(2)}) collective-permute-start(f32[128,2,256]{2,1,0:T(2,128)S(1)} %pad_maximum_fusion), channel_id=1, source_target_pairs={{0,32},{32,64},{64,96},{96,128},{128,160},{160,192},{192,224},{224... | collective-permute-start | bytes 786440 | tf_op jit(solution)/shard_map/ppermute | solution.py:15
  25.1 11.5 %collective-permute-start.1 = (bf16[128,2,256]{0,2,1:T(8,128)(2,1)S(1)}, bf16[128,2,256]{0,2,1:T(8,128)(2,1)S(1)}, u32[]{:S(2)}, u32[]{:S(2)}) collective-permute-start(bf16[128,2,256]{0,2,1:T(8,128)(2,1)S(1)} %collective-permute-done), channel_id=1, source_target_pairs={{0,32},{32,64},{64,96},{96,128},{128,160},{160,192},{192,224},{224... | collective-permute-start | bytes 393224 | tf_op jit(solution)/shard_map/ppermute | solution.py:15
  33.7 20.2 %collective-permute-start.8 = (f32[128,2,256]{2,1,0:T(2,128)}, f32[128,2,256]{2,1,0:T(2,128)}, u32[]{:S(2)}, u32[]{:S(2)}) collective-permute-start(f32[128,2,256]{2,1,0:T(2,128)} %maximum_add_fusion), channel_id=1, source_target_pairs={{0,32},{32,64},{64,96},{96,128},{128,160},{160,192},{192,224},{224... | collective-permute-start | bytes 786440 | tf_op jit(solution)/shard_map/ppermute | solution.py:15
  39.4 10.0 %collective-permute-start.2 = (bf16[128,2,256]{0,2,1:T(8,128)(2,1)}, bf16[128,2,256]{0,2,1:T(8,128)(2,1)}, u32[]{:S(2)}, u32[]{:S(2)}) collective-permute-start(bf16[128,2,256]{0,2,1:T(8,128)(2,1)} %copy-done.17), channel_id=1, source_target_pairs={{0,32},{32,64},{64,96},{96,128},{128,160},{160,192},{192,224},{224... | collective-permute-start | bytes 393224 | tf_op jit(solution)/shard_map/ppermute | solution.py:15
  40.5 13.4 %copy-start.16 = (f32[128,1,256]{2,1,0:T(1,128)S(1)}, f32[128,1,256]{2,1,0:T(1,128)}, u32[]{:S(2)}) copy-start(f32[128,1,256]{2,1,0:T(1,128)} %copy.156) | copy-start | bytes 393220
  53.9 8.1 %collective-permute-start.3 = (bf16[128,2,256]{0,2,1:T(8,128)(2,1)}, bf16[128,2,256]{0,2,1:T(8,128)(2,1)S(1)}, u32[]{:S(2)}, u32[]{:S(2)}) collective-permute-start(bf16[128,2,256]{0,2,1:T(8,128)(2,1)} %collective-permute-done.2), channel_id=1, source_target_pairs={{0,32},{32,64},{64,96},{96,128},{128,160},{160,192},{192,224},{224... | collective-permute-start | bytes 393224 | tf_op jit(solution)/shard_map/ppermute | solution.py:15
  55.9 23.2 %collective-permute-start.9 = (f32[128,2,256]{2,1,0:T(2,128)}, f32[128,2,256]{2,1,0:T(2,128)}, u32[]{:S(2)}, u32[]{:S(2)}) collective-permute-start(f32[128,2,256]{2,1,0:T(2,128)} %maximum_add_fusion.1), channel_id=1, source_target_pairs={{0,32},{32,64},{64,96},{96,128},{128,160},{160,192},{192,224},{224... | collective-permute-start | bytes 786440 | tf_op jit(solution)/shard_map/ppermute | solution.py:15
  66.4 8.2 %collective-permute-start.4 = (bf16[128,2,256]{0,2,1:T(8,128)(2,1)}, bf16[128,2,256]{0,2,1:T(8,128)(2,1)}, u32[]{:S(2)}, u32[]{:S(2)}) collective-permute-start(bf16[128,2,256]{0,2,1:T(8,128)(2,1)} %copy-done.18), channel_id=1, source_target_pairs={{0,32},{32,64},{64,96},{96,128},{128,160},{160,192},{192,224},{224... | collective-permute-start | bytes 393224 | tf_op jit(solution)/shard_map/ppermute | solution.py:15
  67.5 11.5 %copy-start.14 = (f32[128,1,256]{2,1,0:T(1,128)S(1)}, f32[128,1,256]{2,1,0:T(1,128)}, u32[]{:S(2)}) copy-start(f32[128,1,256]{2,1,0:T(1,128)} %copy.162) | copy-start | bytes 393220
  67.5 11.5 %copy-start.15 = (f32[128,1,256]{2,1,0:T(1,128)S(1)}, f32[128,1,256]{2,1,0:T(1,128)}, u32[]{:S(2)}) copy-start(f32[128,1,256]{2,1,0:T(1,128)} %copy.161) | copy-start | bytes 393220
  67.5 20.6 %copy-start.19 = (pred[128,128]{0,1:T(8,128)(4,1)S(1)}, pred[128,128]{0,1:T(8,128)(4,1)}, u32[]{:S(2)}) copy-start(pred[128,128]{0,1:T(8,128)(4,1)} %get-tuple-element.36) | copy-start | bytes 49156
  79.0 8.2 %collective-permute-start.5 = (bf16[128,2,256]{0,2,1:T(8,128)(2,1)}, bf16[128,2,256]{0,2,1:T(8,128)(2,1)}, u32[]{:S(2)}, u32[]{:S(2)}) collective-permute-start(bf16[128,2,256]{0,2,1:T(8,128)(2,1)} %collective-permute-done.4), channel_id=1, source_target_pairs={{0,32},{32,64},{64,96},{96,128},{128,160},{160,192},{192,224},{224... | collective-permute-start | bytes 393224 | tf_op jit(solution)/shard_map/ppermute | solution.py:15
  81.0 17.3 %collective-permute-start.10 = (f32[128,2,256]{2,1,0:T(2,128)}, f32[128,2,256]{2,1,0:T(2,128)}, u32[]{:S(2)}, u32[]{:S(2)}) collective-permute-start(f32[128,2,256]{2,1,0:T(2,128)} %maximum_add_fusion.2), channel_id=1, source_target_pairs={{0,32},{32,64},{64,96},{96,128},{128,160},{160,192},{192,224},{224... | collective-permute-start | bytes 786440 | tf_op jit(solution)/shard_map/ppermute | solution.py:15
  87.2 10.2 %collective-permute-start.6 = (bf16[128,2,256]{0,2,1:T(8,128)(2,1)}, bf16[128,2,256]{0,2,1:T(8,128)(2,1)}, u32[]{:S(2)}, u32[]{:S(2)}) collective-permute-start(bf16[128,2,256]{0,2,1:T(8,128)(2,1)} %collective-permute-done.5), channel_id=1, source_target_pairs={{0,32},{32,64},{64,96},{96,128},{128,160},{160,192},{192,224},{224... | collective-permute-start | bytes 393224 | tf_op jit(solution)/shard_map/ppermute | solution.py:15
  89.9 503.5 %copy-start.6 = (bf16[2,8,128,128]{2,3,1,0:T(8,128)(2,1)}, bf16[2,8,128,128]{2,3,1,0:T(8,128)(2,1)S(1)}, u32[]{:S(2)}) copy-start(bf16[2,8,128,128]{2,3,1,0:T(8,128)(2,1)S(1)} %fusion.50) | copy-start | bytes 1572868
  99.7 9.5 %collective-permute-start.11 = (f32[128,2,256]{2,1,0:T(2,128)S(1)}, f32[128,2,256]{2,1,0:T(2,128)S(1)}, u32[]{:S(2)}, u32[]{:S(2)}) collective-permute-start(f32[128,2,256]{2,1,0:T(2,128)S(1)} %maximum_add_fusion.3), channel_id=1, source_target_pairs={{0,32},{32,64},{64,96},{96,128},{128,160},{160,192},{192,224},{224... | collective-permute-start | bytes 786440 | tf_op jit(solution)/shard_map/ppermute | solution.py:15
  110.5 11.3 %collective-permute-start.12 = (f32[128,2,256]{2,1,0:T(2,128)S(1)}, f32[128,2,256]{2,1,0:T(2,128)S(1)}, u32[]{:S(2)}, u32[]{:S(2)}) collective-permute-start(f32[128,2,256]{2,1,0:T(2,128)S(1)} %maximum_add_fusion.4), channel_id=1, source_target_pairs={{0,32},{32,64},{64,96},{96,128},{128,160},{160,192},{192,224},{224... | collective-permute-start | bytes 786440 | tf_op jit(solution)/shard_map/ppermute | solution.py:15
  123.8 11.5 %collective-permute-start.13 = (f32[128,2,256]{2,1,0:T(2,128)}, f32[128,2,256]{2,1,0:T(2,128)}, u32[]{:S(2)}, u32[]{:S(2)}) collective-permute-start(f32[128,2,256]{2,1,0:T(2,128)} %maximum_add_fusion.5), channel_id=1, source_target_pairs={{0,32},{32,64},{64,96},{96,128},{128,160},{160,192},{192,224},{224... | collective-permute-start | bytes 786440 | tf_op jit(solution)/shard_map/ppermute | solution.py:15
  136.5 12.7 %collective-permute-start.14 = (f32[128,2,256]{2,1,0:T(2,128)S(1)}, f32[128,2,256]{2,1,0:T(2,128)S(1)}, u32[]{:S(2)}, u32[]{:S(2)}) collective-permute-start(f32[128,2,256]{2,1,0:T(2,128)S(1)} %maximum_add_fusion.6), channel_id=1, source_target_pairs={{0,32},{32,64},{64,96},{96,128},{128,160},{160,192},{192,224},{224... | collective-permute-start | bytes 786440 | tf_op jit(solution)/shard_map/ppermute | solution.py:15
  149.2 10.0 %collective-permute-start.15 = (f32[128,2,256]{2,1,0:T(2,128)S(1)}, f32[128,2,256]{2,1,0:T(2,128)S(1)}, u32[]{:S(2)}, u32[]{:S(2)}) collective-permute-start(f32[128,2,256]{2,1,0:T(2,128)S(1)} %collective-permute-done.14), channel_id=1, source_target_pairs={{0,2},{2,4},{4,6},{6,8},{8,10},{10,12},{12,14},{14,16},{16,18},{18... | collective-permute-start | bytes 786440 | tf_op jit(solution)/shard_map/ppermute | solution.py:15
  (14 other events, 35.0 us)
Sparse Core Ops, SparseCore 0:
  9.8 583.4 all-gather.1
  601.8 101.4 reduce-scatter.1
where the time goes:
time: 714 us; the launch traced here: 713 us
  waiting for transfers between devices  617 us (86%)
  matrix products  30 us (4%)
  local copies, waits for them, and re-layouts  25.4 us (4%)
  other arithmetic  20.5 us (3%)
  between operations  14.7 us (2%)
    all_gather x1, waiting for transfers between devices, shards(): piece = lax.all_gather(kv_weight, ('inner', 'outer'), axis=0, tiled=True)  432 us
    reduce_scatter x1, waiting for transfers between devices, shards(): lax.psum_scatter(partial_dx, 'head', scatter_dimension=1, tiled=True)  96.4 us
    ppermute x16, waiting for transfers between devices, from_behind(): return lax.ppermute(value, axis, pairs)  88.4 us
  transfers between devices with their start and end apart: 18, of which 14 were waited for; matrix products, arithmetic and copies ran while one was open for 8% of the time, Pallas kernels for 0%

commit v1 on v0

v1 whole, which is shorter than its diff:
```python
import math

import jax
import jax.numpy as jnp
from jax import lax
from jax.experimental import pallas as pl
from jax.experimental.pallas import tpu as pltpu
from jax.sharding import Mesh, PartitionSpec as P

HD = 128
SPAN = 64
ROWS = 128
AXES = ("yh", "x", "yl", "z", "core")
SIZES = (2, 4, 2, 8, 2)
LOG2E = math.log2(math.e)
SCALE = 1.0 / math.sqrt(HD)
F32 = jnp.float32
BF16 = jnp.bfloat16
MIB = 1 << 20


def permute(value, move):
    pairs = []
    for a in range(2):
        for x in range(4):
            for b in range(2):
                for z in range(8):
                    for h in range(2):
                        flat = lambda c: (((c[0] * 4 + c[1]) * 2 + c[2]) * 8 + c[3]) * 2 + c[4]
                        pairs.append((flat((a, x, b, z, h)), flat(move(a, x, b, z, h))))
    return lax.ppermute(value, AXES, pairs)


def along_x(steps):
    return lambda a, x, b, z, h: (a, (x + steps) % 4, b, z, h)


def ring4(steps, core_zero_on_x):
    def move(a, x, b, z, h):
        if (h == 0) == core_zero_on_x:
            return (a, (x + steps) % 4, b, z, h)
        y = (a * 2 + b + steps) % 4
        return (y // 2, x, y % 2, z, h)

    return move


def next_outer(flip):
    def move(a, x, b, z, h):
        g = (b * 8 + z + 1) % 16
        return (a ^ flip, x, g // 8, g % 8, h)

    return move


def delta_body(do_ref, o_ref, lse_ref, delta_ref, lse2_ref):
    ones = jnp.ones((8, HD), F32)
    for h in range(16):
        cols = slice(h * HD, (h + 1) * HD)
        prod = do_ref[:, cols].astype(F32) * o_ref[:, cols].astype(F32)
        row = lax.dot_general(
            ones, prod, (((1,), (1,)), ((), ())),
            precision=lax.Precision.HIGHEST, preferred_element_type=F32,
        )
        delta_ref[h : h + 1, :] = row[0:1]
    lse2_ref[...] = lse_ref[...] * LOG2E


def attend_body(shift, spans, q_ref, do_ref, lse_ref, delta_ref, kv_ref, dqin_ref, terms_ref, dq_ref, dk_s, dv_s):
    head = pl.program_id(0)
    part = pl.program_id(1)
    yh = lax.axis_index("yh")
    x = lax.axis_index("x")
    outer = lax.axis_index("yl") * 8 + lax.axis_index("z")
    mine = (yh * 4 + x) * 16 + outer
    key_outer = lax.rem(outer + 1, 16)
    key_x = lax.rem(x + 4 - shift, 4)
    first = (yh * 4 + key_x) * 16 + key_outer
    second = ((1 - yh) * 4 + key_x) * 16 + key_outer
    lane = lax.broadcasted_iota(jnp.int32, (1, ROWS), 1)
    q_pos = jnp.where(lane < SPAN, spans[2 * mine] * SPAN + lane, spans[2 * mine + 1] * SPAN + lane - SPAN)
    row = lax.broadcasted_iota(jnp.int32, (2 * ROWS, 1), 0)
    k_span = jnp.where(
        row < 2 * SPAN,
        jnp.where(row < SPAN, spans[2 * first], spans[2 * first + 1]),
        jnp.where(row < 3 * SPAN, spans[2 * second], spans[2 * second + 1]),
    )
    k_pos = k_span * SPAN + lax.rem(row, SPAN)
    allowed = k_pos <= q_pos
    allowed = jnp.concatenate([allowed, allowed], axis=1)
    at = pl.ds(pl.multiple_of(head * HD, HD), HD)
    at_v = pl.ds(pl.multiple_of(head * HD + 2 * HD, HD), HD)
    keys = jnp.concatenate([kv_ref[0, :, at], kv_ref[1, :, at]], axis=0)
    values = jnp.concatenate([kv_ref[0, :, at_v], kv_ref[1, :, at_v]], axis=0)
    nt = (((1,), (1,)), ((), ()))
    dk = None
    for pair in range(2):
        c0 = slice(pair * 256, pair * 256 + 128)
        c1 = slice(pair * 256 + 128, pair * 256 + 256)
        h0 = head * 8 + part * 4 + pair * 2
        q2 = jnp.concatenate([q_ref[:, c0], q_ref[:, c1]], axis=0)
        do2 = jnp.concatenate([do_ref[:, c0], do_ref[:, c1]], axis=0)
        lse = jnp.concatenate([lse_ref[pl.ds(h0, 1), :], lse_ref[pl.ds(h0 + 1, 1), :]], axis=1)
        delta = jnp.concatenate([delta_ref[pl.ds(h0, 1), :], delta_ref[pl.ds(h0 + 1, 1), :]], axis=1)
        s = lax.dot_general(keys, q2, nt, preferred_element_type=F32)
        p = jnp.where(allowed, jnp.exp2(s * (SCALE * LOG2E) - lse), 0.0)
        dp = lax.dot_general(values, do2, nt, preferred_element_type=F32)
        ds = (p * (dp - delta)).astype(BF16)
        pb = p.astype(BF16)
        dv_t = jnp.dot(pb, do2, preferred_element_type=F32)
        dk_t = jnp.dot(ds, q2, preferred_element_type=F32)
        dk = dk_t if dk is None else dk + dk_t
        dv = dv_t if pair == 0 else dv + dv_t
        dq = lax.dot_general(ds, keys, (((0,), (0,)), ((), ())), preferred_element_type=F32)
        dq_ref[:, c0] = dqin_ref[:, c0] + dq[:ROWS] * SCALE
        dq_ref[:, c1] = dqin_ref[:, c1] + dq[ROWS:] * SCALE

    @pl.when(part == 0)
    def _():
        dk_s[...] = dk
        dv_s[...] = dv

    @pl.when(part == 1)
    def _():
        k = ((dk_s[...] + dk) * SCALE).astype(BF16)
        v = (dv_s[...] + dv).astype(BF16)
        terms_ref[0, :, at] = k[:ROWS]
        terms_ref[1, :, at] = k[ROWS:]
        terms_ref[0, :, at_v] = v[:ROWS]
        terms_ref[1, :, at_v] = v[ROWS:]


def attend(shift, spans, q, do, lse2, delta, kvp, dq_in, alias):
    half = lambda i, j, s: (0, i * 2 + j)
    whole2 = lambda i, j, s: (0, 0)
    return pl.pallas_call(
        lambda *refs: attend_body(shift, *refs),
        grid_spec=pltpu.PrefetchScalarGridSpec(
            num_scalar_prefetch=1,
            grid=(2, 2),
            in_specs=[
                pl.BlockSpec((ROWS, 512), half),
                pl.BlockSpec((ROWS, 512), half),
                pl.BlockSpec((16, ROWS), whole2),
                pl.BlockSpec((16, ROWS), whole2),
                pl.BlockSpec((2, ROWS, 512), lambda i, j, s: (0, 0, 0)),
                pl.BlockSpec((ROWS, 512), half),
            ],
            out_specs=[
                pl.BlockSpec((2, ROWS, 512), lambda i, j, s: (0, 0, 0)),
                pl.BlockSpec((ROWS, 512), half),
            ],
            scratch_shapes=[pltpu.VMEM((256, HD), F32), pltpu.VMEM((256, HD), F32)],
        ),
        out_shape=[
            jax.ShapeDtypeStruct((2, ROWS, 512), BF16),
            jax.ShapeDtypeStruct((ROWS, 2048), F32),
        ],
        input_output_aliases={6: 1} if alias else {},
        compiler_params=pltpu.CompilerParams(vmem_limit_bytes=24 * MIB),
        cost_estimate=pl.CostEstimate(flops=700_000_000, bytes_accessed=4_000_000, transcendentals=524288),
        name="attend",
    )(spans, q, do, lse2, delta, kvp, dq_in)


def reduce_body(t0, t1, t2, t3, r0, r1):
    total = t0[...].astype(F32) + t1[...].astype(F32) + t2[...].astype(F32) + t3[...].astype(F32)
    total = total.astype(BF16)
    r0[...] = total[0]
    r1[...] = total[1]


def final_body(acc, r0, r1, dkv, dkvb):
    total = acc[...] + (r0[...].astype(F32) + r1[...].astype(F32))
    dkv[...] = total
    dkvb[...] = total.astype(BF16)


def dx_body(own_ref, other_ref, *refs):
    a_refs, b_refs = refs[:8], refs[8:12]
    out_ref, wa, wb, dk, sems = refs[12:]
    yh = lax.axis_index("yh")
    x = lax.axis_index("x")
    yl = lax.axis_index("yl")
    z = lax.axis_index("z")
    core = lax.axis_index("core")
    y = yh * 2 + yl
    copies = [pltpu.make_async_copy(r, wa.at[k], sems.at[k]) for k, r in enumerate(a_refs)]
    copies += [pltpu.make_async_copy(r, wb.at[k], sems.at[8 + k]) for k, r in enumerate(b_refs)]
    for c in copies:
        c.start()
    dk[core] = own_ref[...]
    dk[1 - core] = other_ref[...]
    for c in copies:
        c.wait()
    nt = (((1,), (1,)), ((), ()))
    p_at = jnp.where(core == 0, x, y)
    q_at = jnp.where(core == 0, y, x)

    @pl.loop(0, 16)
    def _(tile):
        tx = tile // 4
        tb = lax.rem(tile // 2, 2)
        tz = lax.rem(tile, 2) * 4
        total = None
        for a in range(2):
            ty = a * 2 + tb
            p_to = jnp.where(core == 0, tx, ty)
            q_to = jnp.where(core == 0, ty, tx)
            s = lax.rem(p_at - p_to + 4, 4)
            t = lax.rem(q_at - q_to + 4, 4)
            wa_rows = []
            wb_rows = []
            for m in range(4):
                zz = tz + m
                k = jnp.where(core == 0, lax.rem(z - zz + 8, 8), lax.rem(zz - z + 8, 8))
                wa_rows.append(wa[k, t * 4 + s])
                e = lax.bitwise_xor(z, zz)
                wb_rows.append(wb[t, s * 8 + e])
            w_a = jnp.concatenate(wa_rows, axis=0)
            w_b = jnp.concatenate(wb_rows, axis=0)
            got = lax.dot_general(dk[a, :, 0:256], w_a, nt, preferred_element_type=F32)
            got = got + lax.dot_general(dk[a, :, 256:512], w_b, nt, preferred_element_type=F32)
            total = got if total is None else total + got
        out_ref[:, pl.ds(pl.multiple_of(tile * 256, 256), 256)] = total.astype(BF16)


def shards(queries, out_grad, outputs, log_norm, kv_held, span_order, dq_acc, dkv_acc, kv_weight):
    vmem = pl.BlockSpec(memory_space=pltpu.VMEM)

    w0 = permute(kv_weight.reshape(64, 512), lambda a, x, b, z, h: (h, x, b, z, a))
    kv0 = kv_held.reshape(ROWS, 512)
    kvy = permute(kv0, lambda a, x, b, z, h: (1 - a, x, b, z, h))
    delta, lse2 = pl.pallas_call(
        delta_body,
        in_specs=[vmem] * 3,
        out_specs=[vmem] * 2,
        out_shape=[jax.ShapeDtypeStruct((16, ROWS), F32)] * 2,
        cost_estimate=pl.CostEstimate(flops=10_000_000, bytes_accessed=1_000_000, transcendentals=0),
        name="row_sums",
    )(out_grad, outputs, log_norm)
    pair = jnp.stack([kv0, kvy])
    pairs = {s: permute(pair, along_x(s)) for s in (1, 3, 2)}

    wa = w0[:, :256]
    wb = w0[:, 256:]
    a1 = jnp.stack([wa] + [permute(wa, ring4(s, True)) for s in (1, 2, 3)])
    for bit in (1, 2, 4):
        cur = wb[None] if bit == 1 else cur
        got = permute(cur, lambda a, x, b, z, h: (a, x, b, z ^ bit, h))
        cur = jnp.concatenate([cur, got], axis=0)
    a2 = jnp.concatenate([a1] + [permute(a1, ring4(s, False)) for s in (1, 2, 3)], axis=0)
    b2 = jnp.concatenate([cur] + [permute(cur, ring4(s, True)) for s in (1, 2, 3)], axis=0)
    b_parts = [b2] + [permute(b2, ring4(s, False)) for s in (1, 2, 3)]
    a_parts = [a2]
    for _ in range(7):
        a_parts.append(permute(a_parts[-1], lambda a, x, b, z, h: (a, x, b, (z + 1 - 2 * h) % 8, h)))

    t0, dq = attend(0, span_order, queries, out_grad, lse2, delta, pair, dq_acc, False)
    back = [t0]
    for s in (1, 3, 2):
        term, dq = attend(s, span_order, queries, out_grad, lse2, delta, pairs[s], dq, True)
        back.append(permute(term, along_x(-s)))
    r0, r1 = pl.pallas_call(
        reduce_body,
        in_specs=[vmem] * 4,
        out_specs=[vmem] * 2,
        out_shape=[jax.ShapeDtypeStruct((ROWS, 512), BF16)] * 2,
        cost_estimate=pl.CostEstimate(flops=1_000_000, bytes_accessed=1_300_000, transcendentals=0),
        name="reduce_terms",
    )(*back)
    r0 = permute(r0, next_outer(0))
    r1 = permute(r1, next_outer(1))
    dkv, dkvb = pl.pallas_call(
        final_body,
        in_specs=[vmem] * 3,
        out_specs=[vmem] * 2,
        out_shape=[jax.ShapeDtypeStruct((ROWS, 512), F32), jax.ShapeDtypeStruct((ROWS, 512), BF16)],
        cost_estimate=pl.CostEstimate(flops=1_000_000, bytes_accessed=1_000_000, transcendentals=0),
        name="add_terms",
    )(dkv_acc.reshape(ROWS, 512), r0, r1)
    other = permute(dkvb, lambda a, x, b, z, h: (a, x, b, z, 1 - h))
    dx = pl.pallas_call(
        dx_body,
        in_specs=[vmem] * 2 + [pl.BlockSpec(memory_space=pl.ANY)] * 12,
        out_specs=vmem,
        out_shape=jax.ShapeDtypeStruct((ROWS, 4096), BF16),
        scratch_shapes=[
            pltpu.VMEM((8, 16, 64, 256), BF16),
            pltpu.VMEM((4, 32, 64, 256), BF16),
            pltpu.VMEM((2, ROWS, 512), BF16),
            pltpu.SemaphoreType.DMA((12,)),
        ],
        compiler_params=pltpu.CompilerParams(vmem_limit_bytes=32 * MIB),
        cost_estimate=pl.CostEstimate(flops=1_100_000_000, bytes_accessed=9_000_000, transcendentals=0),
        name="input_grad",
    )(dkvb, other, *a_parts, *b_parts)
    return (dq, dkv.reshape(ROWS, 2, 256), dx)


def solution(mesh):
    fine = Mesh(mesh.devices.reshape(SIZES), AXES)
    tokens = ("yh", "x", "yl", "z")
    return jax.shard_map(
        shards,
        mesh=fine,
        in_specs=(
            P(tokens, "core"),
            P(tokens, "core"),
            P(tokens, "core"),
            P("core", tokens),
            P(tokens, None, "core"),
            P(),
            P(tokens, "core"),
            P(tokens, None, "core"),
            P(tokens, None, "core"),
        ),
        out_specs=(P(tokens, "core"), P(tokens, None, "core"), P(tokens, "core")),
        check_vma=False,
    )
```

time: 714 us -> 175 us (0.25)
  waiting for transfers between devices: 617 us -> 67.9 us
  starting transfers between devices: 4.98 us -> 49.9 us
  Pallas kernels: 0 us -> 37.6 us
  matrix products: 30 us -> 0 us
  other arithmetic: 20.5 us -> 1.03 us
  between operations: 14.7 us -> 1.14 us
  local copies, waits for them, and re-layouts: 25.4 us -> 16.1 us
    all_gather x1 -> x0, waiting for transfers between devices: 432 us -> none  [shards(): piece = lax.all_gather(kv_weight, ('inner', 'outer'), axis=0, tiled=True)]
    reduce_scatter x1 -> x0, waiting for transfers between devices: 96.4 us -> none  [shards(): lax.psum_scatter(partial_dx, 'head', scatter_dimension=1, tiled=True)]
    ppermute x16 -> x33, starting transfers between devices: 4.9 us -> 49.9 us  [permute(): return lax.ppermute(value, AXES, pairs)]
    pallas_call x0 -> x8, Pallas kernels: none -> 37.6 us  [the longest x4 22.1 us: attend(): pl.pallas_call(lambda *refs: attend_body(shift, *refs), grid_spec=pltpu.P...]
    dot_general x41 -> x0, matrix products: 30 us -> none  [the longest x1 8.3 us: shards(): jnp.einsum('ts,ds->td', dkvb, flat, preferred_element_type=jnp.float32)]
    ppermute x16 -> x33, waiting for transfers between devices: 88.4 us -> 67.9 us  [permute(): return lax.ppermute(value, AXES, pairs)]
    add x13 -> x0, other arithmetic: 13.4 us -> none  [the longest x7 10.7 us: shards(): carried = from_behind(carried + dkv_term, 'inner', 1)]
    another operation x16 -> x1, local copies, waits for them, and re-layouts: 11.2 us -> 0.09 us  [shards(): pair = jnp.stack([kv0, kvy])]
  transfers between devices with their start and end apart: 18 -> 33, of which waited for: 14 -> 11; matrix products, arithmetic and copies ran while one was open for 8% -> 2% of each run, Pallas kernels for 0% -> 17%
where the time goes in v1:
time: 175 us; the launch traced here: 174 us
  waiting for transfers between devices  67.9 us (39%)
  starting transfers between devices  49.9 us (29%)
  Pallas kernels  37.6 us (21%)
  local copies, waits for them, and re-layouts  16.1 us (9%)
    ppermute x33, waiting for transfers between devices, permute(): return lax.ppermute(value, AXES, pairs)  67.9 us
    ppermute x33, starting transfers between devices, permute(): return lax.ppermute(value, AXES, pairs)  49.9 us
    pallas_call x4, Pallas kernels, attend(): pl.pallas_call(lambda *refs: attend_body(shift, *refs), grid_spec=pltpu.P...  22.1 us
    unnamed x68, local copies, waits for them, and re-layouts  14.1 us
    pallas_call x1, Pallas kernels, shards(): pl.pallas_call(dx_body, in_specs=[vmem] * 2 + [pl.BlockSpec(memory_space=...  8.05 us
    pallas_call x1, Pallas kernels, shards(): pl.pallas_call(delta_body, in_specs=[vmem] * 3, out_specs=[vmem] * 2, out...  3.63 us
  transfers between devices with their start and end apart: 33, of which 11 were waited for; matrix products, arithmetic and copies ran while one was open for 2% of the time, Pallas kernels for 17%

profile of v1, /device:TPU:1, one launch (start us, length us, event | category | flops | bytes accessed | tf_op | source)
XLA Modules:
  0.0 173.7 jit_solution(7683451531741695252)
XLA Ops:
  1.5 6.2 %collective-permute-start.10 = (bf16[64,512]{1,0:T(8,128)(2,1)S(1)}, bf16[64,512]{1,0:T(8,128)(2,1)S(1)}, u32[]{:S(2)}, u32[]{:S(2)}) collective-permute-start(bf16[64,512]{1,0:T(8,128)(2,1)S(1)} %bitcast.28), channel_id=1, source_target_pairs={{0,0},{1,128},{2,2},{3,130},{4,4},{5,132},{6,6},{7,134},{8,8},{9,1... | collective-permute-start | bytes 196616 | tf_op jit(solution)/shard_map/ppermute | solution.py:31
  10.9 2.3 %collective-permute-start.13 = (bf16[64,256]{1,0:T(8,128)(2,1)S(1)}, bf16[64,256]{1,0:T(8,128)(2,1)S(1)}, u32[]{:S(2)}, u32[]{:S(2)}) collective-permute-start(bf16[64,256]{1,0:T(8,128)(2,1)S(1)} %get-tuple-element.33), channel_id=1, source_target_pairs={{0,96},{1,145},{2,98},{3,147},{4,100},{5,149},{6,102},{7,151},{8,1... | collective-permute-start | bytes 98312 | tf_op jit(solution)/shard_map/ppermute | solution.py:31
  14.5 2.6 %collective-permute-start.16 = (bf16[4,64,256]{2,1,0:T(8,128)(2,1)S(1)}, bf16[4,64,256]{2,1,0:T(8,128)(2,1)S(1)}, u32[]{:S(2)}, u32[]{:S(2)}) collective-permute-start(bf16[4,64,256]{2,1,0:T(8,128)(2,1)S(1)} %pad_maximum_fusion.2), channel_id=1, source_target_pairs={{0,144},{1,97},{2,146},{3,99},{4,148},{5,101},{6,150},{7,103},{8,1... | collective-permute-start | bytes 393224 | tf_op jit(solution)/shard_map/ppermute | solution.py:31
  18.2 5.6 %collective-permute-done.14 = bf16[4,64,256]{2,1,0:T(8,128)(2,1)S(1)} collective-permute-done((bf16[4,64,256]{2,1,0:T(8,128)(2,1)S(1)}, bf16[4,64,256]{2,1,0:T(8,128)(2,1)S(1)}, u32[]{:S(2)}, u32[]{:S(2)}) %collective-permute-start.14) | collective-permute-done | bytes 131104 | tf_op jit(solution)/shard_map/ppermute | solution.py:31
  23.9 5.7 %collective-permute-start.17 = (bf16[16,64,256]{2,1,0:T(8,128)(2,1)S(1)}, bf16[16,64,256]{2,1,0:T(8,128)(2,1)S(1)}, u32[]{:S(2)}, u32[]{:S(2)}) collective-permute-start(bf16[16,64,256]{2,1,0:T(8,128)(2,1)S(1)} %constant_dynamic-update-slice_fusion.refs_0_), channel_id=1, source_target_pairs={{0,2},{1,15},{2,4},{3,1},{4,6},{5,3},{6,8},{7,5},{8,10},{9,7},{10,... | collective-permute-start | bytes 1572872 | tf_op jit(solution)/shard_map/ppermute | solution.py:31
  30.3 5.3 %collective-permute-done.17.refs_1_ = bf16[16,64,256]{2,1,0:T(8,128)(2,1)S(1)} collective-permute-done((bf16[16,64,256]{2,1,0:T(8,128)(2,1)S(1)}, bf16[16,64,256]{2,1,0:T(8,128)(2,1)S(1)}, u32[]{:S(2)}, u32[]{:S(2)}) %collective-permute-start.17) | collective-permute-done | bytes 524320 | tf_op jit(solution)/shard_map/ppermute | solution.py:31
  35.7 3.1 %collective-permute-start.18 = (bf16[16,64,256]{2,1,0:T(8,128)(2,1)S(1)}, bf16[16,64,256]{2,1,0:T(8,128)(2,1)S(1)}, u32[]{:S(2)}, u32[]{:S(2)}) collective-permute-start(bf16[16,64,256]{2,1,0:T(8,128)(2,1)S(1)} %collective-permute-done.17.refs_1_), channel_id=1, source_target_pairs={{0,2},{1,15},{2,4},{3,1},{4,6},{5,3},{6,8},{7,5},{8,10},{9,7},{10,... | collective-permute-start | bytes 1572872 | tf_op jit(solution)/shard_map/ppermute | solution.py:31
  39.6 5.3 %collective-permute-done.18.refs_2_ = bf16[16,64,256]{2,1,0:T(8,128)(2,1)S(1)} collective-permute-done((bf16[16,64,256]{2,1,0:T(8,128)(2,1)S(1)}, bf16[16,64,256]{2,1,0:T(8,128)(2,1)S(1)}, u32[]{:S(2)}, u32[]{:S(2)}) %collective-permute-start.18) | collective-permute-done | bytes 524320 | tf_op jit(solution)/shard_map/ppermute | solution.py:31
  44.9 3.1 %collective-permute-start.19 = (bf16[16,64,256]{2,1,0:T(8,128)(2,1)S(1)}, bf16[16,64,256]{2,1,0:T(8,128)(2,1)S(1)}, u32[]{:S(2)}, u32[]{:S(2)}) collective-permute-start(bf16[16,64,256]{2,1,0:T(8,128)(2,1)S(1)} %collective-permute-done.18.refs_2_), channel_id=1, source_target_pairs={{0,2},{1,15},{2,4},{3,1},{4,6},{5,3},{6,8},{7,5},{8,10},{9,7},{10,... | collective-permute-start | bytes 1572872 | tf_op jit(solution)/shard_map/ppermute | solution.py:31
  48.1 3.1 %collective-permute-start = (bf16[128,512]{1,0:T(8,128)(2,1)S(1)}, bf16[128,512]{1,0:T(8,128)(2,1)}, u32[]{:S(2)}, u32[]{:S(2)}) collective-permute-start(bf16[128,512]{1,0:T(8,128)(2,1)S(1)} %bitcast.23), channel_id=1, source_target_pairs={{0,128},{1,129},{2,130},{3,131},{4,132},{5,133},{6,134},{7,135},{8... | collective-permute-start | bytes 393224 | tf_op jit(solution)/shard_map/ppermute | solution.py:31
  51.2 3.6 %row_sums.1 = (f32[16,128]{1,0:T(8,128)}, f32[16,128]{1,0:T(8,128)}) custom-call(bf16[128,2048]{1,0:T(8,128)(2,1)} %refs_2_.7, bf16[128,2048]{1,0:T(8,128)(2,1)} %o_ref.1, f32[16,128]{1,0:T(8,128)} %lse_ref.1), custom_call_target="tpu_custom_call" | custom-call | flops 10000000 | bytes 1000000 | tf_op jit(solution)/shard_map/row_sums/pallas_call | solution.py:234
  56.1 2.7 %collective-permute-start.2 = (bf16[2,128,512]{2,1,0:T(8,128)(2,1)S(1)}, bf16[2,128,512]{2,1,0:T(8,128)(2,1)S(1)}, u32[]{:S(2)}, u32[]{:S(2)}) collective-permute-start(bf16[2,128,512]{2,1,0:T(8,128)(2,1)S(1)} %pad_maximum_fusion.refs_5_), channel_id=1, source_target_pairs={{0,96},{1,97},{2,98},{3,99},{4,100},{5,101},{6,102},{7,103},{8,104... | collective-permute-start | bytes 786440 | tf_op jit(solution)/shard_map/ppermute | solution.py:31
  60.9 4.1 %collective-permute-start.26 = (bf16[4,64,256]{2,1,0:T(8,128)(2,1)S(1)}, bf16[4,64,256]{2,1,0:T(8,128)(2,1)S(1)}, u32[]{:S(2)}, u32[]{:S(2)}) collective-permute-start(bf16[4,64,256]{2,1,0:T(8,128)(2,1)S(1)} %pad_maximum_fusion.3), channel_id=1, source_target_pairs={{0,8},{1,9},{2,10},{3,11},{4,12},{5,13},{6,14},{7,15},{8,0},{9,1},... | collective-permute-start | bytes 393224 | tf_op jit(solution)/shard_map/ppermute | solution.py:31
  66.8 4.8 %attend.4 = (bf16[2,128,512]{2,1,0:T(8,128)(2,1)S(1)}, f32[128,2048]{1,0:T(8,128)}) custom-call(s32[256]{0:T(256)S(1)} %copy-done.19, bf16[128,2048]{1,0:T(8,128)(2,1)S(1)} %copy-done.16, bf16[128,2048]{1,0:T(8,128)(2,1)S(1)} %copy-done.12, f32[16,128]{1,0:T(8,128)S(1)} %copy-done.18, f32[16,128]{1,0:T(8,128)S(1)} %copy-done.17, ...), custom_call_target="tpu_custom_call" | custom-call | flops 700000000 | bytes 4000000 | tf_op jit(solution)/shard_map/attend/pallas_call | solution.py:136
  74.5 2.3 %collective-permute-start.21 = (bf16[16,64,256]{2,1,0:T(8,128)(2,1)S(1)}, bf16[16,64,256]{2,1,0:T(8,128)(2,1)S(1)}, u32[]{:S(2)}, u32[]{:S(2)}) collective-permute-start(bf16[16,64,256]{2,1,0:T(8,128)(2,1)S(1)} %collective-permute-done.20.refs_4_), channel_id=1, source_target_pairs={{0,2},{1,15},{2,4},{3,1},{4,6},{5,3},{6,8},{7,5},{8,10},{9,7},{10,... | collective-permute-start | bytes 1572872 | tf_op jit(solution)/shard_map/ppermute | solution.py:31
  76.9 5.8 %attend.5 = (bf16[2,128,512]{2,1,0:T(8,128)(2,1)S(1)}, f32[128,2048]{1,0:T(8,128)}) custom-call(s32[256]{0:T(256)S(1)} %copy-done.19, bf16[128,2048]{1,0:T(8,128)(2,1)S(1)} %copy-done.16, bf16[128,2048]{1,0:T(8,128)(2,1)S(1)} %copy-done.12, f32[16,128]{1,0:T(8,128)S(1)} %copy-done.18, f32[16,128]{1,0:T(8,128)S(1)} %copy-done.17, ...), custom_call_target="tpu_custom_call", output_to_operand_aliasing={{1}: (6, {})} | custom-call | flops 700000000 | bytes 4000000 | tf_op jit(solution)/shard_map/attend/pallas_call | solution.py:136
  83.6 5.8 %attend.6 = (bf16[2,128,512]{2,1,0:T(8,128)(2,1)S(1)}, f32[128,2048]{1,0:T(8,128)}) custom-call(s32[256]{0:T(256)S(1)} %copy-done.19, bf16[128,2048]{1,0:T(8,128)(2,1)S(1)} %copy-done.16, bf16[128,2048]{1,0:T(8,128)(2,1)S(1)} %copy-done.12, f32[16,128]{1,0:T(8,128)S(1)} %copy-done.18, f32[16,128]{1,0:T(8,128)S(1)} %copy-done.17, ...), custom_call_target="tpu_custom_call", output_to_operand_aliasing={{1}: (6, {})} | custom-call | flops 700000000 | bytes 4000000 | tf_op jit(solution)/shard_map/attend/pallas_call | solution.py:136
  89.4 5.8 %attend.7 = (bf16[2,128,512]{2,1,0:T(8,128)(2,1)S(1)}, f32[128,2048]{1,0:T(8,128)}) custom-call(s32[256]{0:T(256)S(1)} %copy-done.19, bf16[128,2048]{1,0:T(8,128)(2,1)S(1)} %copy-done.16, bf16[128,2048]{1,0:T(8,128)(2,1)S(1)} %copy-done.12, f32[16,128]{1,0:T(8,128)S(1)} %copy-done.18, f32[16,128]{1,0:T(8,128)S(1)} %copy-done.17, ...), custom_call_target="tpu_custom_call", output_to_operand_aliasing={{1}: (6, {})} | custom-call | flops 700000000 | bytes 4000000 | tf_op jit(solution)/shard_map/attend/pallas_call | solution.py:136
  95.1 2.7 %collective-permute-start.6 = (bf16[2,128,512]{2,1,0:T(8,128)(2,1)S(1)}, bf16[2,128,512]{2,1,0:T(8,128)(2,1)S(1)}, u32[]{:S(2)}, u32[]{:S(2)}) collective-permute-start(bf16[2,128,512]{2,1,0:T(8,128)(2,1)S(1)} %get-tuple-element.26), channel_id=1, source_target_pairs={{0,64},{1,65},{2,66},{3,67},{4,68},{5,69},{6,70},{7,71},{8,72},{9,... | collective-permute-start | bytes 786440 | tf_op jit(solution)/shard_map/ppermute | solution.py:31
  102.3 31.0 %collective-permute-done.5.t2 = bf16[2,128,512]{2,1,0:T(8,128)(2,1)S(1)} collective-permute-done((bf16[2,128,512]{2,1,0:T(8,128)(2,1)S(1)}, bf16[2,128,512]{2,1,0:T(8,128)(2,1)S(1)}, u32[]{:S(2)}, u32[]{:S(2)}) %collective-permute-start.5) | collective-permute-done | bytes 262176 | tf_op jit(solution)/shard_map/ppermute | solution.py:31
  133.7 4.9 %collective-permute-done.4.t1 = bf16[2,128,512]{2,1,0:T(8,128)(2,1)S(1)} collective-permute-done((bf16[2,128,512]{2,1,0:T(8,128)(2,1)S(1)}, bf16[2,128,512]{2,1,0:T(8,128)(2,1)S(1)}, u32[]{:S(2)}, u32[]{:S(2)}) %collective-permute-start.4) | collective-permute-done | bytes 262176 | tf_op jit(solution)/shard_map/ppermute | solution.py:31
  143.1 4.3 %collective-permute-done.7.r0 = bf16[128,512]{1,0:T(8,128)(2,1)S(1)} collective-permute-done((bf16[128,512]{1,0:T(8,128)(2,1)}, bf16[128,512]{1,0:T(8,128)(2,1)S(1)}, u32[]{:S(2)}, u32[]{:S(2)}) %collective-permute-start.7) | collective-permute-done | bytes 131104 | tf_op jit(solution)/shard_map/ppermute | solution.py:31
  148.2 6.6 %collective-permute-done.8.r1 = bf16[128,512]{1,0:T(8,128)(2,1)S(1)} collective-permute-done((bf16[128,512]{1,0:T(8,128)(2,1)}, bf16[128,512]{1,0:T(8,128)(2,1)S(1)}, u32[]{:S(2)}, u32[]{:S(2)}) %collective-permute-start.8) | collective-permute-done | bytes 131104 | tf_op jit(solution)/shard_map/ppermute | solution.py:31
  165.5 8.1 %input_grad.1 = bf16[128,4096]{1,0:T(8,128)(2,1)} custom-call(bf16[128,512]{1,0:T(8,128)(2,1)S(1)} %copy-done.14, bf16[128,512]{1,0:T(8,128)(2,1)S(1)} %collective-permute-done.9.other_ref, bf16[16,64,256]{2,1,0:T(8,128)(2,1)S(1)} %copy-done.1, bf16[16,64,256]{2,1,0:T(8,128)(2,1)S(1)} %copy-done.3, bf16[16,64,256]{2,1,0:T(8,128)(2,1)S(1)} %copy-done.5, ...), custom_call_target="tpu_custom_call" | custom-call | flops 1100000000 | bytes 9000000 | tf_op jit(solution)/shard_map/input_grad/pallas_call | solution.py:283
  (128 shorter events, 37.9 us)
Async XLA Ops:
  1.5 8.2 %collective-permute-start.10 = (bf16[64,512]{1,0:T(8,128)(2,1)S(1)}, bf16[64,512]{1,0:T(8,128)(2,1)S(1)}, u32[]{:S(2)}, u32[]{:S(2)}) collective-permute-start(bf16[64,512]{1,0:T(8,128)(2,1)S(1)} %bitcast.28), channel_id=1, source_target_pairs={{0,0},{1,128},{2,2},{3,130},{4,4},{5,132},{6,6},{7,134},{8,8},{9,1... | collective-permute-start | bytes 196616 | tf_op jit(solution)/shard_map/ppermute | solution.py:31
  14.5 9.3 %collective-permute-start.16 = (bf16[4,64,256]{2,1,0:T(8,128)(2,1)S(1)}, bf16[4,64,256]{2,1,0:T(8,128)(2,1)S(1)}, u32[]{:S(2)}, u32[]{:S(2)}) collective-permute-start(bf16[4,64,256]{2,1,0:T(8,128)(2,1)S(1)} %pad_maximum_fusion.2), channel_id=1, source_target_pairs={{0,144},{1,97},{2,146},{3,99},{4,148},{5,101},{6,150},{7,103},{8,1... | collective-permute-start | bytes 393224 | tf_op jit(solution)/shard_map/ppermute | solution.py:31
  17.1 6.7 %collective-permute-start.15 = (bf16[4,64,256]{2,1,0:T(8,128)(2,1)S(1)}, bf16[4,64,256]{2,1,0:T(8,128)(2,1)S(1)}, u32[]{:S(2)}, u32[]{:S(2)}) collective-permute-start(bf16[4,64,256]{2,1,0:T(8,128)(2,1)S(1)} %pad_maximum_fusion.2), channel_id=1, source_target_pairs={{0,128},{1,65},{2,130},{3,67},{4,132},{5,69},{6,134},{7,71},{8,136... | collective-permute-start | bytes 393224 | tf_op jit(solution)/shard_map/ppermute | solution.py:31
  23.9 11.8 %collective-permute-start.17 = (bf16[16,64,256]{2,1,0:T(8,128)(2,1)S(1)}, bf16[16,64,256]{2,1,0:T(8,128)(2,1)S(1)}, u32[]{:S(2)}, u32[]{:S(2)}) collective-permute-start(bf16[16,64,256]{2,1,0:T(8,128)(2,1)S(1)} %constant_dynamic-update-slice_fusion.refs_0_), channel_id=1, source_target_pairs={{0,2},{1,15},{2,4},{3,1},{4,6},{5,3},{6,8},{7,5},{8,10},{9,7},{10,... | collective-permute-start | bytes 1572872 | tf_op jit(solution)/shard_map/ppermute | solution.py:31
  35.7 9.2 %collective-permute-start.18 = (bf16[16,64,256]{2,1,0:T(8,128)(2,1)S(1)}, bf16[16,64,256]{2,1,0:T(8,128)(2,1)S(1)}, u32[]{:S(2)}, u32[]{:S(2)}) collective-permute-start(bf16[16,64,256]{2,1,0:T(8,128)(2,1)S(1)} %collective-permute-done.17.refs_1_), channel_id=1, source_target_pairs={{0,2},{1,15},{2,4},{3,1},{4,6},{5,3},{6,8},{7,5},{8,10},{9,7},{10,... | collective-permute-start | bytes 1572872 | tf_op jit(solution)/shard_map/ppermute | solution.py:31
  44.9 13.9 %collective-permute-start.19 = (bf16[16,64,256]{2,1,0:T(8,128)(2,1)S(1)}, bf16[16,64,256]{2,1,0:T(8,128)(2,1)S(1)}, u32[]{:S(2)}, u32[]{:S(2)}) collective-permute-start(bf16[16,64,256]{2,1,0:T(8,128)(2,1)S(1)} %collective-permute-done.18.refs_2_), channel_id=1, source_target_pairs={{0,2},{1,15},{2,4},{3,1},{4,6},{5,3},{6,8},{7,5},{8,10},{9,7},{10,... | collective-permute-start | bytes 1572872 | tf_op jit(solution)/shard_map/ppermute | solution.py:31
  48.0 6.9 %collective-permute-start.24 = (bf16[1,64,256]{2,1,0:T(8,128)(2,1)S(1)}, bf16[1,64,256]{2,1,0:T(8,128)(2,1)S(1)}, u32[]{:S(2)}, u32[]{:S(2)}) collective-permute-start(bf16[1,64,256]{2,1,0:T(8,128)(2,1)S(1)} %get-tuple-element.31), channel_id=1, source_target_pairs={{0,2},{1,3},{2,0},{3,1},{4,6},{5,7},{6,4},{7,5},{8,10},{9,11},{10,... | collective-permute-start | bytes 98312 | tf_op jit(solution)/shard_map/ppermute | solution.py:31
  48.1 7.0 %collective-permute-start = (bf16[128,512]{1,0:T(8,128)(2,1)S(1)}, bf16[128,512]{1,0:T(8,128)(2,1)}, u32[]{:S(2)}, u32[]{:S(2)}) collective-permute-start(bf16[128,512]{1,0:T(8,128)(2,1)S(1)} %bitcast.23), channel_id=1, source_target_pairs={{0,128},{1,129},{2,130},{3,131},{4,132},{5,133},{6,134},{7,135},{8... | collective-permute-start | bytes 393224 | tf_op jit(solution)/shard_map/ppermute | solution.py:31
  56.0 16.7 %collective-permute-start.3 = (bf16[2,128,512]{2,1,0:T(8,128)(2,1)S(1)}, bf16[2,128,512]{2,1,0:T(8,128)(2,1)S(1)}, u32[]{:S(2)}, u32[]{:S(2)}) collective-permute-start(bf16[2,128,512]{2,1,0:T(8,128)(2,1)S(1)} %pad_maximum_fusion.refs_5_), channel_id=1, source_target_pairs={{0,32},{1,33},{2,34},{3,35},{4,36},{5,37},{6,38},{7,39},{8,40},{9,... | collective-permute-start | bytes 786440 | tf_op jit(solution)/shard_map/ppermute | solution.py:31
  56.1 26.5 %collective-permute-start.2 = (bf16[2,128,512]{2,1,0:T(8,128)(2,1)S(1)}, bf16[2,128,512]{2,1,0:T(8,128)(2,1)S(1)}, u32[]{:S(2)}, u32[]{:S(2)}) collective-permute-start(bf16[2,128,512]{2,1,0:T(8,128)(2,1)S(1)} %pad_maximum_fusion.refs_5_), channel_id=1, source_target_pairs={{0,96},{1,97},{2,98},{3,99},{4,100},{5,101},{6,102},{7,103},{8,104... | collective-permute-start | bytes 786440 | tf_op jit(solution)/shard_map/ppermute | solution.py:31
  58.8 30.6 %collective-permute-start.1 = (bf16[2,128,512]{2,1,0:T(8,128)(2,1)S(1)}, bf16[2,128,512]{2,1,0:T(8,128)(2,1)S(1)}, u32[]{:S(2)}, u32[]{:S(2)}) collective-permute-start(bf16[2,128,512]{2,1,0:T(8,128)(2,1)S(1)} %pad_maximum_fusion.refs_5_), channel_id=1, source_target_pairs={{0,64},{1,65},{2,66},{3,67},{4,68},{5,69},{6,70},{7,71},{8,72},{9,... | collective-permute-start | bytes 786440 | tf_op jit(solution)/shard_map/ppermute | solution.py:31
  58.8 15.7 %collective-permute-start.20 = (bf16[16,64,256]{2,1,0:T(8,128)(2,1)S(1)}, bf16[16,64,256]{2,1,0:T(8,128)(2,1)S(1)}, u32[]{:S(2)}, u32[]{:S(2)}) collective-permute-start(bf16[16,64,256]{2,1,0:T(8,128)(2,1)S(1)} %collective-permute-done.19.refs_3_), channel_id=1, source_target_pairs={{0,2},{1,15},{2,4},{3,1},{4,6},{5,3},{6,8},{7,5},{8,10},{9,7},{10,... | collective-permute-start | bytes 1572872 | tf_op jit(solution)/shard_map/ppermute | solution.py:31
  60.9 10.6 %collective-permute-start.26 = (bf16[4,64,256]{2,1,0:T(8,128)(2,1)S(1)}, bf16[4,64,256]{2,1,0:T(8,128)(2,1)S(1)}, u32[]{:S(2)}, u32[]{:S(2)}) collective-permute-start(bf16[4,64,256]{2,1,0:T(8,128)(2,1)S(1)} %pad_maximum_fusion.3), channel_id=1, source_target_pairs={{0,8},{1,9},{2,10},{3,11},{4,12},{5,13},{6,14},{7,15},{8,0},{9,1},... | collective-permute-start | bytes 393224 | tf_op jit(solution)/shard_map/ppermute | solution.py:31
  72.2 25.6 %collective-permute-start.27 = (bf16[8,64,256]{2,1,0:T(8,128)(2,1)S(1)}, bf16[8,64,256]{2,1,0:T(8,128)(2,1)S(1)}, u32[]{:S(2)}, u32[]{:S(2)}) collective-permute-start(bf16[8,64,256]{2,1,0:T(8,128)(2,1)S(1)} %pad_maximum_fusion.1), channel_id=1, source_target_pairs={{0,32},{1,17},{2,34},{3,19},{4,36},{5,21},{6,38},{7,23},{8,40},{9,... | collective-permute-start | bytes 786440 | tf_op jit(solution)/shard_map/ppermute | solution.py:31
  72.8 25.1 %collective-permute-start.28 = (bf16[8,64,256]{2,1,0:T(8,128)(2,1)S(1)}, bf16[8,64,256]{2,1,0:T(8,128)(2,1)S(1)}, u32[]{:S(2)}, u32[]{:S(2)}) collective-permute-start(bf16[8,64,256]{2,1,0:T(8,128)(2,1)S(1)} %pad_maximum_fusion.1), channel_id=1, source_target_pairs={{0,64},{1,129},{2,66},{3,131},{4,68},{5,133},{6,70},{7,135},{8,72}... | collective-permute-start | bytes 786440 | tf_op jit(solution)/shard_map/ppermute | solution.py:31
  74.5 25.0 %collective-permute-start.21 = (bf16[16,64,256]{2,1,0:T(8,128)(2,1)S(1)}, bf16[16,64,256]{2,1,0:T(8,128)(2,1)S(1)}, u32[]{:S(2)}, u32[]{:S(2)}) collective-permute-start(bf16[16,64,256]{2,1,0:T(8,128)(2,1)S(1)} %collective-permute-done.20.refs_4_), channel_id=1, source_target_pairs={{0,2},{1,15},{2,4},{3,1},{4,6},{5,3},{6,8},{7,5},{8,10},{9,7},{10,... | collective-permute-start | bytes 1572872 | tf_op jit(solution)/shard_map/ppermute | solution.py:31
  82.6 15.2 %collective-permute-start.29 = (bf16[8,64,256]{2,1,0:T(8,128)(2,1)S(1)}, bf16[8,64,256]{2,1,0:T(8,128)(2,1)S(1)}, u32[]{:S(2)}, u32[]{:S(2)}) collective-permute-start(bf16[8,64,256]{2,1,0:T(8,128)(2,1)S(1)} %pad_maximum_fusion.1), channel_id=1, source_target_pairs={{0,96},{1,145},{2,98},{3,147},{4,100},{5,149},{6,102},{7,151},{8,1... | collective-permute-start | bytes 786440 | tf_op jit(solution)/shard_map/ppermute | solution.py:31
  97.9 61.2 %collective-permute-start.32 = (bf16[32,64,256]{2,1,0:T(8,128)(2,1)S(1)}, bf16[32,64,256]{2,1,0:T(8,128)(2,1)S(1)}, u32[]{:S(2)}, u32[]{:S(2)}) collective-permute-start(bf16[32,64,256]{2,1,0:T(8,128)(2,1)S(1)} %constant_dynamic-update-slice_fusion.7.refs_8_), channel_id=1, source_target_pairs={{0,144},{1,97},{2,146},{3,99},{4,148},{5,101},{6,150},{7,103},{8,1... | collective-permute-start | bytes 3145736 | tf_op jit(solution)/shard_map/ppermute | solution.py:31
  98.0 61.1 %collective-permute-start.31 = (bf16[32,64,256]{2,1,0:T(8,128)(2,1)S(1)}, bf16[32,64,256]{2,1,0:T(8,128)(2,1)S(1)}, u32[]{:S(2)}, u32[]{:S(2)}) collective-permute-start(bf16[32,64,256]{2,1,0:T(8,128)(2,1)S(1)} %constant_dynamic-update-slice_fusion.7.refs_8_), channel_id=1, source_target_pairs={{0,128},{1,65},{2,130},{3,67},{4,132},{5,69},{6,134},{7,71},{8,136... | collective-permute-start | bytes 3145736 | tf_op jit(solution)/shard_map/ppermute | solution.py:31
  98.7 60.5 %collective-permute-start.30 = (bf16[32,64,256]{2,1,0:T(8,128)(2,1)S(1)}, bf16[32,64,256]{2,1,0:T(8,128)(2,1)}, u32[]{:S(2)}, u32[]{:S(2)}) collective-permute-start(bf16[32,64,256]{2,1,0:T(8,128)(2,1)S(1)} %constant_dynamic-update-slice_fusion.7.refs_8_), channel_id=1, source_target_pairs={{0,16},{1,33},{2,18},{3,35},{4,20},{5,37},{6,22},{7,39},{8,24},{9,... | collective-permute-start | bytes 3145736 | tf_op jit(solution)/shard_map/ppermute | solution.py:31
  99.5 34.2 %collective-permute-start.22 = (bf16[16,64,256]{2,1,0:T(8,128)(2,1)S(1)}, bf16[16,64,256]{2,1,0:T(8,128)(2,1)}, u32[]{:S(2)}, u32[]{:S(2)}) collective-permute-start(bf16[16,64,256]{2,1,0:T(8,128)(2,1)S(1)} %collective-permute-done.21.refs_5_), channel_id=1, source_target_pairs={{0,2},{1,15},{2,4},{3,1},{4,6},{5,3},{6,8},{7,5},{8,10},{9,7},{10,... | collective-permute-start | bytes 1572872 | tf_op jit(solution)/shard_map/ppermute | solution.py:31
  101.9 31.5 %collective-permute-start.5 = (bf16[2,128,512]{2,1,0:T(8,128)(2,1)S(1)}, bf16[2,128,512]{2,1,0:T(8,128)(2,1)S(1)}, u32[]{:S(2)}, u32[]{:S(2)}) collective-permute-start(bf16[2,128,512]{2,1,0:T(8,128)(2,1)S(1)} %get-tuple-element.25), channel_id=1, source_target_pairs={{0,32},{1,33},{2,34},{3,35},{4,36},{5,37},{6,38},{7,39},{8,40},{9,... | collective-permute-start | bytes 786440 | tf_op jit(solution)/shard_map/ppermute | solution.py:31
  133.6 25.5 %collective-permute-start.23 = (bf16[16,64,256]{2,1,0:T(8,128)(2,1)}, bf16[16,64,256]{2,1,0:T(8,128)(2,1)}, u32[]{:S(2)}, u32[]{:S(2)}) collective-permute-start(bf16[16,64,256]{2,1,0:T(8,128)(2,1)} %collective-permute-done.22.refs_6_), channel_id=1, source_target_pairs={{0,2},{1,15},{2,4},{3,1},{4,6},{5,3},{6,8},{7,5},{8,10},{9,7},{10,... | collective-permute-start | bytes 1572872 | tf_op jit(solution)/shard_map/ppermute | solution.py:31
  147.4 7.3 %collective-permute-start.8 = (bf16[128,512]{1,0:T(8,128)(2,1)}, bf16[128,512]{1,0:T(8,128)(2,1)S(1)}, u32[]{:S(2)}, u32[]{:S(2)}) collective-permute-start(bf16[128,512]{1,0:T(8,128)(2,1)} %get-tuple-element.28), channel_id=1, source_target_pairs={{0,130},{1,131},{2,132},{3,133},{4,134},{5,135},{6,136},{7,137},{8... | collective-permute-start | bytes 393224 | tf_op jit(solution)/shard_map/ppermute | solution.py:31
  (36 other events, 207.0 us)

commit v2 on v1

v2 whole, which is shorter than its diff:
```python
import math

import jax
import jax.numpy as jnp
from jax import lax
from jax.experimental import pallas as pl
from jax.experimental.pallas import tpu as pltpu
from jax.sharding import Mesh, PartitionSpec as P

HD = 128
SPAN = 64
ROWS = 128
AXES = ("yh", "x", "yl", "z", "core")
SIZES = (2, 4, 2, 8, 2)
LOG2E = math.log2(math.e)
SCALE = 1.0 / math.sqrt(HD)
F32 = jnp.float32
BF16 = jnp.bfloat16
MIB = 1 << 20
SMALL = pl.CostEstimate(flops=1000, bytes_accessed=1000, transcendentals=0)


def permute(value, move):
    pairs = []
    for a in range(2):
        for x in range(4):
            for b in range(2):
                for z in range(8):
                    for h in range(2):
                        flat = lambda c: (((c[0] * 4 + c[1]) * 2 + c[2]) * 8 + c[3]) * 2 + c[4]
                        pairs.append((flat((a, x, b, z, h)), flat(move(a, x, b, z, h))))
    return lax.ppermute(value, AXES, pairs)


def along_x(steps):
    return lambda a, x, b, z, h: (a, (x + steps) % 4, b, z, h)


def next_outer(flip):
    def move(a, x, b, z, h):
        g = (b * 8 + z + 1) % 16
        return (a ^ flip, x, g // 8, g % 8, h)

    return move


def delta_body(do_ref, o_ref, lse_ref, delta_ref, lse2_ref):
    ones = jnp.ones((8, HD), F32)
    for h in range(16):
        cols = slice(h * HD, (h + 1) * HD)
        prod = do_ref[:, cols].astype(F32) * o_ref[:, cols].astype(F32)
        row = lax.dot_general(
            ones, prod, (((1,), (1,)), ((), ())),
            precision=lax.Precision.HIGHEST, preferred_element_type=F32,
        )
        delta_ref[h : h + 1, :] = row[0:1]
    lse2_ref[...] = lse_ref[...] * LOG2E


def attend_body(shift, spans, q_ref, do_ref, lse_ref, delta_ref, kv_ref, dqin_ref, terms_ref, dq_ref):
    yh = lax.axis_index("yh")
    x = lax.axis_index("x")
    outer = lax.axis_index("yl") * 8 + lax.axis_index("z")
    mine = (yh * 4 + x) * 16 + outer
    key_outer = lax.rem(outer + 1, 16)
    key_x = lax.rem(x + 4 - shift, 4)
    first = (yh * 4 + key_x) * 16 + key_outer
    second = ((1 - yh) * 4 + key_x) * 16 + key_outer
    lane = lax.broadcasted_iota(jnp.int32, (1, ROWS), 1)
    q_pos = jnp.where(lane < SPAN, spans[2 * mine] * SPAN + lane, spans[2 * mine + 1] * SPAN + lane - SPAN)
    row = lax.broadcasted_iota(jnp.int32, (2 * ROWS, 1), 0)
    k_span = jnp.where(
        row < 2 * SPAN,
        jnp.where(row < SPAN, spans[2 * first], spans[2 * first + 1]),
        jnp.where(row < 3 * SPAN, spans[2 * second], spans[2 * second + 1]),
    )
    k_pos = k_span * SPAN + lax.rem(row, SPAN)
    allowed = k_pos <= q_pos
    allowed = jnp.concatenate([allowed, allowed], axis=1)
    nt = (((1,), (1,)), ((), ()))
    for head in range(2):
        at = slice(head * HD, (head + 1) * HD)
        at_v = slice(head * HD + 2 * HD, head * HD + 3 * HD)
        keys = jnp.concatenate([kv_ref[0, :, at], kv_ref[1, :, at]], axis=0)
        values = jnp.concatenate([kv_ref[0, :, at_v], kv_ref[1, :, at_v]], axis=0)
        dk = dv = None
        for pair in range(4):
            h0 = head * 8 + pair * 2
            c0 = slice(h0 * HD, (h0 + 1) * HD)
            c1 = slice((h0 + 1) * HD, (h0 + 2) * HD)
            q2 = jnp.concatenate([q_ref[:, c0], q_ref[:, c1]], axis=0)
            do2 = jnp.concatenate([do_ref[:, c0], do_ref[:, c1]], axis=0)
            lse = jnp.concatenate([lse_ref[h0 : h0 + 1, :], lse_ref[h0 + 1 : h0 + 2, :]], axis=1)
            delta = jnp.concatenate([delta_ref[h0 : h0 + 1, :], delta_ref[h0 + 1 : h0 + 2, :]], axis=1)
            s = lax.dot_general(keys, q2, nt, preferred_element_type=F32)
            dp = lax.dot_general(values, do2, nt, preferred_element_type=F32)
            p = jnp.where(allowed, jnp.exp2(s * (SCALE * LOG2E) - lse), 0.0)
            pb = p.astype(BF16)
            ds = (p * (dp - delta)).astype(BF16)
            dv_t = jnp.dot(pb, do2, preferred_element_type=F32)
            dk_t = jnp.dot(ds, q2, preferred_element_type=F32)
            dk = dk_t if dk is None else dk + dk_t
            dv = dv_t if dv is None else dv + dv_t
            dq = lax.dot_general(ds, keys, (((0,), (0,)), ((), ())), preferred_element_type=F32)
            dq_ref[:, c0] = dqin_ref[:, c0] + dq[:ROWS] * SCALE
            dq_ref[:, c1] = dqin_ref[:, c1] + dq[ROWS:] * SCALE
        dk = (dk * SCALE).astype(BF16)
        dv = dv.astype(BF16)
        terms_ref[0, :, at] = dk[:ROWS]
        terms_ref[1, :, at] = dk[ROWS:]
        terms_ref[0, :, at_v] = dv[:ROWS]
        terms_ref[1, :, at_v] = dv[ROWS:]


def attend(shift, spans, q, do, lse2, delta, kvp, dq_in, alias):
    vmem = pl.BlockSpec(memory_space=pltpu.VMEM)
    return pl.pallas_call(
        lambda *refs: attend_body(shift, *refs),
        in_specs=[pl.BlockSpec(memory_space=pltpu.SMEM)] + [vmem] * 6,
        out_specs=[vmem] * 2,
        out_shape=[
            jax.ShapeDtypeStruct((2, ROWS, 512), BF16),
            jax.ShapeDtypeStruct((ROWS, 2048), F32),
        ],
        input_output_aliases={6: 1} if alias else {},
        compiler_params=pltpu.CompilerParams(vmem_limit_bytes=24 * MIB),
        cost_estimate=SMALL,
        name="attend",
    )(spans, q, do, lse2, delta, kvp, dq_in)


def dx_body(own_ref, other_ref, *refs):
    w_refs, out_refs, (wz, dk) = refs[:8], refs[8:-2], refs[-2:]
    rows = len(out_refs) * ROWS
    yl = lax.axis_index("yl")
    z = lax.axis_index("z")
    core = lax.axis_index("core")
    for k, ref in enumerate(w_refs):
        wz[lax.rem(z + 8 - k, 8)] = ref[...]
    dk[core] = own_ref[...].reshape(rows, 512)
    dk[1 - core] = other_ref[...].reshape(rows, 512)
    nt = (((1,), (1,)), ((), ()))
    for tile in range(4):
        beta = lax.bitwise_xor(yl, tile // 2)
        total = None
        for half in range(2):
            piece = beta * 2 + lax.bitwise_xor(core, half)
            w = jnp.concatenate([wz[(tile % 2) * 4 + m, piece] for m in range(4)], axis=0)
            got = lax.dot_general(dk[half], w, nt, preferred_element_type=F32)
            total = got if total is None else total + got
        total = total.astype(BF16)
        for n, ref in enumerate(out_refs):
            ref[:, tile * 256 : (tile + 1) * 256] = total[n * ROWS : (n + 1) * ROWS]


def dx_parts(own, other, weights):
    count = own.shape[0]
    vmem = pl.BlockSpec(memory_space=pltpu.VMEM)
    return pl.pallas_call(
        dx_body,
        in_specs=[vmem] * 10,
        out_specs=[vmem] * count,
        out_shape=[jax.ShapeDtypeStruct((ROWS, 1024), BF16)] * count,
        scratch_shapes=[pltpu.VMEM((8, 4, 64, 512), BF16), pltpu.VMEM((2, count * ROWS, 512), BF16)],
        compiler_params=pltpu.CompilerParams(vmem_limit_bytes=24 * MIB),
        cost_estimate=SMALL,
        name="input_grad",
    )(own, other, *weights)


def gather_body(*refs):
    out_ref = refs[4]
    x = lax.axis_index("x")
    for s in range(4):
        to = lax.rem(x + s, 4) * 1024
        out_ref[:, pl.ds(pl.multiple_of(to, 1024), 1024)] = refs[s][...]


def shards(queries, out_grad, outputs, log_norm, kv_held, span_order, dq_acc, dkv_acc, kv_weight):
    vmem = pl.BlockSpec(memory_space=pltpu.VMEM)
    both = permute(jnp.concatenate([kv_held, kv_weight], axis=0), lambda a, x, b, z, h: (1 - a, x, b, z, h))
    core = lax.axis_index("core")

    def step(value, by):
        return permute(value, lambda a, x, b, z, h: (a, x, b, (z + by) % 8, h))

    delta, lse2 = pl.pallas_call(
        delta_body,
        in_specs=[vmem] * 3,
        out_specs=[vmem] * 2,
        out_shape=[jax.ShapeDtypeStruct((16, ROWS), F32)] * 2,
        cost_estimate=SMALL,
        name="row_sums",
    )(out_grad, outputs, log_norm)
    both, delta, lse2 = lax.optimization_barrier((both, delta, lse2))
    pair = jnp.stack([kv_held, both[:ROWS]]).reshape(2, ROWS, 512)
    pairs = {s: permute(pair, along_x(s)) for s in (1, 3, 2)}

    mine = kv_weight.reshape(1, 64, 512)
    theirs = both[ROWS:].reshape(1, 64, 512)
    same = core == lax.axis_index("yh")
    kept, sent = jnp.where(same, mine, theirs), jnp.where(same, theirs, mine)
    w = jnp.concatenate([kept, permute(sent, lambda a, x, b, z, h: (a, x, b, z, 1 - h))], axis=0)
    w = jnp.concatenate([w, permute(w, lambda a, x, b, z, h: (a, x, 1 - b, z, h))], axis=0)
    f1, g1 = step(w, 1), step(w, -1)
    t0, dq = attend(0, span_order, queries, out_grad, lse2, delta, pair, dq_acc, False)
    t1, dq = attend(1, span_order, queries, out_grad, lse2, delta, pairs[1], dq, True)
    back1 = permute(t1, along_x(-1))
    dq, f1, g1 = lax.optimization_barrier((dq, f1, g1))
    f2, g2 = step(f1, 1), step(g1, -1)
    t3, dq = attend(3, span_order, queries, out_grad, lse2, delta, pairs[3], dq, True)
    back3 = permute(t3, along_x(-3))
    dq, back1, f2, g2 = lax.optimization_barrier((dq, back1, f2, g2))
    f3, g3 = step(f2, 1), step(g2, -1)
    t2, dq = attend(2, span_order, queries, out_grad, lse2, delta, pairs[2], dq, True)
    back2 = permute(t2, along_x(-2))
    back2, f3, g3 = lax.optimization_barrier((back2, f3, g3))
    f4 = step(f3, 1)
    back = (t0, back1, back3, back2)
    total = sum(t.astype(F32) for t in back).astype(BF16)
    r0, r1 = total[0], total[1]
    r0 = permute(r0, next_outer(0))
    r1 = permute(r1, next_outer(1))
    r0, f4 = lax.optimization_barrier((r0, f4))
    weights = [w, f1, f2, f3, f4, g3, g2, g1]
    dkv = dkv_acc.reshape(ROWS, 512) + (r0.astype(F32) + r1.astype(F32))
    dkvb = dkv.astype(BF16)

    swap = lambda a, x, b, z, h: (a, x, b, z, 1 - h)
    near = jnp.stack([permute(dkvb, along_x(s)) for s in (1, 2, 3)])
    alone = dkvb[None]
    parts = dx_parts(near, permute(near, swap), weights)
    got = [permute(part, along_x(-s)) for s, part in zip((1, 2, 3), parts)]
    own = dx_parts(alone, permute(alone, swap), weights)
    dx = pl.pallas_call(
        gather_body,
        in_specs=[vmem] * 4,
        out_specs=vmem,
        out_shape=jax.ShapeDtypeStruct((ROWS, 4096), BF16),
        cost_estimate=SMALL,
        name="join_parts",
    )(own[0], *got)
    return (dq, dkv.reshape(ROWS, 2, 256), dx)


def solution(mesh):
    fine = Mesh(mesh.devices.reshape(SIZES), AXES)
    tokens = ("yh", "x", "yl", "z")
    return jax.shard_map(
        shards,
        mesh=fine,
        in_specs=(
            P(tokens, "core"),
            P(tokens, "core"),
            P(tokens, "core"),
            P("core", tokens),
            P(tokens, None, "core"),
            P(),
            P(tokens, "core"),
            P(tokens, None, "core"),
            P(tokens, None, "core"),
        ),
        out_specs=(P(tokens, "core"), P(tokens, None, "core"), P(tokens, "core")),
        check_vma=False,
    )
```

time: 175 us -> 110 us (0.63)
  waiting for transfers between devices: 67.9 us -> 38.1 us
  local copies, waits for them, and re-layouts: 16.1 us -> 2.62 us
  Pallas kernels: 37.6 us -> 26.4 us
  starting transfers between devices: 49.9 us -> 39.8 us
    ppermute x33 -> x26, waiting for transfers between devices: 67.9 us -> 38.1 us  [permute(): return lax.ppermute(value, AXES, pairs)]
    unnamed x68 -> x24, local copies, waits for them, and re-layouts: 14.1 us -> 1.34 us
    pallas_call x7, Pallas kernels: 34 us -> 22.9 us  [the longest x4 18.5 us: attend(): pl.pallas_call(lambda *refs: attend_body(shift, *refs), in_specs=[pl.Bloc...]
    ppermute x33 -> x26, starting transfers between devices: 49.9 us -> 39.8 us  [permute(): return lax.ppermute(value, AXES, pairs)]
  transfers between devices with their start and end apart: 33 -> 26, of which waited for: 11 -> 14; matrix products, arithmetic and copies ran while one was open for 2% -> 1% of each run, Pallas kernels for 17% -> 17%
where the time goes in v2:
time: 110 us; the launch traced here: 109 us
  starting transfers between devices  39.8 us (36%)
  waiting for transfers between devices  38.1 us (35%)
  Pallas kernels  26.4 us (24%)
  local copies, waits for them, and re-layouts  2.62 us (2%)
  other arithmetic  1.55 us (1%)
    ppermute x26, starting transfers between devices, permute(): return lax.ppermute(value, AXES, pairs)  39.8 us
    ppermute x26, waiting for transfers between devices, permute(): return lax.ppermute(value, AXES, pairs)  38.1 us
    pallas_call x4, Pallas kernels, attend(): pl.pallas_call(lambda *refs: attend_body(shift, *refs), in_specs=[pl.Bloc...  18.5 us
    pallas_call x1, Pallas kernels, shards(): pl.pallas_call(delta_body, in_specs=[vmem] * 3, out_specs=[vmem] * 2, out...  3.54 us
    pallas_call x1, Pallas kernels, shards(): pl.pallas_call(gather_body, in_specs=[vmem] * 4, out_specs=vmem, out_shap...  2.24 us
  transfers between devices with their start and end apart: 26, of which 14 were waited for; matrix products, arithmetic and copies ran while one was open for 1% of the time, Pallas kernels for 17%

profile of v2, /device:TPU:1, one launch (start us, length us, event | category | flops | bytes accessed | tf_op | source)
XLA Modules:
  0.0 109.3 jit_solution(6297872531988399076)
XLA Ops:
  1.8 3.8 %collective-permute-start = (bf16[192,2,256]{2,1,0:T(2,128)(2,1)S(1)}, bf16[192,2,256]{2,1,0:T(2,128)(2,1)S(1)}, u32[]{:S(2)}, u32[]{:S(2)}) collective-permute-start(bf16[192,2,256]{2,1,0:T(2,128)(2,1)S(1)} %pad_maximum_fusion.1), channel_id=1, source_target_pairs={{0,128},{1,129},{2,130},{3,131},{4,132},{5,133},{6,134},{7,135},{8... | collective-permute-start | bytes 589832 | tf_op jit(solution)/shard_map/ppermute | solution.py:32
  5.7 3.5 %row_sums.1 = (f32[16,128]{1,0:T(8,128)}, f32[16,128]{1,0:T(8,128)}) custom-call(bf16[128,2048]{1,0:T(8,128)(2,1)} %refs_2_.7, bf16[128,2048]{1,0:T(8,128)(2,1)} %o_ref.1, f32[16,128]{1,0:T(8,128)} %lse_ref.1), custom_call_target="tpu_custom_call" | custom-call | flops 1000 | bytes 1000 | tf_op jit(solution)/shard_map/row_sums/pallas_call | solution.py:187
  10.4 2.5 %collective-permute-start.4 = (bf16[1,64,512]{2,1,0:T(8,128)(2,1)S(1)}, bf16[1,64,512]{2,1,0:T(8,128)(2,1)S(1)}, u32[]{:S(2)}, u32[]{:S(2)}) collective-permute-start(bf16[1,64,512]{2,1,0:T(8,128)(2,1)S(1)} %select_n.38), channel_id=1, source_target_pairs={{0,1},{1,0},{2,3},{3,2},{4,5},{5,4},{6,7},{7,6},{8,9},{9,8},{10,11... | collective-permute-start | bytes 196616 | tf_op jit(solution)/shard_map/ppermute | solution.py:32
  15.7 3.0 %collective-permute-done.5 = bf16[2,64,512]{2,1,0:T(8,128)(2,1)S(1)} collective-permute-done((bf16[2,64,512]{2,1,0:T(8,128)(2,1)S(1)}, bf16[2,64,512]{2,1,0:T(8,128)(2,1)S(1)}, u32[]{:S(2)}, u32[]{:S(2)}) %collective-permute-start.5) | collective-permute-done | bytes 131104 | tf_op jit(solution)/shard_map/ppermute | solution.py:32
  19.6 4.0 %collective-permute-start.7 = (bf16[4,64,512]{2,1,0:T(8,128)(2,1)S(1)}, bf16[4,64,512]{2,1,0:T(8,128)(2,1)S(1)}, u32[]{:S(2)}, u32[]{:S(2)}) collective-permute-start(bf16[4,64,512]{2,1,0:T(8,128)(2,1)S(1)} %constant_dynamic-update-slice_fusion.2.refs_0_), channel_id=1, source_target_pairs={{0,14},{1,15},{2,0},{3,1},{4,2},{5,3},{6,4},{7,5},{8,6},{9,7},{10,... | collective-permute-start | bytes 786440 | tf_op jit(solution)/shard_map/ppermute | solution.py:32
  23.6 2.5 %collective-permute-start.2 = (bf16[2,128,512]{2,1,0:T(8,128)(2,1)S(1)}, bf16[2,128,512]{2,1,0:T(8,128)(2,1)S(1)}, u32[]{:S(2)}, u32[]{:S(2)}) collective-permute-start(bf16[2,128,512]{2,1,0:T(8,128)(2,1)S(1)} %constant_dynamic-update-slice_fusion.refs_5_), channel_id=1, source_target_pairs={{0,96},{1,97},{2,98},{3,99},{4,100},{5,101},{6,102},{7,103},{8,104... | collective-permute-start | bytes 786440 | tf_op jit(solution)/shard_map/ppermute | solution.py:32
  26.1 4.1 %attend.4 = (bf16[2,128,512]{2,1,0:T(8,128)(2,1)S(1)}, f32[128,2048]{1,0:T(8,128)}) custom-call(s32[256]{0:T(256)S(1)} %copy-done.6, bf16[128,2048]{1,0:T(8,128)(2,1)S(1)} %copy-done.1, bf16[128,2048]{1,0:T(8,128)(2,1)S(1)} %copy-done, f32[16,128]{1,0:T(8,128)S(1)} %copy-done.5, f32[16,128]{1,0:T(8,128)S(1)} %copy-done.4, ...), custom_call_target="tpu_custom_call" | custom-call | flops 1000 | bytes 1000 | tf_op jit(solution)/shard_map/attend/pallas_call | solution.py:117
  30.2 4.8 %attend.5 = (bf16[2,128,512]{2,1,0:T(8,128)(2,1)S(1)}, f32[128,2048]{1,0:T(8,128)}) custom-call(s32[256]{0:T(256)S(1)} %copy-done.6, bf16[128,2048]{1,0:T(8,128)(2,1)S(1)} %copy-done.1, bf16[128,2048]{1,0:T(8,128)(2,1)S(1)} %copy-done, f32[16,128]{1,0:T(8,128)S(1)} %copy-done.5, f32[16,128]{1,0:T(8,128)S(1)} %copy-done.4, ...), custom_call_target="tpu_custom_call", output_to_operand_aliasing={{1}: (6, {})} | custom-call | flops 1000 | bytes 1000 | tf_op jit(solution)/shard_map/attend/pallas_call | solution.py:117
  37.4 4.8 %attend.6 = (bf16[2,128,512]{2,1,0:T(8,128)(2,1)S(1)}, f32[128,2048]{1,0:T(8,128)}) custom-call(s32[256]{0:T(256)S(1)} %copy-done.6, bf16[128,2048]{1,0:T(8,128)(2,1)S(1)} %copy-done.1, bf16[128,2048]{1,0:T(8,128)(2,1)S(1)} %copy-done, f32[16,128]{1,0:T(8,128)S(1)} %copy-done.5, f32[16,128]{1,0:T(8,128)S(1)} %copy-done.4, ...), custom_call_target="tpu_custom_call", output_to_operand_aliasing={{1}: (6, {})} | custom-call | flops 1000 | bytes 1000 | tf_op jit(solution)/shard_map/attend/pallas_call | solution.py:117
  43.8 4.8 %attend.7 = (bf16[2,128,512]{2,1,0:T(8,128)(2,1)S(1)}, f32[128,2048]{1,0:T(8,128)}) custom-call(s32[256]{0:T(256)S(1)} %copy-done.6, bf16[128,2048]{1,0:T(8,128)(2,1)S(1)} %copy-done.1, bf16[128,2048]{1,0:T(8,128)(2,1)S(1)} %copy-done, f32[16,128]{1,0:T(8,128)S(1)} %copy-done.5, f32[16,128]{1,0:T(8,128)S(1)} %copy-done.4, ...), custom_call_target="tpu_custom_call", output_to_operand_aliasing={{1}: (6, {})} | custom-call | flops 1000 | bytes 1000 | tf_op jit(solution)/shard_map/attend/pallas_call | solution.py:117
  49.7 2.7 %collective-permute-start.14 = (bf16[4,64,512]{2,1,0:T(8,128)(2,1)S(1)}, bf16[4,64,512]{2,1,0:T(8,128)(2,1)S(1)}, u32[]{:S(2)}, u32[]{:S(2)}) collective-permute-start(bf16[4,64,512]{2,1,0:T(8,128)(2,1)S(1)} %collective-permute-done.10.refs_6_), channel_id=1, source_target_pairs={{0,14},{1,15},{2,0},{3,1},{4,2},{5,3},{6,4},{7,5},{8,6},{9,7},{10,... | collective-permute-start | bytes 786440 | tf_op jit(solution)/shard_map/ppermute | solution.py:32
  52.3 4.8 %collective-permute-start.11 = (bf16[2,128,512]{2,1,0:T(8,128)(2,1)S(1)}, bf16[2,128,512]{2,1,0:T(8,128)(2,1)S(1)}, u32[]{:S(2)}, u32[]{:S(2)}) collective-permute-start(bf16[2,128,512]{2,1,0:T(8,128)(2,1)S(1)} %get-tuple-element.47), channel_id=1, source_target_pairs={{0,32},{1,33},{2,34},{3,35},{4,36},{5,37},{6,38},{7,39},{8,40},{9,... | collective-permute-start | bytes 786440 | tf_op jit(solution)/shard_map/ppermute | solution.py:32
  57.3 6.5 %collective-permute-done.11 = bf16[2,128,512]{2,1,0:T(8,128)(2,1)S(1)} collective-permute-done((bf16[2,128,512]{2,1,0:T(8,128)(2,1)S(1)}, bf16[2,128,512]{2,1,0:T(8,128)(2,1)S(1)}, u32[]{:S(2)}, u32[]{:S(2)}) %collective-permute-start.11) | collective-permute-done | bytes 262176 | tf_op jit(solution)/shard_map/ppermute | solution.py:32
  64.4 2.7 %collective-permute-start.17 = (bf16[128,512]{1,0:T(8,128)(2,1)S(1)}, bf16[128,512]{1,0:T(8,128)(2,1)S(1)}, u32[]{:S(2)}, u32[]{:S(2)}) collective-permute-start(bf16[128,512]{1,0:T(8,128)(2,1)S(1)} %get-tuple-element.62), channel_id=1, source_target_pairs={{0,130},{1,131},{2,132},{3,133},{4,134},{5,135},{6,136},{7,137},{8... | collective-permute-start | bytes 393224 | tf_op jit(solution)/shard_map/ppermute | solution.py:32
  67.2 4.2 %collective-permute-done.15 = bf16[128,512]{1,0:T(8,128)(2,1)S(1)} collective-permute-done((bf16[128,512]{1,0:T(8,128)(2,1)S(1)}, bf16[128,512]{1,0:T(8,128)(2,1)S(1)}, u32[]{:S(2)}, u32[]{:S(2)}) %collective-permute-start.15) | collective-permute-done | bytes 131104 | tf_op jit(solution)/shard_map/ppermute | solution.py:32
  71.4 4.9 %collective-permute-done.17 = bf16[128,512]{1,0:T(8,128)(2,1)S(1)} collective-permute-done((bf16[128,512]{1,0:T(8,128)(2,1)S(1)}, bf16[128,512]{1,0:T(8,128)(2,1)S(1)}, u32[]{:S(2)}, u32[]{:S(2)}) %collective-permute-start.17) | collective-permute-done | bytes 131104 | tf_op jit(solution)/shard_map/ppermute | solution.py:32
  76.8 2.5 %collective-permute-start.21 = (bf16[128,512]{1,0:T(8,128)(2,1)S(1)}, bf16[128,512]{1,0:T(8,128)(2,1)S(1)}, u32[]{:S(2)}, u32[]{:S(2)}) collective-permute-start(bf16[128,512]{1,0:T(8,128)(2,1)S(1)} %get-tuple-element.59), channel_id=1, source_target_pairs={{0,96},{1,97},{2,98},{3,99},{4,100},{5,101},{6,102},{7,103},{8,104... | collective-permute-start | bytes 393224 | tf_op jit(solution)/shard_map/ppermute | solution.py:32
  79.2 4.6 %collective-permute-done.19 = bf16[128,512]{1,0:T(8,128)(2,1)S(1)} collective-permute-done((bf16[128,512]{1,0:T(8,128)(2,1)S(1)}, bf16[128,512]{1,0:T(8,128)(2,1)S(1)}, u32[]{:S(2)}, u32[]{:S(2)}) %collective-permute-start.19) | collective-permute-done | bytes 131104 | tf_op jit(solution)/shard_map/ppermute | solution.py:32
  84.3 3.0 %collective-permute-start.22 = (bf16[3,128,512]{2,1,0:T(8,128)(2,1)S(1)}, bf16[3,128,512]{2,1,0:T(8,128)(2,1)S(1)}, u32[]{:S(2)}, u32[]{:S(2)}) collective-permute-start(bf16[3,128,512]{2,1,0:T(8,128)(2,1)S(1)} %pad_maximum_fusion.own_ref), channel_id=1, source_target_pairs={{0,1},{1,0},{2,3},{3,2},{4,5},{5,4},{6,7},{7,6},{8,9},{9,8},{10,11... | collective-permute-start | bytes 1179656 | tf_op jit(solution)/shard_map/ppermute | solution.py:32
  89.8 2.5 %collective-permute-start.23 = (bf16[128,1024]{1,0:T(8,128)(2,1)S(1)}, bf16[128,1024]{1,0:T(8,128)(2,1)}, u32[]{:S(2)}, u32[]{:S(2)}) collective-permute-start(bf16[128,1024]{1,0:T(8,128)(2,1)S(1)} %get-tuple-element.56), channel_id=1, source_target_pairs={{0,96},{1,97},{2,98},{3,99},{4,100},{5,101},{6,102},{7,103},{8,104... | collective-permute-start | bytes 786440 | tf_op jit(solution)/shard_map/ppermute | solution.py:32
  96.5 1.7 %collective-permute-done.23.refs_1_ = bf16[128,1024]{1,0:T(8,128)(2,1)} collective-permute-done((bf16[128,1024]{1,0:T(8,128)(2,1)S(1)}, bf16[128,1024]{1,0:T(8,128)(2,1)}, u32[]{:S(2)}, u32[]{:S(2)}) %collective-permute-start.23) | collective-permute-done | bytes 262176 | tf_op jit(solution)/shard_map/ppermute | solution.py:32
  98.2 2.9 %collective-permute-done.24.refs_2_ = bf16[128,1024]{1,0:T(8,128)(2,1)} collective-permute-done((bf16[128,1024]{1,0:T(8,128)(2,1)S(1)}, bf16[128,1024]{1,0:T(8,128)(2,1)}, u32[]{:S(2)}, u32[]{:S(2)}) %collective-permute-start.24) | collective-permute-done | bytes 262176 | tf_op jit(solution)/shard_map/ppermute | solution.py:32
  101.1 5.9 %collective-permute-done.25.refs_3_ = bf16[128,1024]{1,0:T(8,128)(2,1)} collective-permute-done((bf16[128,1024]{1,0:T(8,128)(2,1)S(1)}, bf16[128,1024]{1,0:T(8,128)(2,1)}, u32[]{:S(2)}, u32[]{:S(2)}) %collective-permute-start.25) | collective-permute-done | bytes 262176 | tf_op jit(solution)/shard_map/ppermute | solution.py:32
  107.1 2.2 %join_parts.1 = bf16[128,4096]{1,0:T(8,128)(2,1)} custom-call(bf16[128,1024]{1,0:T(8,128)(2,1)} %copy-done.3, bf16[128,1024]{1,0:T(8,128)(2,1)} %collective-permute-done.23.refs_1_, bf16[128,1024]{1,0:T(8,128)(2,1)} %collective-permute-done.24.refs_2_, bf16[128,1024]{1,0:T(8,128)(2,1)} %collective-permute-done.25.refs_3_), custom_call_target="tpu_custom_call" | custom-call | flops 1000 | bytes 1000 | tf_op jit(solution)/shard_map/join_parts/pallas_call | solution.py:235
  (75 shorter events, 19.5 us)
Async XLA Ops:
  1.8 7.5 %collective-permute-start = (bf16[192,2,256]{2,1,0:T(2,128)(2,1)S(1)}, bf16[192,2,256]{2,1,0:T(2,128)(2,1)S(1)}, u32[]{:S(2)}, u32[]{:S(2)}) collective-permute-start(bf16[192,2,256]{2,1,0:T(2,128)(2,1)S(1)} %pad_maximum_fusion.1), channel_id=1, source_target_pairs={{0,128},{1,129},{2,130},{3,131},{4,132},{5,133},{6,134},{7,135},{8... | collective-permute-start | bytes 589832 | tf_op jit(solution)/shard_map/ppermute | solution.py:32
  13.8 4.8 %collective-permute-start.5 = (bf16[2,64,512]{2,1,0:T(8,128)(2,1)S(1)}, bf16[2,64,512]{2,1,0:T(8,128)(2,1)S(1)}, u32[]{:S(2)}, u32[]{:S(2)}) collective-permute-start(bf16[2,64,512]{2,1,0:T(8,128)(2,1)S(1)} %pad_maximum_fusion.2), channel_id=1, source_target_pairs={{0,16},{1,17},{2,18},{3,19},{4,20},{5,21},{6,22},{7,23},{8,24},{9,... | collective-permute-start | bytes 393224 | tf_op jit(solution)/shard_map/ppermute | solution.py:32
  14.4 15.8 %collective-permute-start.3 = (bf16[2,128,512]{2,1,0:T(8,128)(2,1)S(1)}, bf16[2,128,512]{2,1,0:T(8,128)(2,1)S(1)}, u32[]{:S(2)}, u32[]{:S(2)}) collective-permute-start(bf16[2,128,512]{2,1,0:T(8,128)(2,1)S(1)} %constant_dynamic-update-slice_fusion.refs_5_), channel_id=1, source_target_pairs={{0,32},{1,33},{2,34},{3,35},{4,36},{5,37},{6,38},{7,39},{8,40},{9,... | collective-permute-start | bytes 786440 | tf_op jit(solution)/shard_map/ppermute | solution.py:32
  18.6 17.0 %collective-permute-start.6 = (bf16[4,64,512]{2,1,0:T(8,128)(2,1)S(1)}, bf16[4,64,512]{2,1,0:T(8,128)(2,1)S(1)}, u32[]{:S(2)}, u32[]{:S(2)}) collective-permute-start(bf16[4,64,512]{2,1,0:T(8,128)(2,1)S(1)} %constant_dynamic-update-slice_fusion.2.refs_0_), channel_id=1, source_target_pairs={{0,2},{1,3},{2,4},{3,5},{4,6},{5,7},{6,8},{7,9},{8,10},{9,11},{10,... | collective-permute-start | bytes 786440 | tf_op jit(solution)/shard_map/ppermute | solution.py:32
  19.6 16.0 %collective-permute-start.7 = (bf16[4,64,512]{2,1,0:T(8,128)(2,1)S(1)}, bf16[4,64,512]{2,1,0:T(8,128)(2,1)S(1)}, u32[]{:S(2)}, u32[]{:S(2)}) collective-permute-start(bf16[4,64,512]{2,1,0:T(8,128)(2,1)S(1)} %constant_dynamic-update-slice_fusion.2.refs_0_), channel_id=1, source_target_pairs={{0,14},{1,15},{2,0},{3,1},{4,2},{5,3},{6,4},{7,5},{8,6},{9,7},{10,... | collective-permute-start | bytes 786440 | tf_op jit(solution)/shard_map/ppermute | solution.py:32
  23.6 13.7 %collective-permute-start.2 = (bf16[2,128,512]{2,1,0:T(8,128)(2,1)S(1)}, bf16[2,128,512]{2,1,0:T(8,128)(2,1)S(1)}, u32[]{:S(2)}, u32[]{:S(2)}) collective-permute-start(bf16[2,128,512]{2,1,0:T(8,128)(2,1)S(1)} %constant_dynamic-update-slice_fusion.refs_5_), channel_id=1, source_target_pairs={{0,96},{1,97},{2,98},{3,99},{4,100},{5,101},{6,102},{7,103},{8,104... | collective-permute-start | bytes 786440 | tf_op jit(solution)/shard_map/ppermute | solution.py:32
  35.1 7.1 %collective-permute-start.8 = (bf16[2,128,512]{2,1,0:T(8,128)(2,1)S(1)}, bf16[2,128,512]{2,1,0:T(8,128)(2,1)S(1)}, u32[]{:S(2)}, u32[]{:S(2)}) collective-permute-start(bf16[2,128,512]{2,1,0:T(8,128)(2,1)S(1)} %get-tuple-element.40), channel_id=1, source_target_pairs={{0,96},{1,97},{2,98},{3,99},{4,100},{5,101},{6,102},{7,103},{8,104... | collective-permute-start | bytes 786440 | tf_op jit(solution)/shard_map/ppermute | solution.py:32
  35.6 6.6 %collective-permute-start.10 = (bf16[4,64,512]{2,1,0:T(8,128)(2,1)S(1)}, bf16[4,64,512]{2,1,0:T(8,128)(2,1)S(1)}, u32[]{:S(2)}, u32[]{:S(2)}) collective-permute-start(bf16[4,64,512]{2,1,0:T(8,128)(2,1)S(1)} %collective-permute-done.7.refs_7_), channel_id=1, source_target_pairs={{0,14},{1,15},{2,0},{3,1},{4,2},{5,3},{6,4},{7,5},{8,6},{9,7},{10,... | collective-permute-start | bytes 786440 | tf_op jit(solution)/shard_map/ppermute | solution.py:32
  37.0 6.4 %collective-permute-start.9 = (bf16[4,64,512]{2,1,0:T(8,128)(2,1)S(1)}, bf16[4,64,512]{2,1,0:T(8,128)(2,1)S(1)}, u32[]{:S(2)}, u32[]{:S(2)}) collective-permute-start(bf16[4,64,512]{2,1,0:T(8,128)(2,1)S(1)} %collective-permute-done.6.refs_1_), channel_id=1, source_target_pairs={{0,2},{1,3},{2,4},{3,5},{4,6},{5,7},{6,8},{7,9},{8,10},{9,11},{10,... | collective-permute-start | bytes 786440 | tf_op jit(solution)/shard_map/ppermute | solution.py:32
  37.1 6.7 %collective-permute-start.1 = (bf16[2,128,512]{2,1,0:T(8,128)(2,1)S(1)}, bf16[2,128,512]{2,1,0:T(8,128)(2,1)S(1)}, u32[]{:S(2)}, u32[]{:S(2)}) collective-permute-start(bf16[2,128,512]{2,1,0:T(8,128)(2,1)S(1)} %constant_dynamic-update-slice_fusion.refs_5_), channel_id=1, source_target_pairs={{0,64},{1,65},{2,66},{3,67},{4,68},{5,69},{6,70},{7,71},{8,72},{9,... | collective-permute-start | bytes 786440 | tf_op jit(solution)/shard_map/ppermute | solution.py:32
  48.6 8.6 %collective-permute-start.12 = (bf16[2,128,512]{2,1,0:T(8,128)(2,1)S(1)}, bf16[2,128,512]{2,1,0:T(8,128)(2,1)S(1)}, u32[]{:S(2)}, u32[]{:S(2)}) collective-permute-start(bf16[2,128,512]{2,1,0:T(8,128)(2,1)S(1)} %get-tuple-element.48), channel_id=1, source_target_pairs={{0,64},{1,65},{2,66},{3,67},{4,68},{5,69},{6,70},{7,71},{8,72},{9,... | collective-permute-start | bytes 786440 | tf_op jit(solution)/shard_map/ppermute | solution.py:32
  49.7 7.5 %collective-permute-start.13 = (bf16[4,64,512]{2,1,0:T(8,128)(2,1)S(1)}, bf16[4,64,512]{2,1,0:T(8,128)(2,1)S(1)}, u32[]{:S(2)}, u32[]{:S(2)}) collective-permute-start(bf16[4,64,512]{2,1,0:T(8,128)(2,1)S(1)} %collective-permute-done.9.refs_2_), channel_id=1, source_target_pairs={{0,2},{1,3},{2,4},{3,5},{4,6},{5,7},{6,8},{7,9},{8,10},{9,11},{10,... | collective-permute-start | bytes 786440 | tf_op jit(solution)/shard_map/ppermute | solution.py:32
  49.7 7.5 %collective-permute-start.14 = (bf16[4,64,512]{2,1,0:T(8,128)(2,1)S(1)}, bf16[4,64,512]{2,1,0:T(8,128)(2,1)S(1)}, u32[]{:S(2)}, u32[]{:S(2)}) collective-permute-start(bf16[4,64,512]{2,1,0:T(8,128)(2,1)S(1)} %collective-permute-done.10.refs_6_), channel_id=1, source_target_pairs={{0,14},{1,15},{2,0},{3,1},{4,2},{5,3},{6,4},{7,5},{8,6},{9,7},{10,... | collective-permute-start | bytes 786440 | tf_op jit(solution)/shard_map/ppermute | solution.py:32
  52.3 11.4 %collective-permute-start.11 = (bf16[2,128,512]{2,1,0:T(8,128)(2,1)S(1)}, bf16[2,128,512]{2,1,0:T(8,128)(2,1)S(1)}, u32[]{:S(2)}, u32[]{:S(2)}) collective-permute-start(bf16[2,128,512]{2,1,0:T(8,128)(2,1)S(1)} %get-tuple-element.47), channel_id=1, source_target_pairs={{0,32},{1,33},{2,34},{3,35},{4,36},{5,37},{6,38},{7,39},{8,40},{9,... | collective-permute-start | bytes 786440 | tf_op jit(solution)/shard_map/ppermute | solution.py:32
  57.2 14.2 %collective-permute-start.16 = (bf16[4,64,512]{2,1,0:T(8,128)(2,1)S(1)}, bf16[4,64,512]{2,1,0:T(8,128)(2,1)S(1)}, u32[]{:S(2)}, u32[]{:S(2)}) collective-permute-start(bf16[4,64,512]{2,1,0:T(8,128)(2,1)S(1)} %collective-permute-done.13.refs_3_), channel_id=1, source_target_pairs={{0,2},{1,3},{2,4},{3,5},{4,6},{5,7},{6,8},{7,9},{8,10},{9,11},{10,... | collective-permute-start | bytes 786440 | tf_op jit(solution)/shard_map/ppermute | solution.py:32
  63.9 7.4 %collective-permute-start.15 = (bf16[128,512]{1,0:T(8,128)(2,1)S(1)}, bf16[128,512]{1,0:T(8,128)(2,1)S(1)}, u32[]{:S(2)}, u32[]{:S(2)}) collective-permute-start(bf16[128,512]{1,0:T(8,128)(2,1)S(1)} %get-tuple-element.61), channel_id=1, source_target_pairs={{0,2},{1,3},{2,4},{3,5},{4,6},{5,7},{6,8},{7,9},{8,10},{9,11},{10,... | collective-permute-start | bytes 393224 | tf_op jit(solution)/shard_map/ppermute | solution.py:32
  64.4 11.8 %collective-permute-start.17 = (bf16[128,512]{1,0:T(8,128)(2,1)S(1)}, bf16[128,512]{1,0:T(8,128)(2,1)S(1)}, u32[]{:S(2)}, u32[]{:S(2)}) collective-permute-start(bf16[128,512]{1,0:T(8,128)(2,1)S(1)} %get-tuple-element.62), channel_id=1, source_target_pairs={{0,130},{1,131},{2,132},{3,133},{4,134},{5,135},{6,136},{7,137},{8... | collective-permute-start | bytes 393224 | tf_op jit(solution)/shard_map/ppermute | solution.py:32
  76.3 7.6 %collective-permute-start.19 = (bf16[128,512]{1,0:T(8,128)(2,1)S(1)}, bf16[128,512]{1,0:T(8,128)(2,1)S(1)}, u32[]{:S(2)}, u32[]{:S(2)}) collective-permute-start(bf16[128,512]{1,0:T(8,128)(2,1)S(1)} %get-tuple-element.59), channel_id=1, source_target_pairs={{0,32},{1,33},{2,34},{3,35},{4,36},{5,37},{6,38},{7,39},{8,40},{9,... | collective-permute-start | bytes 393224 | tf_op jit(solution)/shard_map/ppermute | solution.py:32
  76.6 7.3 %collective-permute-start.20 = (bf16[128,512]{1,0:T(8,128)(2,1)S(1)}, bf16[128,512]{1,0:T(8,128)(2,1)S(1)}, u32[]{:S(2)}, u32[]{:S(2)}) collective-permute-start(bf16[128,512]{1,0:T(8,128)(2,1)S(1)} %get-tuple-element.59), channel_id=1, source_target_pairs={{0,64},{1,65},{2,66},{3,67},{4,68},{5,69},{6,70},{7,71},{8,72},{9,... | collective-permute-start | bytes 393224 | tf_op jit(solution)/shard_map/ppermute | solution.py:32
  76.8 7.4 %collective-permute-start.21 = (bf16[128,512]{1,0:T(8,128)(2,1)S(1)}, bf16[128,512]{1,0:T(8,128)(2,1)S(1)}, u32[]{:S(2)}, u32[]{:S(2)}) collective-permute-start(bf16[128,512]{1,0:T(8,128)(2,1)S(1)} %get-tuple-element.59), channel_id=1, source_target_pairs={{0,96},{1,97},{2,98},{3,99},{4,100},{5,101},{6,102},{7,103},{8,104... | collective-permute-start | bytes 393224 | tf_op jit(solution)/shard_map/ppermute | solution.py:32
  84.3 4.3 %collective-permute-start.22 = (bf16[3,128,512]{2,1,0:T(8,128)(2,1)S(1)}, bf16[3,128,512]{2,1,0:T(8,128)(2,1)S(1)}, u32[]{:S(2)}, u32[]{:S(2)}) collective-permute-start(bf16[3,128,512]{2,1,0:T(8,128)(2,1)S(1)} %pad_maximum_fusion.own_ref), channel_id=1, source_target_pairs={{0,1},{1,0},{2,3},{3,2},{4,5},{5,4},{6,7},{7,6},{8,9},{9,8},{10,11... | collective-permute-start | bytes 1179656 | tf_op jit(solution)/shard_map/ppermute | solution.py:32
  89.8 8.5 %collective-permute-start.23 = (bf16[128,1024]{1,0:T(8,128)(2,1)S(1)}, bf16[128,1024]{1,0:T(8,128)(2,1)}, u32[]{:S(2)}, u32[]{:S(2)}) collective-permute-start(bf16[128,1024]{1,0:T(8,128)(2,1)S(1)} %get-tuple-element.56), channel_id=1, source_target_pairs={{0,96},{1,97},{2,98},{3,99},{4,100},{5,101},{6,102},{7,103},{8,104... | collective-permute-start | bytes 786440 | tf_op jit(solution)/shard_map/ppermute | solution.py:32
  92.2 8.9 %collective-permute-start.24 = (bf16[128,1024]{1,0:T(8,128)(2,1)S(1)}, bf16[128,1024]{1,0:T(8,128)(2,1)}, u32[]{:S(2)}, u32[]{:S(2)}) collective-permute-start(bf16[128,1024]{1,0:T(8,128)(2,1)S(1)} %get-tuple-element.57), channel_id=1, source_target_pairs={{0,64},{1,65},{2,66},{3,67},{4,68},{5,69},{6,70},{7,71},{8,72},{9,... | collective-permute-start | bytes 786440 | tf_op jit(solution)/shard_map/ppermute | solution.py:32
  92.3 14.8 %collective-permute-start.25 = (bf16[128,1024]{1,0:T(8,128)(2,1)S(1)}, bf16[128,1024]{1,0:T(8,128)(2,1)}, u32[]{:S(2)}, u32[]{:S(2)}) collective-permute-start(bf16[128,1024]{1,0:T(8,128)(2,1)S(1)} %get-tuple-element.58), channel_id=1, source_target_pairs={{0,32},{1,33},{2,34},{3,35},{4,36},{5,37},{6,38},{7,39},{8,40},{9,... | collective-permute-start | bytes 786440 | tf_op jit(solution)/shard_map/ppermute | solution.py:32
  (12 other events, 109.7 us)

commit v3 on v2

--- a/solution.py
+++ b/solution.py
@@ -57,7 +57,7 @@
     lse2_ref[...] = lse_ref[...] * LOG2E
 
 
-def attend_body(shift, spans, q_ref, do_ref, lse_ref, delta_ref, kv_ref, dqin_ref, terms_ref, dq_ref):
+def attend_body(shift, spans, q_ref, do_ref, lse_ref, delta_ref, kv_ref, terms_ref, ds_ref):
     yh = lax.axis_index("yh")
     x = lax.axis_index("x")
     outer = lax.axis_index("yl") * 8 + lax.axis_index("z")
@@ -101,9 +101,7 @@
             dk_t = jnp.dot(ds, q2, preferred_element_type=F32)
             dk = dk_t if dk is None else dk + dk_t
             dv = dv_t if dv is None else dv + dv_t
-            dq = lax.dot_general(ds, keys, (((0,), (0,)), ((), ())), preferred_element_type=F32)
-            dq_ref[:, c0] = dqin_ref[:, c0] + dq[:ROWS] * SCALE
-            dq_ref[:, c1] = dqin_ref[:, c1] + dq[ROWS:] * SCALE
+            ds_ref[:, h0 * HD : (h0 + 2) * HD] = ds
         dk = (dk * SCALE).astype(BF16)
         dv = dv.astype(BF16)
         terms_ref[0, :, at] = dk[:ROWS]
@@ -112,21 +110,36 @@
         terms_ref[1, :, at_v] = dv[ROWS:]
 
 
-def attend(shift, spans, q, do, lse2, delta, kvp, dq_in, alias):
+def attend(shift, spans, q, do, lse2, delta, kvp):
     vmem = pl.BlockSpec(memory_space=pltpu.VMEM)
     return pl.pallas_call(
         lambda *refs: attend_body(shift, *refs),
-        in_specs=[pl.BlockSpec(memory_space=pltpu.SMEM)] + [vmem] * 6,
+        in_specs=[pl.BlockSpec(memory_space=pltpu.SMEM)] + [vmem] * 5,
         out_specs=[vmem] * 2,
         out_shape=[
             jax.ShapeDtypeStruct((2, ROWS, 512), BF16),
-            jax.ShapeDtypeStruct((ROWS, 2048), F32),
+            jax.ShapeDtypeStruct((2 * ROWS, 2048), BF16),
         ],
-        input_output_aliases={6: 1} if alias else {},
         compiler_params=pltpu.CompilerParams(vmem_limit_bytes=24 * MIB),
         cost_estimate=SMALL,
         name="attend",
-    )(spans, q, do, lse2, delta, kvp, dq_in)
+    )(spans, q, do, lse2, delta, kvp)
+
+
+def dq_body(*refs):
+    kv_refs, ds_refs, acc_ref, out_ref = refs[:4], refs[4:8], refs[8], refs[9]
+    for head in range(2):
+        at = slice(head * HD, (head + 1) * HD)
+        keys = [jnp.concatenate([kv[0, :, at], kv[1, :, at]], axis=0).T for kv in kv_refs]
+        for pair in range(4):
+            h0 = head * 8 + pair * 2
+            total = None
+            for k in range(4):
+                got = jnp.dot(keys[k], ds_refs[k][:, h0 * HD : (h0 + 2) * HD], preferred_element_type=F32)
+                total = got if total is None else total + got
+            for n in range(2):
+                cols = slice((h0 + n) * HD, (h0 + n + 1) * HD)
+                out_ref[:, cols] = acc_ref[:, cols] + total[:, n * HD : (n + 1) * HD].T * SCALE
 
 
 def dx_body(own_ref, other_ref, *refs):
@@ -168,17 +181,24 @@
     )(own, other, *weights)
 
 
-def gather_body(*refs):
-    out_ref = refs[4]
+def gather_body(p0, p1, p2, p3, out_ref, sems):
     x = lax.axis_index("x")
-    for s in range(4):
-        to = lax.rem(x + s, 4) * 1024
-        out_ref[:, pl.ds(pl.multiple_of(to, 1024), 1024)] = refs[s][...]
+    copies = []
+    for s, ref in enumerate((p0, p1, p2, p3)):
+        to = pl.multiple_of(lax.rem(x + s, 4) * 1024, 1024)
+        copies.append(pltpu.make_async_copy(ref, out_ref.at[:, pl.ds(to, 1024)], sems.at[s]))
+    for copy in copies:
+        copy.start()
+    for copy in copies:
+        copy.wait()
 
 
 def shards(queries, out_grad, outputs, log_norm, kv_held, span_order, dq_acc, dkv_acc, kv_weight):
     vmem = pl.BlockSpec(memory_space=pltpu.VMEM)
-    both = permute(jnp.concatenate([kv_held, kv_weight], axis=0), lambda a, x, b, z, h: (1 - a, x, b, z, h))
+    across = lambda a, x, b, z, h: (1 - a, x, b, z, h)
+    kvy = permute(kv_held, across)
+    mine = kv_weight.reshape(1, 64, 512)
+    theirs = permute(mine, across)
     core = lax.axis_index("core")
 
     def step(value, by):
@@ -192,42 +212,56 @@
         cost_estimate=SMALL,
         name="row_sums",
     )(out_grad, outputs, log_norm)
-    both, delta, lse2 = lax.optimization_barrier((both, delta, lse2))
-    pair = jnp.stack([kv_held, both[:ROWS]]).reshape(2, ROWS, 512)
+    kvy, delta, lse2 = lax.optimization_barrier((kvy, delta, lse2))
+    pair = jnp.stack([kv_held, kvy]).reshape(2, ROWS, 512)
     pairs = {s: permute(pair, along_x(s)) for s in (1, 3, 2)}
 
-    mine = kv_weight.reshape(1, 64, 512)
-    theirs = both[ROWS:].reshape(1, 64, 512)
+    def run(s, kvp):
+        return attend(s, span_order, queries, out_grad, lse2, delta, kvp)
+
+    pair, theirs = lax.optimization_barrier((pair, theirs))
     same = core == lax.axis_index("yh")
     kept, sent = jnp.where(same, mine, theirs), jnp.where(same, theirs, mine)
     w = jnp.concatenate([kept, permute(sent, lambda a, x, b, z, h: (a, x, b, z, 1 - h))], axis=0)
     w = jnp.concatenate([w, permute(w, lambda a, x, b, z, h: (a, x, 1 - b, z, h))], axis=0)
     f1, g1 = step(w, 1), step(w, -1)
-    t0, dq = attend(0, span_order, queries, out_grad, lse2, delta, pair, dq_acc, False)
-    t1, dq = attend(1, span_order, queries, out_grad, lse2, delta, pairs[1], dq, True)
+    pairs[1], pairs[3], pairs[2] = lax.optimization_barrier((pairs[1], pairs[3], pairs[2]))
+    t1, ds1 = run(1, pairs[1])
     back1 = permute(t1, along_x(-1))
-    dq, f1, g1 = lax.optimization_barrier((dq, f1, g1))
+    ds1, pairs[3] = lax.optimization_barrier((ds1, pairs[3]))
+    t3, ds3 = run(3, pairs[3])
+    back3 = permute(t3, along_x(-3))
+    ds3, pairs[2], f1, g1 = lax.optimization_barrier((ds3, pairs[2], f1, g1))
+    t2, ds2 = run(2, pairs[2])
+    back2 = permute(t2, along_x(-2))
     f2, g2 = step(f1, 1), step(g1, -1)
-    t3, dq = attend(3, span_order, queries, out_grad, lse2, delta, pairs[3], dq, True)
-    back3 = permute(t3, along_x(-3))
-    dq, back1, f2, g2 = lax.optimization_barrier((dq, back1, f2, g2))
+    ds2, own_pair = lax.optimization_barrier((ds2, pair))
+    t0, ds0 = run(0, own_pair)
+    back2, f2, g2 = lax.optimization_barrier((back2, f2, g2))
     f3, g3 = step(f2, 1), step(g2, -1)
-    t2, dq = attend(2, span_order, queries, out_grad, lse2, delta, pairs[2], dq, True)
-    back2 = permute(t2, along_x(-2))
-    back2, f3, g3 = lax.optimization_barrier((back2, f3, g3))
-    f4 = step(f3, 1)
     back = (t0, back1, back3, back2)
+    dq = pl.pallas_call(
+        dq_body,
+        in_specs=[vmem] * 9,
+        out_specs=vmem,
+        out_shape=jax.ShapeDtypeStruct((ROWS, 2048), F32),
+        compiler_params=pltpu.CompilerParams(vmem_limit_bytes=24 * MIB),
+        cost_estimate=pl.CostEstimate(flops=1000, bytes_accessed=12_000_000, transcendentals=0),
+        name="query_grad",
+    )(pair, pairs[1], pairs[3], pairs[2], ds0, ds1, ds3, ds2, dq_acc)
     total = sum(t.astype(F32) for t in back).astype(BF16)
     r0, r1 = total[0], total[1]
     r0 = permute(r0, next_outer(0))
     r1 = permute(r1, next_outer(1))
-    r0, f4 = lax.optimization_barrier((r0, f4))
-    weights = [w, f1, f2, f3, f4, g3, g2, g1]
+    r0, f3, g3, dq = lax.optimization_barrier((r0, f3, g3, dq))
+    f4 = step(f3, 1)
     dkv = dkv_acc.reshape(ROWS, 512) + (r0.astype(F32) + r1.astype(F32))
     dkvb = dkv.astype(BF16)
 
     swap = lambda a, x, b, z, h: (a, x, b, z, 1 - h)
     near = jnp.stack([permute(dkvb, along_x(s)) for s in (1, 2, 3)])
+    near, f4 = lax.optimization_barrier((near, f4))
+    weights = [w, f1, f2, f3, f4, g3, g2, g1]
     alone = dkvb[None]
     parts = dx_parts(near, permute(near, swap), weights)
     got = [permute(part, along_x(-s)) for s, part in zip((1, 2, 3), parts)]
@@ -235,8 +269,9 @@
     dx = pl.pallas_call(
         gather_body,
         in_specs=[vmem] * 4,
-        out_specs=vmem,
+        out_specs=pl.BlockSpec(memory_space=pl.ANY),
         out_shape=jax.ShapeDtypeStruct((ROWS, 4096), BF16),
+        scratch_shapes=[pltpu.SemaphoreType.DMA((4,))],
         cost_estimate=SMALL,
         name="join_parts",
     )(own[0], *got)

time: 110 us -> 96.4 us (0.88)
  waiting for transfers between devices: 38.1 us -> 28.6 us
  Pallas kernels: 26.4 us -> 19 us
  starting transfers between devices: 39.8 us -> 44.6 us
  other arithmetic: 1.55 us -> 0.28 us
    ppermute x26 -> x27, waiting for transfers between devices: 38.1 us -> 28.6 us  [permute(): return lax.ppermute(value, AXES, pairs)]
    pallas_call x4, Pallas kernels: 18.5 us -> 9.3 us  [attend(): pl.pallas_call(lambda *refs: attend_body(shift, *refs), in_specs=[pl.Bloc...]
    ppermute x26 -> x27, starting transfers between devices: 39.8 us -> 44.6 us  [permute(): return lax.ppermute(value, AXES, pairs)]
    pallas_call x1 -> x2, Pallas kernels: 2.24 us -> 4.03 us  [the longest x1 2.18 us: shards(): pl.pallas_call(gather_body, in_specs=[vmem] * 4, out_specs=pl.BlockSpec(m...]
    concatenate x1, other arithmetic: 1.2 us -> 0.03 us  [shards(): jnp.concatenate([w, permute(w, lambda a, x, b, z, h: (a, x, 1 - b, z, h))...]
  transfers between devices with their start and end apart: 26 -> 27, of which waited for: 14 -> 14; matrix products, arithmetic and copies ran while one was open for 1% -> 2% of each run, Pallas kernels for 17% -> 14%
where the time goes in v3:
time: 96.4 us; the launch traced here: 96.3 us
  starting transfers between devices  44.6 us (46%)
  waiting for transfers between devices  28.6 us (30%)
  Pallas kernels  19 us (20%)
  local copies, waits for them, and re-layouts  2.72 us (3%)
  between operations  1.12 us (1%)
    ppermute x27, starting transfers between devices, permute(): return lax.ppermute(value, AXES, pairs)  44.6 us
    ppermute x27, waiting for transfers between devices, permute(): return lax.ppermute(value, AXES, pairs)  28.6 us
    pallas_call x4, Pallas kernels, attend(): pl.pallas_call(lambda *refs: attend_body(shift, *refs), in_specs=[pl.Bloc...  9.3 us
    pallas_call x1, Pallas kernels, shards(): pl.pallas_call(delta_body, in_specs=[vmem] * 3, out_specs=[vmem] * 2, out...  3.54 us
    pallas_call x1, Pallas kernels, shards(): pl.pallas_call(gather_body, in_specs=[vmem] * 4, out_specs=pl.BlockSpec(m...  2.18 us
    pallas_call x2, Pallas kernels, dx_parts(): pl.pallas_call(dx_body, in_specs=[vmem] * 10, out_specs=[vmem] * count, o...  2.11 us
  transfers between devices with their start and end apart: 27, of which 14 were waited for; matrix products, arithmetic and copies ran while one was open for 2% of the time, Pallas kernels for 14%

profile of v3, /device:TPU:1, one launch (start us, length us, event | category | flops | bytes accessed | tf_op | source)
XLA Modules:
  0.0 96.3 jit_solution(17493518869931678108)
XLA Ops:
  0.6 3.8 %collective-permute-start = (bf16[128,2,256]{2,1,0:T(2,128)(2,1)}, bf16[128,2,256]{2,1,0:T(2,128)(2,1)S(1)}, u32[]{:S(2)}, u32[]{:S(2)}) collective-permute-start(bf16[128,2,256]{2,1,0:T(2,128)(2,1)} %param.13), channel_id=1, source_target_pairs={{0,128},{1,129},{2,130},{3,131},{4,132},{5,133},{6,134},{7,135},{8... | collective-permute-start | bytes 393224 | tf_op jit(solution)/shard_map/ppermute | solution.py:32
  5.5 3.5 %row_sums.1 = (f32[16,128]{1,0:T(8,128)}, f32[16,128]{1,0:T(8,128)}) custom-call(bf16[128,2048]{1,0:T(8,128)(2,1)} %refs_2_.7, bf16[128,2048]{1,0:T(8,128)(2,1)} %o_ref.1, f32[16,128]{1,0:T(8,128)} %lse_ref.1), custom_call_target="tpu_custom_call" | custom-call | flops 1000 | bytes 1000 | tf_op jit(solution)/shard_map/row_sums/pallas_call | solution.py:207
  19.8 4.0 %collective-permute-start.8 = (bf16[4,64,512]{2,1,0:T(8,128)(2,1)S(1)}, bf16[4,64,512]{2,1,0:T(8,128)(2,1)S(1)}, u32[]{:S(2)}, u32[]{:S(2)}) collective-permute-start(bf16[4,64,512]{2,1,0:T(8,128)(2,1)S(1)} %pad_maximum_fusion.1.refs_0_), channel_id=1, source_target_pairs={{0,14},{1,15},{2,0},{3,1},{4,2},{5,3},{6,4},{7,5},{8,6},{9,7},{10,... | collective-permute-start | bytes 786440 | tf_op jit(solution)/shard_map/ppermute | solution.py:32
  23.8 4.9 %collective-permute-done.3.refs_5_.refs_3_ = bf16[2,128,512]{2,1,0:T(8,128)(2,1)S(1)} collective-permute-done((bf16[2,128,512]{2,1,0:T(8,128)(2,1)S(1)}, bf16[2,128,512]{2,1,0:T(8,128)(2,1)S(1)}, u32[]{:S(2)}, u32[]{:S(2)}) %collective-permute-start.3) | collective-permute-done | bytes 262176 | tf_op jit(solution)/shard_map/ppermute | solution.py:32
  28.8 2.3 %attend.4 = (bf16[2,128,512]{2,1,0:T(8,128)(2,1)S(1)}, bf16[256,2048]{1,0:T(8,128)(2,1)S(1)}) custom-call(s32[256]{0:T(256)S(1)} %copy-done.6, bf16[128,2048]{1,0:T(8,128)(2,1)S(1)} %copy-done.1, bf16[128,2048]{1,0:T(8,128)(2,1)S(1)} %copy-done, f32[16,128]{1,0:T(8,128)S(1)} %copy-done.5, f32[16,128]{1,0:T(8,128)S(1)} %copy-done.4, ...), custom_call_target="tpu_custom_call" | custom-call | flops 1000 | bytes 1000 | tf_op jit(solution)/shard_map/attend/pallas_call | solution.py:115
  31.1 2.3 %attend.5 = (bf16[2,128,512]{2,1,0:T(8,128)(2,1)S(1)}, bf16[256,2048]{1,0:T(8,128)(2,1)S(1)}) custom-call(s32[256]{0:T(256)S(1)} %copy-done.6, bf16[128,2048]{1,0:T(8,128)(2,1)S(1)} %copy-done.1, bf16[128,2048]{1,0:T(8,128)(2,1)S(1)} %copy-done, f32[16,128]{1,0:T(8,128)S(1)} %copy-done.5, f32[16,128]{1,0:T(8,128)S(1)} %copy-done.4, ...), custom_call_target="tpu_custom_call" | custom-call | flops 1000 | bytes 1000 | tf_op jit(solution)/shard_map/attend/pallas_call | solution.py:115
  33.4 2.3 %attend.6 = (bf16[2,128,512]{2,1,0:T(8,128)(2,1)S(1)}, bf16[256,2048]{1,0:T(8,128)(2,1)S(1)}) custom-call(s32[256]{0:T(256)S(1)} %copy-done.6, bf16[128,2048]{1,0:T(8,128)(2,1)S(1)} %copy-done.1, bf16[128,2048]{1,0:T(8,128)(2,1)S(1)} %copy-done, f32[16,128]{1,0:T(8,128)S(1)} %copy-done.5, f32[16,128]{1,0:T(8,128)S(1)} %copy-done.4, ...), custom_call_target="tpu_custom_call" | custom-call | flops 1000 | bytes 1000 | tf_op jit(solution)/shard_map/attend/pallas_call | solution.py:115
  36.6 1.6 %collective-permute-start.12 = (bf16[4,64,512]{2,1,0:T(8,128)(2,1)S(1)}, bf16[4,64,512]{2,1,0:T(8,128)(2,1)S(1)}, u32[]{:S(2)}, u32[]{:S(2)}) collective-permute-start(bf16[4,64,512]{2,1,0:T(8,128)(2,1)S(1)} %collective-permute-done.7.refs_1_), channel_id=1, source_target_pairs={{0,2},{1,3},{2,4},{3,5},{4,6},{5,7},{6,8},{7,9},{8,10},{9,11},{10,... | collective-permute-start | bytes 786440 | tf_op jit(solution)/shard_map/ppermute | solution.py:32
  38.2 3.9 %collective-permute-start.13 = (bf16[4,64,512]{2,1,0:T(8,128)(2,1)S(1)}, bf16[4,64,512]{2,1,0:T(8,128)(2,1)S(1)}, u32[]{:S(2)}, u32[]{:S(2)}) collective-permute-start(bf16[4,64,512]{2,1,0:T(8,128)(2,1)S(1)} %collective-permute-done.8.refs_7_), channel_id=1, source_target_pairs={{0,14},{1,15},{2,0},{3,1},{4,2},{5,3},{6,4},{7,5},{8,6},{9,7},{10,... | collective-permute-start | bytes 786440 | tf_op jit(solution)/shard_map/ppermute | solution.py:32
  44.8 2.3 %attend.7 = (bf16[2,128,512]{2,1,0:T(8,128)(2,1)S(1)}, bf16[256,2048]{1,0:T(8,128)(2,1)S(1)}) custom-call(s32[256]{0:T(256)S(1)} %copy-done.6, bf16[128,2048]{1,0:T(8,128)(2,1)S(1)} %copy-done.1, bf16[128,2048]{1,0:T(8,128)(2,1)S(1)} %copy-done, f32[16,128]{1,0:T(8,128)S(1)} %copy-done.5, f32[16,128]{1,0:T(8,128)S(1)} %copy-done.4, ...), custom_call_target="tpu_custom_call" | custom-call | flops 1000 | bytes 1000 | tf_op jit(solution)/shard_map/attend/pallas_call | solution.py:115
  47.3 2.7 %collective-permute-start.16 = (bf16[4,64,512]{2,1,0:T(8,128)(2,1)S(1)}, bf16[4,64,512]{2,1,0:T(8,128)(2,1)S(1)}, u32[]{:S(2)}, u32[]{:S(2)}) collective-permute-start(bf16[4,64,512]{2,1,0:T(8,128)(2,1)S(1)} %collective-permute-done.13.refs_6_), channel_id=1, source_target_pairs={{0,14},{1,15},{2,0},{3,1},{4,2},{5,3},{6,4},{7,5},{8,6},{9,7},{10,... | collective-permute-start | bytes 786440 | tf_op jit(solution)/shard_map/ppermute | solution.py:32
  50.1 2.7 %collective-permute-start.14 = (bf16[128,512]{1,0:T(8,128)(2,1)S(1)}, bf16[128,512]{1,0:T(8,128)(2,1)S(1)}, u32[]{:S(2)}, u32[]{:S(2)}) collective-permute-start(bf16[128,512]{1,0:T(8,128)(2,1)S(1)} %get-tuple-element.82), channel_id=1, source_target_pairs={{0,2},{1,3},{2,4},{3,5},{4,6},{5,7},{6,8},{7,9},{8,10},{9,11},{10,... | collective-permute-start | bytes 393224 | tf_op jit(solution)/shard_map/ppermute | solution.py:32
  52.8 3.3 %collective-permute-start.17 = (bf16[128,512]{1,0:T(8,128)(2,1)S(1)}, bf16[128,512]{1,0:T(8,128)(2,1)S(1)}, u32[]{:S(2)}, u32[]{:S(2)}) collective-permute-start(bf16[128,512]{1,0:T(8,128)(2,1)S(1)} %get-tuple-element.81), channel_id=1, source_target_pairs={{0,130},{1,131},{2,132},{3,133},{4,134},{5,135},{6,136},{7,137},{8... | collective-permute-start | bytes 393224 | tf_op jit(solution)/shard_map/ppermute | solution.py:32
  56.2 1.8 %query_grad.1 = f32[128,2048]{1,0:T(8,128)} custom-call(bf16[2,128,512]{2,1,0:T(8,128)(2,1)S(1)} %constant_dynamic-update-slice_fusion.refs_5_.refs_0_, bf16[2,128,512]{2,1,0:T(8,128)(2,1)S(1)} %collective-permute-done.1.refs_5_.refs_1_, bf16[2,128,512]{2,1,0:T(8,128)(2,1)S(1)} %collective-permute-done.2.refs_5_.refs_2_, ...), custom_call_target="tpu_custom_call" | custom-call | flops 1000 | bytes 12000000 | tf_op jit(solution)/shard_map/query_grad/pallas_call | solution.py:243
  58.0 2.7 %collective-permute-done.14 = bf16[128,512]{1,0:T(8,128)(2,1)S(1)} collective-permute-done((bf16[128,512]{1,0:T(8,128)(2,1)S(1)}, bf16[128,512]{1,0:T(8,128)(2,1)S(1)}, u32[]{:S(2)}, u32[]{:S(2)}) %collective-permute-start.14) | collective-permute-done | bytes 131104 | tf_op jit(solution)/shard_map/ppermute | solution.py:32
  60.7 2.1 %collective-permute-done.17 = bf16[128,512]{1,0:T(8,128)(2,1)S(1)} collective-permute-done((bf16[128,512]{1,0:T(8,128)(2,1)S(1)}, bf16[128,512]{1,0:T(8,128)(2,1)S(1)}, u32[]{:S(2)}, u32[]{:S(2)}) %collective-permute-start.17) | collective-permute-done | bytes 131104 | tf_op jit(solution)/shard_map/ppermute | solution.py:32
  63.8 2.0 %collective-permute-start.20 = (bf16[128,512]{1,0:T(8,128)(2,1)S(1)}, bf16[128,512]{1,0:T(8,128)(2,1)S(1)}, u32[]{:S(2)}, u32[]{:S(2)}) collective-permute-start(bf16[128,512]{1,0:T(8,128)(2,1)S(1)} %get-tuple-element.79), channel_id=1, source_target_pairs={{0,64},{1,65},{2,66},{3,67},{4,68},{5,69},{6,70},{7,71},{8,72},{9,... | collective-permute-start | bytes 393224 | tf_op jit(solution)/shard_map/ppermute | solution.py:32
  66.3 2.0 %collective-permute-done.19 = bf16[128,512]{1,0:T(8,128)(2,1)S(1)} collective-permute-done((bf16[128,512]{1,0:T(8,128)(2,1)S(1)}, bf16[128,512]{1,0:T(8,128)(2,1)S(1)}, u32[]{:S(2)}, u32[]{:S(2)}) %collective-permute-start.19) | collective-permute-done | bytes 131104 | tf_op jit(solution)/shard_map/ppermute | solution.py:32
  70.3 3.7 %collective-permute-start.23 = (bf16[3,128,512]{2,1,0:T(8,128)(2,1)S(1)}, bf16[3,128,512]{2,1,0:T(8,128)(2,1)S(1)}, u32[]{:S(2)}, u32[]{:S(2)}) collective-permute-start(bf16[3,128,512]{2,1,0:T(8,128)(2,1)S(1)} %pad_maximum_fusion.own_ref), channel_id=1, source_target_pairs={{0,1},{1,0},{2,3},{3,2},{4,5},{5,4},{6,7},{7,6},{8,9},{9,8},{10,11... | collective-permute-start | bytes 1179656 | tf_op jit(solution)/shard_map/ppermute | solution.py:32
  76.6 2.5 %collective-permute-start.24 = (bf16[128,1024]{1,0:T(8,128)(2,1)S(1)}, bf16[128,1024]{1,0:T(8,128)(2,1)}, u32[]{:S(2)}, u32[]{:S(2)}) collective-permute-start(bf16[128,1024]{1,0:T(8,128)(2,1)S(1)} %get-tuple-element.76), channel_id=1, source_target_pairs={{0,96},{1,97},{2,98},{3,99},{4,100},{5,101},{6,102},{7,103},{8,104... | collective-permute-start | bytes 786440 | tf_op jit(solution)/shard_map/ppermute | solution.py:32
  83.3 1.7 %collective-permute-done.24.p1 = bf16[128,1024]{1,0:T(8,128)(2,1)} collective-permute-done((bf16[128,1024]{1,0:T(8,128)(2,1)S(1)}, bf16[128,1024]{1,0:T(8,128)(2,1)}, u32[]{:S(2)}, u32[]{:S(2)}) %collective-permute-start.24) | collective-permute-done | bytes 262176 | tf_op jit(solution)/shard_map/ppermute | solution.py:32
  85.0 2.9 %collective-permute-done.25.p2 = bf16[128,1024]{1,0:T(8,128)(2,1)} collective-permute-done((bf16[128,1024]{1,0:T(8,128)(2,1)S(1)}, bf16[128,1024]{1,0:T(8,128)(2,1)}, u32[]{:S(2)}, u32[]{:S(2)}) %collective-permute-start.25) | collective-permute-done | bytes 262176 | tf_op jit(solution)/shard_map/ppermute | solution.py:32
  87.9 5.9 %collective-permute-done.26.p3 = bf16[128,1024]{1,0:T(8,128)(2,1)} collective-permute-done((bf16[128,1024]{1,0:T(8,128)(2,1)S(1)}, bf16[128,1024]{1,0:T(8,128)(2,1)}, u32[]{:S(2)}, u32[]{:S(2)}) %collective-permute-start.26) | collective-permute-done | bytes 262176 | tf_op jit(solution)/shard_map/ppermute | solution.py:32
  93.9 2.2 %join_parts.1 = bf16[128,4096]{1,0:T(8,128)(2,1)} custom-call(bf16[128,1024]{1,0:T(8,128)(2,1)} %copy-done.3, bf16[128,1024]{1,0:T(8,128)(2,1)} %collective-permute-done.24.p1, bf16[128,1024]{1,0:T(8,128)(2,1)} %collective-permute-done.25.p2, bf16[128,1024]{1,0:T(8,128)(2,1)} %collective-permute-done.26.p3), custom_call_target="tpu_custom_call" | custom-call | flops 1000 | bytes 1000 | tf_op jit(solution)/shard_map/join_parts/pallas_call | solution.py:269
  (71 shorter events, 25.6 us)
Async XLA Ops:
  0.6 8.5 %collective-permute-start = (bf16[128,2,256]{2,1,0:T(2,128)(2,1)}, bf16[128,2,256]{2,1,0:T(2,128)(2,1)S(1)}, u32[]{:S(2)}, u32[]{:S(2)}) collective-permute-start(bf16[128,2,256]{2,1,0:T(2,128)(2,1)} %param.13), channel_id=1, source_target_pairs={{0,128},{1,129},{2,130},{3,131},{4,132},{5,133},{6,134},{7,135},{8... | collective-permute-start | bytes 393224 | tf_op jit(solution)/shard_map/ppermute | solution.py:32
  5.4 5.5 %collective-permute-start.4 = (bf16[1,64,512]{2,1,0:T(8,128)(2,1)S(1)}, bf16[1,64,512]{2,1,0:T(8,128)(2,1)S(1)}, u32[]{:S(2)}, u32[]{:S(2)}) collective-permute-start(bf16[1,64,512]{2,1,0:T(8,128)(2,1)S(1)} %reshape.20), channel_id=1, source_target_pairs={{0,128},{1,129},{2,130},{3,131},{4,132},{5,133},{6,134},{7,135},{8... | collective-permute-start | bytes 196616 | tf_op jit(solution)/shard_map/ppermute | solution.py:32
  13.4 4.8 %collective-permute-start.6 = (bf16[2,64,512]{2,1,0:T(8,128)(2,1)S(1)}, bf16[2,64,512]{2,1,0:T(8,128)(2,1)S(1)}, u32[]{:S(2)}, u32[]{:S(2)}) collective-permute-start(bf16[2,64,512]{2,1,0:T(8,128)(2,1)S(1)} %pad_maximum_fusion.2), channel_id=1, source_target_pairs={{0,16},{1,17},{2,18},{3,19},{4,20},{5,21},{6,22},{7,23},{8,24},{9,... | collective-permute-start | bytes 393224 | tf_op jit(solution)/shard_map/ppermute | solution.py:32
  13.7 10.1 %collective-permute-start.1 = (bf16[2,128,512]{2,1,0:T(8,128)(2,1)S(1)}, bf16[2,128,512]{2,1,0:T(8,128)(2,1)S(1)}, u32[]{:S(2)}, u32[]{:S(2)}) collective-permute-start(bf16[2,128,512]{2,1,0:T(8,128)(2,1)S(1)} %constant_dynamic-update-slice_fusion.refs_5_.refs_0_), channel_id=1, source_target_pairs={{0,32},{1,33},{2,34},{3,35},{4,36},{5,37},{6,38},{7,39},{8,40},{9,... | collective-permute-start | bytes 786440 | tf_op jit(solution)/shard_map/ppermute | solution.py:32
  14.9 8.9 %collective-permute-start.2 = (bf16[2,128,512]{2,1,0:T(8,128)(2,1)S(1)}, bf16[2,128,512]{2,1,0:T(8,128)(2,1)S(1)}, u32[]{:S(2)}, u32[]{:S(2)}) collective-permute-start(bf16[2,128,512]{2,1,0:T(8,128)(2,1)S(1)} %constant_dynamic-update-slice_fusion.refs_5_.refs_0_), channel_id=1, source_target_pairs={{0,96},{1,97},{2,98},{3,99},{4,100},{5,101},{6,102},{7,103},{8,104... | collective-permute-start | bytes 786440 | tf_op jit(solution)/shard_map/ppermute | solution.py:32
  16.4 12.4 %collective-permute-start.3 = (bf16[2,128,512]{2,1,0:T(8,128)(2,1)S(1)}, bf16[2,128,512]{2,1,0:T(8,128)(2,1)S(1)}, u32[]{:S(2)}, u32[]{:S(2)}) collective-permute-start(bf16[2,128,512]{2,1,0:T(8,128)(2,1)S(1)} %constant_dynamic-update-slice_fusion.refs_5_.refs_0_), channel_id=1, source_target_pairs={{0,64},{1,65},{2,66},{3,67},{4,68},{5,69},{6,70},{7,71},{8,72},{9,... | collective-permute-start | bytes 786440 | tf_op jit(solution)/shard_map/ppermute | solution.py:32
  18.2 15.2 %collective-permute-start.7 = (bf16[4,64,512]{2,1,0:T(8,128)(2,1)S(1)}, bf16[4,64,512]{2,1,0:T(8,128)(2,1)S(1)}, u32[]{:S(2)}, u32[]{:S(2)}) collective-permute-start(bf16[4,64,512]{2,1,0:T(8,128)(2,1)S(1)} %pad_maximum_fusion.1.refs_0_), channel_id=1, source_target_pairs={{0,2},{1,3},{2,4},{3,5},{4,6},{5,7},{6,8},{7,9},{8,10},{9,11},{10,... | collective-permute-start | bytes 786440 | tf_op jit(solution)/shard_map/ppermute | solution.py:32
  19.8 13.7 %collective-permute-start.8 = (bf16[4,64,512]{2,1,0:T(8,128)(2,1)S(1)}, bf16[4,64,512]{2,1,0:T(8,128)(2,1)S(1)}, u32[]{:S(2)}, u32[]{:S(2)}) collective-permute-start(bf16[4,64,512]{2,1,0:T(8,128)(2,1)S(1)} %pad_maximum_fusion.1.refs_0_), channel_id=1, source_target_pairs={{0,14},{1,15},{2,0},{3,1},{4,2},{5,3},{6,4},{7,5},{8,6},{9,7},{10,... | collective-permute-start | bytes 786440 | tf_op jit(solution)/shard_map/ppermute | solution.py:32
  35.8 11.4 %collective-permute-start.11 = (bf16[2,128,512]{2,1,0:T(8,128)(2,1)S(1)}, bf16[2,128,512]{2,1,0:T(8,128)(2,1)S(1)}, u32[]{:S(2)}, u32[]{:S(2)}) collective-permute-start(bf16[2,128,512]{2,1,0:T(8,128)(2,1)S(1)} %get-tuple-element.60), channel_id=1, source_target_pairs={{0,64},{1,65},{2,66},{3,67},{4,68},{5,69},{6,70},{7,71},{8,72},{9,... | collective-permute-start | bytes 786440 | tf_op jit(solution)/shard_map/ppermute | solution.py:32
  36.6 10.6 %collective-permute-start.12 = (bf16[4,64,512]{2,1,0:T(8,128)(2,1)S(1)}, bf16[4,64,512]{2,1,0:T(8,128)(2,1)S(1)}, u32[]{:S(2)}, u32[]{:S(2)}) collective-permute-start(bf16[4,64,512]{2,1,0:T(8,128)(2,1)S(1)} %collective-permute-done.7.refs_1_), channel_id=1, source_target_pairs={{0,2},{1,3},{2,4},{3,5},{4,6},{5,7},{6,8},{7,9},{8,10},{9,11},{10,... | collective-permute-start | bytes 786440 | tf_op jit(solution)/shard_map/ppermute | solution.py:32
  38.2 9.0 %collective-permute-start.13 = (bf16[4,64,512]{2,1,0:T(8,128)(2,1)S(1)}, bf16[4,64,512]{2,1,0:T(8,128)(2,1)S(1)}, u32[]{:S(2)}, u32[]{:S(2)}) collective-permute-start(bf16[4,64,512]{2,1,0:T(8,128)(2,1)S(1)} %collective-permute-done.8.refs_7_), channel_id=1, source_target_pairs={{0,14},{1,15},{2,0},{3,1},{4,2},{5,3},{6,4},{7,5},{8,6},{9,7},{10,... | collective-permute-start | bytes 786440 | tf_op jit(solution)/shard_map/ppermute | solution.py:32
  42.1 7.8 %collective-permute-start.10 = (bf16[2,128,512]{2,1,0:T(8,128)(2,1)S(1)}, bf16[2,128,512]{2,1,0:T(8,128)(2,1)S(1)}, u32[]{:S(2)}, u32[]{:S(2)}) collective-permute-start(bf16[2,128,512]{2,1,0:T(8,128)(2,1)S(1)} %get-tuple-element.59), channel_id=1, source_target_pairs={{0,32},{1,33},{2,34},{3,35},{4,36},{5,37},{6,38},{7,39},{8,40},{9,... | collective-permute-start | bytes 786440 | tf_op jit(solution)/shard_map/ppermute | solution.py:32
  43.3 6.6 %collective-permute-start.9 = (bf16[2,128,512]{2,1,0:T(8,128)(2,1)S(1)}, bf16[2,128,512]{2,1,0:T(8,128)(2,1)S(1)}, u32[]{:S(2)}, u32[]{:S(2)}) collective-permute-start(bf16[2,128,512]{2,1,0:T(8,128)(2,1)S(1)} %get-tuple-element.58), channel_id=1, source_target_pairs={{0,96},{1,97},{2,98},{3,99},{4,100},{5,101},{6,102},{7,103},{8,104... | collective-permute-start | bytes 786440 | tf_op jit(solution)/shard_map/ppermute | solution.py:32
  47.2 13.5 %collective-permute-start.15 = (bf16[4,64,512]{2,1,0:T(8,128)(2,1)S(1)}, bf16[4,64,512]{2,1,0:T(8,128)(2,1)S(1)}, u32[]{:S(2)}, u32[]{:S(2)}) collective-permute-start(bf16[4,64,512]{2,1,0:T(8,128)(2,1)S(1)} %collective-permute-done.12.refs_2_), channel_id=1, source_target_pairs={{0,2},{1,3},{2,4},{3,5},{4,6},{5,7},{6,8},{7,9},{8,10},{9,11},{10,... | collective-permute-start | bytes 786440 | tf_op jit(solution)/shard_map/ppermute | solution.py:32
  47.3 13.4 %collective-permute-start.16 = (bf16[4,64,512]{2,1,0:T(8,128)(2,1)S(1)}, bf16[4,64,512]{2,1,0:T(8,128)(2,1)S(1)}, u32[]{:S(2)}, u32[]{:S(2)}) collective-permute-start(bf16[4,64,512]{2,1,0:T(8,128)(2,1)S(1)} %collective-permute-done.13.refs_6_), channel_id=1, source_target_pairs={{0,14},{1,15},{2,0},{3,1},{4,2},{5,3},{6,4},{7,5},{8,6},{9,7},{10,... | collective-permute-start | bytes 786440 | tf_op jit(solution)/shard_map/ppermute | solution.py:32
  50.1 10.6 %collective-permute-start.14 = (bf16[128,512]{1,0:T(8,128)(2,1)S(1)}, bf16[128,512]{1,0:T(8,128)(2,1)S(1)}, u32[]{:S(2)}, u32[]{:S(2)}) collective-permute-start(bf16[128,512]{1,0:T(8,128)(2,1)S(1)} %get-tuple-element.82), channel_id=1, source_target_pairs={{0,2},{1,3},{2,4},{3,5},{4,6},{5,7},{6,8},{7,9},{8,10},{9,11},{10,... | collective-permute-start | bytes 393224 | tf_op jit(solution)/shard_map/ppermute | solution.py:32
  52.8 10.0 %collective-permute-start.17 = (bf16[128,512]{1,0:T(8,128)(2,1)S(1)}, bf16[128,512]{1,0:T(8,128)(2,1)S(1)}, u32[]{:S(2)}, u32[]{:S(2)}) collective-permute-start(bf16[128,512]{1,0:T(8,128)(2,1)S(1)} %get-tuple-element.81), channel_id=1, source_target_pairs={{0,130},{1,131},{2,132},{3,133},{4,134},{5,135},{6,136},{7,137},{8... | collective-permute-start | bytes 393224 | tf_op jit(solution)/shard_map/ppermute | solution.py:32
  60.7 9.6 %collective-permute-start.22 = (bf16[4,64,512]{2,1,0:T(8,128)(2,1)S(1)}, bf16[4,64,512]{2,1,0:T(8,128)(2,1)S(1)}, u32[]{:S(2)}, u32[]{:S(2)}) collective-permute-start(bf16[4,64,512]{2,1,0:T(8,128)(2,1)S(1)} %collective-permute-done.15.refs_3_), channel_id=1, source_target_pairs={{0,2},{1,3},{2,4},{3,5},{4,6},{5,7},{6,8},{7,9},{8,10},{9,11},{10,... | collective-permute-start | bytes 786440 | tf_op jit(solution)/shard_map/ppermute | solution.py:32
  62.9 5.4 %collective-permute-start.19 = (bf16[128,512]{1,0:T(8,128)(2,1)S(1)}, bf16[128,512]{1,0:T(8,128)(2,1)S(1)}, u32[]{:S(2)}, u32[]{:S(2)}) collective-permute-start(bf16[128,512]{1,0:T(8,128)(2,1)S(1)} %get-tuple-element.79), channel_id=1, source_target_pairs={{0,32},{1,33},{2,34},{3,35},{4,36},{5,37},{6,38},{7,39},{8,40},{9,... | collective-permute-start | bytes 393224 | tf_op jit(solution)/shard_map/ppermute | solution.py:32
  63.8 5.8 %collective-permute-start.20 = (bf16[128,512]{1,0:T(8,128)(2,1)S(1)}, bf16[128,512]{1,0:T(8,128)(2,1)S(1)}, u32[]{:S(2)}, u32[]{:S(2)}) collective-permute-start(bf16[128,512]{1,0:T(8,128)(2,1)S(1)} %get-tuple-element.79), channel_id=1, source_target_pairs={{0,64},{1,65},{2,66},{3,67},{4,68},{5,69},{6,70},{7,71},{8,72},{9,... | collective-permute-start | bytes 393224 | tf_op jit(solution)/shard_map/ppermute | solution.py:32
  70.3 5.1 %collective-permute-start.23 = (bf16[3,128,512]{2,1,0:T(8,128)(2,1)S(1)}, bf16[3,128,512]{2,1,0:T(8,128)(2,1)S(1)}, u32[]{:S(2)}, u32[]{:S(2)}) collective-permute-start(bf16[3,128,512]{2,1,0:T(8,128)(2,1)S(1)} %pad_maximum_fusion.own_ref), channel_id=1, source_target_pairs={{0,1},{1,0},{2,3},{3,2},{4,5},{5,4},{6,7},{7,6},{8,9},{9,8},{10,11... | collective-permute-start | bytes 1179656 | tf_op jit(solution)/shard_map/ppermute | solution.py:32
  76.6 8.5 %collective-permute-start.24 = (bf16[128,1024]{1,0:T(8,128)(2,1)S(1)}, bf16[128,1024]{1,0:T(8,128)(2,1)}, u32[]{:S(2)}, u32[]{:S(2)}) collective-permute-start(bf16[128,1024]{1,0:T(8,128)(2,1)S(1)} %get-tuple-element.76), channel_id=1, source_target_pairs={{0,96},{1,97},{2,98},{3,99},{4,100},{5,101},{6,102},{7,103},{8,104... | collective-permute-start | bytes 786440 | tf_op jit(solution)/shard_map/ppermute | solution.py:32
  79.0 8.9 %collective-permute-start.25 = (bf16[128,1024]{1,0:T(8,128)(2,1)S(1)}, bf16[128,1024]{1,0:T(8,128)(2,1)}, u32[]{:S(2)}, u32[]{:S(2)}) collective-permute-start(bf16[128,1024]{1,0:T(8,128)(2,1)S(1)} %get-tuple-element.77), channel_id=1, source_target_pairs={{0,64},{1,65},{2,66},{3,67},{4,68},{5,69},{6,70},{7,71},{8,72},{9,... | collective-permute-start | bytes 786440 | tf_op jit(solution)/shard_map/ppermute | solution.py:32
  79.0 14.8 %collective-permute-start.26 = (bf16[128,1024]{1,0:T(8,128)(2,1)S(1)}, bf16[128,1024]{1,0:T(8,128)(2,1)}, u32[]{:S(2)}, u32[]{:S(2)}) collective-permute-start(bf16[128,1024]{1,0:T(8,128)(2,1)S(1)} %get-tuple-element.78), channel_id=1, source_target_pairs={{0,32},{1,33},{2,34},{3,35},{4,36},{5,37},{6,38},{7,39},{8,40},{9,... | collective-permute-start | bytes 786440 | tf_op jit(solution)/shard_map/ppermute | solution.py:32
  (12 other events, 118.8 us)

commit v4 on v3

--- a/solution.py
+++ b/solution.py
@@ -143,13 +143,16 @@
 
 
 def dx_body(own_ref, other_ref, *refs):
-    w_refs, out_refs, (wz, dk) = refs[:8], refs[8:-2], refs[-2:]
+    w_refs, out_refs, (wz, dk) = refs[:9], refs[9:-2], refs[-2:]
     rows = len(out_refs) * ROWS
     yl = lax.axis_index("yl")
     z = lax.axis_index("z")
     core = lax.axis_index("core")
-    for k, ref in enumerate(w_refs):
+    for k, ref in zip((0, 1, 2, 3, 5, 6, 7), w_refs[:4] + w_refs[6:]):
         wz[lax.rem(z + 8 - k, 8)] = ref[...]
+    far = lax.rem(z + 4, 8)
+    wz[far, 0:2] = w_refs[4][...]
+    wz[far, 2:4] = w_refs[5][...]
     dk[core] = own_ref[...].reshape(rows, 512)
     dk[1 - core] = other_ref[...].reshape(rows, 512)
     nt = (((1,), (1,)), ((), ()))
@@ -171,7 +174,7 @@
     vmem = pl.BlockSpec(memory_space=pltpu.VMEM)
     return pl.pallas_call(
         dx_body,
-        in_specs=[vmem] * 10,
+        in_specs=[vmem] * 11,
         out_specs=[vmem] * count,
         out_shape=[jax.ShapeDtypeStruct((ROWS, 1024), BF16)] * count,
         scratch_shapes=[pltpu.VMEM((8, 4, 64, 512), BF16), pltpu.VMEM((2, count * ROWS, 512), BF16)],
@@ -225,19 +228,19 @@
     w = jnp.concatenate([kept, permute(sent, lambda a, x, b, z, h: (a, x, b, z, 1 - h))], axis=0)
     w = jnp.concatenate([w, permute(w, lambda a, x, b, z, h: (a, x, 1 - b, z, h))], axis=0)
     f1, g1 = step(w, 1), step(w, -1)
-    pairs[1], pairs[3], pairs[2] = lax.optimization_barrier((pairs[1], pairs[3], pairs[2]))
+    pairs[1], pairs[3] = lax.optimization_barrier((pairs[1], pairs[3]))
     t1, ds1 = run(1, pairs[1])
     back1 = permute(t1, along_x(-1))
     ds1, pairs[3] = lax.optimization_barrier((ds1, pairs[3]))
     t3, ds3 = run(3, pairs[3])
     back3 = permute(t3, along_x(-3))
-    ds3, pairs[2], f1, g1 = lax.optimization_barrier((ds3, pairs[2], f1, g1))
+    ds3, pairs[2] = lax.optimization_barrier((ds3, pairs[2]))
     t2, ds2 = run(2, pairs[2])
     back2 = permute(t2, along_x(-2))
+    ds2, own_pair, f1, g1 = lax.optimization_barrier((ds2, pair, f1, g1))
     f2, g2 = step(f1, 1), step(g1, -1)
-    ds2, own_pair = lax.optimization_barrier((ds2, pair))
     t0, ds0 = run(0, own_pair)
-    back2, f2, g2 = lax.optimization_barrier((back2, f2, g2))
+    ds0, f2, g2 = lax.optimization_barrier((ds0, f2, g2))
     f3, g3 = step(f2, 1), step(g2, -1)
     back = (t0, back1, back3, back2)
     dq = pl.pallas_call(
@@ -253,15 +256,16 @@
     r0, r1 = total[0], total[1]
     r0 = permute(r0, next_outer(0))
     r1 = permute(r1, next_outer(1))
-    r0, f3, g3, dq = lax.optimization_barrier((r0, f3, g3, dq))
-    f4 = step(f3, 1)
+    r0, dq = lax.optimization_barrier((r0, dq))
     dkv = dkv_acc.reshape(ROWS, 512) + (r0.astype(F32) + r1.astype(F32))
     dkvb = dkv.astype(BF16)
 
     swap = lambda a, x, b, z, h: (a, x, b, z, 1 - h)
+    dkvb, f3, g3 = lax.optimization_barrier((dkvb, f3, g3))
+    f4, g4 = step(f3[:2], 1), step(g3[2:], -1)
     near = jnp.stack([permute(dkvb, along_x(s)) for s in (1, 2, 3)])
-    near, f4 = lax.optimization_barrier((near, f4))
-    weights = [w, f1, f2, f3, f4, g3, g2, g1]
+    near, f4, g4 = lax.optimization_barrier((near, f4, g4))
+    weights = [w, f1, f2, f3, f4, g4, g3, g2, g1]
     alone = dkvb[None]
     parts = dx_parts(near, permute(near, swap), weights)
     got = [permute(part, along_x(-s)) for s, part in zip((1, 2, 3), parts)]

time: 96.4 us -> 97.2 us (level)
  waiting for transfers between devices: 28.6 us -> 33.6 us
  starting transfers between devices: 44.6 us -> 40.3 us
    ppermute x27 -> x28, waiting for transfers between devices: 28.6 us -> 33.6 us  [permute(): return lax.ppermute(value, AXES, pairs)]
    ppermute x27 -> x28, starting transfers between devices: 44.6 us -> 40.3 us  [permute(): return lax.ppermute(value, AXES, pairs)]
  transfers between devices with their start and end apart: 27 -> 28, of which waited for: 14 -> 12; matrix products, arithmetic and copies ran while one was open for 2% -> 2% of each run, Pallas kernels for 14% -> 16%
where the time goes in v4:
time: 97.2 us; the launch traced here: 97 us
  starting transfers between devices  40.3 us (41%)
  waiting for transfers between devices  33.6 us (35%)
  Pallas kernels  19 us (20%)
  local copies, waits for them, and re-layouts  2.75 us (3%)
  between operations  1.15 us (1%)
    ppermute x28, starting transfers between devices, permute(): return lax.ppermute(value, AXES, pairs)  40.3 us
    ppermute x28, waiting for transfers between devices, permute(): return lax.ppermute(value, AXES, pairs)  33.6 us
    pallas_call x4, Pallas kernels, attend(): pl.pallas_call(lambda *refs: attend_body(shift, *refs), in_specs=[pl.Bloc...  9.29 us
    pallas_call x1, Pallas kernels, shards(): pl.pallas_call(delta_body, in_specs=[vmem] * 3, out_specs=[vmem] * 2, out...  3.54 us
    pallas_call x1, Pallas kernels, shards(): pl.pallas_call(gather_body, in_specs=[vmem] * 4, out_specs=pl.BlockSpec(m...  2.18 us
    pallas_call x2, Pallas kernels, dx_parts(): pl.pallas_call(dx_body, in_specs=[vmem] * 11, out_specs=[vmem] * count, o...  2.12 us
  transfers between devices with their start and end apart: 28, of which 12 were waited for; matrix products, arithmetic and copies ran while one was open for 2% of the time, Pallas kernels for 16%

profile of v4, /device:TPU:1, one launch (start us, length us, event | category | flops | bytes accessed | tf_op | source)
XLA Modules:
  0.0 97.0 jit_solution(2567364628358191123)
XLA Ops:
  0.6 3.8 %collective-permute-start = (bf16[128,2,256]{2,1,0:T(2,128)(2,1)}, bf16[128,2,256]{2,1,0:T(2,128)(2,1)S(1)}, u32[]{:S(2)}, u32[]{:S(2)}) collective-permute-start(bf16[128,2,256]{2,1,0:T(2,128)(2,1)} %param.13), channel_id=1, source_target_pairs={{0,128},{1,129},{2,130},{3,131},{4,132},{5,133},{6,134},{7,135},{8... | collective-permute-start | bytes 393224 | tf_op jit(solution)/shard_map/ppermute | solution.py:32
  5.5 3.5 %row_sums.1 = (f32[16,128]{1,0:T(8,128)}, f32[16,128]{1,0:T(8,128)}) custom-call(bf16[128,2048]{1,0:T(8,128)(2,1)} %refs_2_.7, bf16[128,2048]{1,0:T(8,128)(2,1)} %o_ref.1, f32[16,128]{1,0:T(8,128)} %lse_ref.1), custom_call_target="tpu_custom_call" | custom-call | flops 1000 | bytes 1000 | tf_op jit(solution)/shard_map/row_sums/pallas_call | solution.py:210
  17.0 3.7 %collective-permute-done.6 = bf16[2,64,512]{2,1,0:T(8,128)(2,1)S(1)} collective-permute-done((bf16[2,64,512]{2,1,0:T(8,128)(2,1)S(1)}, bf16[2,64,512]{2,1,0:T(8,128)(2,1)S(1)}, u32[]{:S(2)}, u32[]{:S(2)}) %collective-permute-start.6) | collective-permute-done | bytes 131104 | tf_op jit(solution)/shard_map/ppermute | solution.py:32
  20.8 1.7 %collective-permute-start.7 = (bf16[4,64,512]{2,1,0:T(8,128)(2,1)S(1)}, bf16[4,64,512]{2,1,0:T(8,128)(2,1)S(1)}, u32[]{:S(2)}, u32[]{:S(2)}) collective-permute-start(bf16[4,64,512]{2,1,0:T(8,128)(2,1)S(1)} %pad_maximum_fusion.1.refs_0_), channel_id=1, source_target_pairs={{0,2},{1,3},{2,4},{3,5},{4,6},{5,7},{6,8},{7,9},{8,10},{9,11},{10,... | collective-permute-start | bytes 786440 | tf_op jit(solution)/shard_map/ppermute | solution.py:32
  22.5 4.0 %collective-permute-start.8 = (bf16[4,64,512]{2,1,0:T(8,128)(2,1)S(1)}, bf16[4,64,512]{2,1,0:T(8,128)(2,1)S(1)}, u32[]{:S(2)}, u32[]{:S(2)}) collective-permute-start(bf16[4,64,512]{2,1,0:T(8,128)(2,1)S(1)} %pad_maximum_fusion.1.refs_0_), channel_id=1, source_target_pairs={{0,14},{1,15},{2,0},{3,1},{4,2},{5,3},{6,4},{7,5},{8,6},{9,7},{10,... | collective-permute-start | bytes 786440 | tf_op jit(solution)/shard_map/ppermute | solution.py:32
  26.6 2.3 %attend.4 = (bf16[2,128,512]{2,1,0:T(8,128)(2,1)S(1)}, bf16[256,2048]{1,0:T(8,128)(2,1)S(1)}) custom-call(s32[256]{0:T(256)S(1)} %copy-done.6, bf16[128,2048]{1,0:T(8,128)(2,1)S(1)} %copy-done.1, bf16[128,2048]{1,0:T(8,128)(2,1)S(1)} %copy-done, f32[16,128]{1,0:T(8,128)S(1)} %copy-done.5, f32[16,128]{1,0:T(8,128)S(1)} %copy-done.4, ...), custom_call_target="tpu_custom_call" | custom-call | flops 1000 | bytes 1000 | tf_op jit(solution)/shard_map/attend/pallas_call | solution.py:115
  28.9 2.3 %attend.5 = (bf16[2,128,512]{2,1,0:T(8,128)(2,1)S(1)}, bf16[256,2048]{1,0:T(8,128)(2,1)S(1)}) custom-call(s32[256]{0:T(256)S(1)} %copy-done.6, bf16[128,2048]{1,0:T(8,128)(2,1)S(1)} %copy-done.1, bf16[128,2048]{1,0:T(8,128)(2,1)S(1)} %copy-done, f32[16,128]{1,0:T(8,128)S(1)} %copy-done.5, f32[16,128]{1,0:T(8,128)S(1)} %copy-done.4, ...), custom_call_target="tpu_custom_call" | custom-call | flops 1000 | bytes 1000 | tf_op jit(solution)/shard_map/attend/pallas_call | solution.py:115
  31.2 2.3 %attend.6 = (bf16[2,128,512]{2,1,0:T(8,128)(2,1)S(1)}, bf16[256,2048]{1,0:T(8,128)(2,1)S(1)}) custom-call(s32[256]{0:T(256)S(1)} %copy-done.6, bf16[128,2048]{1,0:T(8,128)(2,1)S(1)} %copy-done.1, bf16[128,2048]{1,0:T(8,128)(2,1)S(1)} %copy-done, f32[16,128]{1,0:T(8,128)S(1)} %copy-done.5, f32[16,128]{1,0:T(8,128)S(1)} %copy-done.4, ...), custom_call_target="tpu_custom_call" | custom-call | flops 1000 | bytes 1000 | tf_op jit(solution)/shard_map/attend/pallas_call | solution.py:115
  35.3 2.7 %collective-permute-start.9 = (bf16[2,128,512]{2,1,0:T(8,128)(2,1)S(1)}, bf16[2,128,512]{2,1,0:T(8,128)(2,1)S(1)}, u32[]{:S(2)}, u32[]{:S(2)}) collective-permute-start(bf16[2,128,512]{2,1,0:T(8,128)(2,1)S(1)} %get-tuple-element.58), channel_id=1, source_target_pairs={{0,96},{1,97},{2,98},{3,99},{4,100},{5,101},{6,102},{7,103},{8,104... | collective-permute-start | bytes 786440 | tf_op jit(solution)/shard_map/ppermute | solution.py:32
  38.0 2.3 %attend.7 = (bf16[2,128,512]{2,1,0:T(8,128)(2,1)S(1)}, bf16[256,2048]{1,0:T(8,128)(2,1)S(1)}) custom-call(s32[256]{0:T(256)S(1)} %copy-done.6, bf16[128,2048]{1,0:T(8,128)(2,1)S(1)} %copy-done.1, bf16[128,2048]{1,0:T(8,128)(2,1)S(1)} %copy-done, f32[16,128]{1,0:T(8,128)S(1)} %copy-done.5, f32[16,128]{1,0:T(8,128)S(1)} %copy-done.4, ...), custom_call_target="tpu_custom_call" | custom-call | flops 1000 | bytes 1000 | tf_op jit(solution)/shard_map/attend/pallas_call | solution.py:115
  40.4 2.7 %collective-permute-start.14 = (bf16[4,64,512]{2,1,0:T(8,128)(2,1)S(1)}, bf16[4,64,512]{2,1,0:T(8,128)(2,1)S(1)}, u32[]{:S(2)}, u32[]{:S(2)}) collective-permute-start(bf16[4,64,512]{2,1,0:T(8,128)(2,1)S(1)} %collective-permute-done.8.refs_8_), channel_id=1, source_target_pairs={{0,14},{1,15},{2,0},{3,1},{4,2},{5,3},{6,4},{7,5},{8,6},{9,7},{10,... | collective-permute-start | bytes 786440 | tf_op jit(solution)/shard_map/ppermute | solution.py:32
  43.0 5.7 %collective-permute-done.10 = bf16[2,128,512]{2,1,0:T(8,128)(2,1)S(1)} collective-permute-done((bf16[2,128,512]{2,1,0:T(8,128)(2,1)S(1)}, bf16[2,128,512]{2,1,0:T(8,128)(2,1)S(1)}, u32[]{:S(2)}, u32[]{:S(2)}) %collective-permute-start.10) | collective-permute-done | bytes 262176 | tf_op jit(solution)/shard_map/ppermute | solution.py:32
  49.1 2.3 %collective-permute-start.16 = (bf16[4,64,512]{2,1,0:T(8,128)(2,1)S(1)}, bf16[4,64,512]{2,1,0:T(8,128)(2,1)S(1)}, u32[]{:S(2)}, u32[]{:S(2)}) collective-permute-start(bf16[4,64,512]{2,1,0:T(8,128)(2,1)S(1)} %collective-permute-done.13.refs_2_), channel_id=1, source_target_pairs={{0,2},{1,3},{2,4},{3,5},{4,6},{5,7},{6,8},{7,9},{8,10},{9,11},{10,... | collective-permute-start | bytes 786440 | tf_op jit(solution)/shard_map/ppermute | solution.py:32
  52.8 1.9 %query_grad.1 = f32[128,2048]{1,0:T(8,128)} custom-call(bf16[2,128,512]{2,1,0:T(8,128)(2,1)S(1)} %constant_dynamic-update-slice_fusion.refs_5_.refs_0_, bf16[2,128,512]{2,1,0:T(8,128)(2,1)S(1)} %collective-permute-done.1.refs_5_.refs_1_, bf16[2,128,512]{2,1,0:T(8,128)(2,1)S(1)} %collective-permute-done.2.refs_5_.refs_2_, ...), custom_call_target="tpu_custom_call" | custom-call | flops 1000 | bytes 12000000 | tf_op jit(solution)/shard_map/query_grad/pallas_call | solution.py:246
  54.9 2.9 %collective-permute-done.15 = bf16[128,512]{1,0:T(8,128)(2,1)S(1)} collective-permute-done((bf16[128,512]{1,0:T(8,128)(2,1)S(1)}, bf16[128,512]{1,0:T(8,128)(2,1)S(1)}, u32[]{:S(2)}, u32[]{:S(2)}) %collective-permute-start.15) | collective-permute-done | bytes 131104 | tf_op jit(solution)/shard_map/ppermute | solution.py:32
  57.9 4.9 %collective-permute-done.16.refs_3_ = bf16[4,64,512]{2,1,0:T(8,128)(2,1)S(1)} collective-permute-done((bf16[4,64,512]{2,1,0:T(8,128)(2,1)S(1)}, bf16[4,64,512]{2,1,0:T(8,128)(2,1)S(1)}, u32[]{:S(2)}, u32[]{:S(2)}) %collective-permute-start.16) | collective-permute-done | bytes 262176 | tf_op jit(solution)/shard_map/ppermute | solution.py:32
  62.8 2.5 %collective-permute-start.20 = (bf16[128,512]{1,0:T(8,128)(2,1)S(1)}, bf16[128,512]{1,0:T(8,128)(2,1)S(1)}, u32[]{:S(2)}, u32[]{:S(2)}) collective-permute-start(bf16[128,512]{1,0:T(8,128)(2,1)S(1)} %get-tuple-element.72), channel_id=1, source_target_pairs={{0,64},{1,65},{2,66},{3,67},{4,68},{5,69},{6,70},{7,71},{8,72},{9,... | collective-permute-start | bytes 393224 | tf_op jit(solution)/shard_map/ppermute | solution.py:32
  66.2 3.0 %collective-permute-start.23 = (bf16[2,64,512]{2,1,0:T(8,128)(2,1)S(1)}, bf16[2,64,512]{2,1,0:T(8,128)(2,1)S(1)}, u32[]{:S(2)}, u32[]{:S(2)}) collective-permute-start(bf16[2,64,512]{2,1,0:T(8,128)(2,1)S(1)} %slice.15), channel_id=1, source_target_pairs={{0,14},{1,15},{2,0},{3,1},{4,2},{5,3},{6,4},{7,5},{8,6},{9,7},{10,... | collective-permute-start | bytes 393224 | tf_op jit(solution)/shard_map/ppermute | solution.py:32
  69.2 2.5 %collective-permute-done.19 = bf16[128,512]{1,0:T(8,128)(2,1)S(1)} collective-permute-done((bf16[128,512]{1,0:T(8,128)(2,1)S(1)}, bf16[128,512]{1,0:T(8,128)(2,1)S(1)}, u32[]{:S(2)}, u32[]{:S(2)}) %collective-permute-start.19) | collective-permute-done | bytes 131104 | tf_op jit(solution)/shard_map/ppermute | solution.py:32
  71.8 2.8 %collective-permute-start.24 = (bf16[3,128,512]{2,1,0:T(8,128)(2,1)S(1)}, bf16[3,128,512]{2,1,0:T(8,128)(2,1)S(1)}, u32[]{:S(2)}, u32[]{:S(2)}) collective-permute-start(bf16[3,128,512]{2,1,0:T(8,128)(2,1)S(1)} %pad_maximum_fusion.own_ref), channel_id=1, source_target_pairs={{0,1},{1,0},{2,3},{3,2},{4,5},{5,4},{6,7},{7,6},{8,9},{9,8},{10,11... | collective-permute-start | bytes 1179656 | tf_op jit(solution)/shard_map/ppermute | solution.py:32
  77.1 2.1 %collective-permute-start.25 = (bf16[128,1024]{1,0:T(8,128)(2,1)S(1)}, bf16[128,1024]{1,0:T(8,128)(2,1)}, u32[]{:S(2)}, u32[]{:S(2)}) collective-permute-start(bf16[128,1024]{1,0:T(8,128)(2,1)S(1)} %get-tuple-element.78), channel_id=1, source_target_pairs={{0,96},{1,97},{2,98},{3,99},{4,100},{5,101},{6,102},{7,103},{8,104... | collective-permute-start | bytes 786440 | tf_op jit(solution)/shard_map/ppermute | solution.py:32
  84.9 3.2 %collective-permute-done.26.p2 = bf16[128,1024]{1,0:T(8,128)(2,1)} collective-permute-done((bf16[128,1024]{1,0:T(8,128)(2,1)S(1)}, bf16[128,1024]{1,0:T(8,128)(2,1)}, u32[]{:S(2)}, u32[]{:S(2)}) %collective-permute-start.26) | collective-permute-done | bytes 262176 | tf_op jit(solution)/shard_map/ppermute | solution.py:32
  88.1 6.6 %collective-permute-done.27.p3 = bf16[128,1024]{1,0:T(8,128)(2,1)} collective-permute-done((bf16[128,1024]{1,0:T(8,128)(2,1)S(1)}, bf16[128,1024]{1,0:T(8,128)(2,1)}, u32[]{:S(2)}, u32[]{:S(2)}) %collective-permute-start.27) | collective-permute-done | bytes 262176 | tf_op jit(solution)/shard_map/ppermute | solution.py:32
  94.7 2.2 %join_parts.1 = bf16[128,4096]{1,0:T(8,128)(2,1)} custom-call(bf16[128,1024]{1,0:T(8,128)(2,1)} %copy-done.3, bf16[128,1024]{1,0:T(8,128)(2,1)} %collective-permute-done.25.p1, bf16[128,1024]{1,0:T(8,128)(2,1)} %collective-permute-done.26.p2, bf16[128,1024]{1,0:T(8,128)(2,1)} %collective-permute-done.27.p3), custom_call_target="tpu_custom_call" | custom-call | flops 1000 | bytes 1000 | tf_op jit(solution)/shard_map/join_parts/pallas_call | solution.py:273
  (75 shorter events, 22.0 us)
Async XLA Ops:
  0.6 8.5 %collective-permute-start = (bf16[128,2,256]{2,1,0:T(2,128)(2,1)}, bf16[128,2,256]{2,1,0:T(2,128)(2,1)S(1)}, u32[]{:S(2)}, u32[]{:S(2)}) collective-permute-start(bf16[128,2,256]{2,1,0:T(2,128)(2,1)} %param.13), channel_id=1, source_target_pairs={{0,128},{1,129},{2,130},{3,131},{4,132},{5,133},{6,134},{7,135},{8... | collective-permute-start | bytes 393224 | tf_op jit(solution)/shard_map/ppermute | solution.py:32
  10.9 5.6 %collective-permute-start.5 = (bf16[1,64,512]{2,1,0:T(8,128)(2,1)S(1)}, bf16[1,64,512]{2,1,0:T(8,128)(2,1)S(1)}, u32[]{:S(2)}, u32[]{:S(2)}) collective-permute-start(bf16[1,64,512]{2,1,0:T(8,128)(2,1)S(1)} %get-tuple-element.86), channel_id=1, source_target_pairs={{0,1},{1,0},{2,3},{3,2},{4,5},{5,4},{6,7},{7,6},{8,9},{9,8},{10,11... | collective-permute-start | bytes 196616 | tf_op jit(solution)/shard_map/ppermute | solution.py:32
  12.4 14.1 %collective-permute-start.1 = (bf16[2,128,512]{2,1,0:T(8,128)(2,1)S(1)}, bf16[2,128,512]{2,1,0:T(8,128)(2,1)S(1)}, u32[]{:S(2)}, u32[]{:S(2)}) collective-permute-start(bf16[2,128,512]{2,1,0:T(8,128)(2,1)S(1)} %constant_dynamic-update-slice_fusion.refs_5_.refs_0_), channel_id=1, source_target_pairs={{0,32},{1,33},{2,34},{3,35},{4,36},{5,37},{6,38},{7,39},{8,40},{9,... | collective-permute-start | bytes 786440 | tf_op jit(solution)/shard_map/ppermute | solution.py:32
  13.5 13.0 %collective-permute-start.2 = (bf16[2,128,512]{2,1,0:T(8,128)(2,1)S(1)}, bf16[2,128,512]{2,1,0:T(8,128)(2,1)S(1)}, u32[]{:S(2)}, u32[]{:S(2)}) collective-permute-start(bf16[2,128,512]{2,1,0:T(8,128)(2,1)S(1)} %constant_dynamic-update-slice_fusion.refs_5_.refs_0_), channel_id=1, source_target_pairs={{0,96},{1,97},{2,98},{3,99},{4,100},{5,101},{6,102},{7,103},{8,104... | collective-permute-start | bytes 786440 | tf_op jit(solution)/shard_map/ppermute | solution.py:32
  15.1 16.1 %collective-permute-start.3 = (bf16[2,128,512]{2,1,0:T(8,128)(2,1)S(1)}, bf16[2,128,512]{2,1,0:T(8,128)(2,1)S(1)}, u32[]{:S(2)}, u32[]{:S(2)}) collective-permute-start(bf16[2,128,512]{2,1,0:T(8,128)(2,1)S(1)} %constant_dynamic-update-slice_fusion.refs_5_.refs_0_), channel_id=1, source_target_pairs={{0,64},{1,65},{2,66},{3,67},{4,68},{5,69},{6,70},{7,71},{8,72},{9,... | collective-permute-start | bytes 786440 | tf_op jit(solution)/shard_map/ppermute | solution.py:32
  20.8 17.2 %collective-permute-start.7 = (bf16[4,64,512]{2,1,0:T(8,128)(2,1)S(1)}, bf16[4,64,512]{2,1,0:T(8,128)(2,1)S(1)}, u32[]{:S(2)}, u32[]{:S(2)}) collective-permute-start(bf16[4,64,512]{2,1,0:T(8,128)(2,1)S(1)} %pad_maximum_fusion.1.refs_0_), channel_id=1, source_target_pairs={{0,2},{1,3},{2,4},{3,5},{4,6},{5,7},{6,8},{7,9},{8,10},{9,11},{10,... | collective-permute-start | bytes 786440 | tf_op jit(solution)/shard_map/ppermute | solution.py:32
  22.5 15.5 %collective-permute-start.8 = (bf16[4,64,512]{2,1,0:T(8,128)(2,1)S(1)}, bf16[4,64,512]{2,1,0:T(8,128)(2,1)S(1)}, u32[]{:S(2)}, u32[]{:S(2)}) collective-permute-start(bf16[4,64,512]{2,1,0:T(8,128)(2,1)S(1)} %pad_maximum_fusion.1.refs_0_), channel_id=1, source_target_pairs={{0,14},{1,15},{2,0},{3,1},{4,2},{5,3},{6,4},{7,5},{8,6},{9,7},{10,... | collective-permute-start | bytes 786440 | tf_op jit(solution)/shard_map/ppermute | solution.py:32
  33.6 9.5 %collective-permute-start.11 = (bf16[2,128,512]{2,1,0:T(8,128)(2,1)S(1)}, bf16[2,128,512]{2,1,0:T(8,128)(2,1)S(1)}, u32[]{:S(2)}, u32[]{:S(2)}) collective-permute-start(bf16[2,128,512]{2,1,0:T(8,128)(2,1)S(1)} %get-tuple-element.60), channel_id=1, source_target_pairs={{0,64},{1,65},{2,66},{3,67},{4,68},{5,69},{6,70},{7,71},{8,72},{9,... | collective-permute-start | bytes 786440 | tf_op jit(solution)/shard_map/ppermute | solution.py:32
  35.3 13.4 %collective-permute-start.10 = (bf16[2,128,512]{2,1,0:T(8,128)(2,1)S(1)}, bf16[2,128,512]{2,1,0:T(8,128)(2,1)S(1)}, u32[]{:S(2)}, u32[]{:S(2)}) collective-permute-start(bf16[2,128,512]{2,1,0:T(8,128)(2,1)S(1)} %get-tuple-element.59), channel_id=1, source_target_pairs={{0,32},{1,33},{2,34},{3,35},{4,36},{5,37},{6,38},{7,39},{8,40},{9,... | collective-permute-start | bytes 786440 | tf_op jit(solution)/shard_map/ppermute | solution.py:32
  35.3 13.4 %collective-permute-start.9 = (bf16[2,128,512]{2,1,0:T(8,128)(2,1)S(1)}, bf16[2,128,512]{2,1,0:T(8,128)(2,1)S(1)}, u32[]{:S(2)}, u32[]{:S(2)}) collective-permute-start(bf16[2,128,512]{2,1,0:T(8,128)(2,1)S(1)} %get-tuple-element.58), channel_id=1, source_target_pairs={{0,96},{1,97},{2,98},{3,99},{4,100},{5,101},{6,102},{7,103},{8,104... | collective-permute-start | bytes 786440 | tf_op jit(solution)/shard_map/ppermute | solution.py:32
  40.3 8.8 %collective-permute-start.13 = (bf16[4,64,512]{2,1,0:T(8,128)(2,1)S(1)}, bf16[4,64,512]{2,1,0:T(8,128)(2,1)S(1)}, u32[]{:S(2)}, u32[]{:S(2)}) collective-permute-start(bf16[4,64,512]{2,1,0:T(8,128)(2,1)S(1)} %collective-permute-done.7.refs_1_), channel_id=1, source_target_pairs={{0,2},{1,3},{2,4},{3,5},{4,6},{5,7},{6,8},{7,9},{8,10},{9,11},{10,... | collective-permute-start | bytes 786440 | tf_op jit(solution)/shard_map/ppermute | solution.py:32
  40.4 8.7 %collective-permute-start.14 = (bf16[4,64,512]{2,1,0:T(8,128)(2,1)S(1)}, bf16[4,64,512]{2,1,0:T(8,128)(2,1)S(1)}, u32[]{:S(2)}, u32[]{:S(2)}) collective-permute-start(bf16[4,64,512]{2,1,0:T(8,128)(2,1)S(1)} %collective-permute-done.8.refs_8_), channel_id=1, source_target_pairs={{0,14},{1,15},{2,0},{3,1},{4,2},{5,3},{6,4},{7,5},{8,6},{9,7},{10,... | collective-permute-start | bytes 786440 | tf_op jit(solution)/shard_map/ppermute | solution.py:32
  48.9 6.0 %collective-permute-start.12 = (bf16[128,512]{1,0:T(8,128)(2,1)S(1)}, bf16[128,512]{1,0:T(8,128)(2,1)S(1)}, u32[]{:S(2)}, u32[]{:S(2)}) collective-permute-start(bf16[128,512]{1,0:T(8,128)(2,1)S(1)} %get-tuple-element.84), channel_id=1, source_target_pairs={{0,2},{1,3},{2,4},{3,5},{4,6},{5,7},{6,8},{7,9},{8,10},{9,11},{10,... | collective-permute-start | bytes 393224 | tf_op jit(solution)/shard_map/ppermute | solution.py:32
  49.0 8.8 %collective-permute-start.15 = (bf16[128,512]{1,0:T(8,128)(2,1)S(1)}, bf16[128,512]{1,0:T(8,128)(2,1)S(1)}, u32[]{:S(2)}, u32[]{:S(2)}) collective-permute-start(bf16[128,512]{1,0:T(8,128)(2,1)S(1)} %get-tuple-element.83), channel_id=1, source_target_pairs={{0,130},{1,131},{2,132},{3,133},{4,134},{5,135},{6,136},{7,137},{8... | collective-permute-start | bytes 393224 | tf_op jit(solution)/shard_map/ppermute | solution.py:32
  49.1 13.7 %collective-permute-start.16 = (bf16[4,64,512]{2,1,0:T(8,128)(2,1)S(1)}, bf16[4,64,512]{2,1,0:T(8,128)(2,1)S(1)}, u32[]{:S(2)}, u32[]{:S(2)}) collective-permute-start(bf16[4,64,512]{2,1,0:T(8,128)(2,1)S(1)} %collective-permute-done.13.refs_2_), channel_id=1, source_target_pairs={{0,2},{1,3},{2,4},{3,5},{4,6},{5,7},{6,8},{7,9},{8,10},{9,11},{10,... | collective-permute-start | bytes 786440 | tf_op jit(solution)/shard_map/ppermute | solution.py:32
  51.4 11.4 %collective-permute-start.17 = (bf16[4,64,512]{2,1,0:T(8,128)(2,1)S(1)}, bf16[4,64,512]{2,1,0:T(8,128)(2,1)S(1)}, u32[]{:S(2)}, u32[]{:S(2)}) collective-permute-start(bf16[4,64,512]{2,1,0:T(8,128)(2,1)S(1)} %collective-permute-done.14.refs_7_), channel_id=1, source_target_pairs={{0,14},{1,15},{2,0},{3,1},{4,2},{5,3},{6,4},{7,5},{8,6},{9,7},{10,... | collective-permute-start | bytes 786440 | tf_op jit(solution)/shard_map/ppermute | solution.py:32
  62.8 6.4 %collective-permute-start.21 = (bf16[128,512]{1,0:T(8,128)(2,1)S(1)}, bf16[128,512]{1,0:T(8,128)(2,1)S(1)}, u32[]{:S(2)}, u32[]{:S(2)}) collective-permute-start(bf16[128,512]{1,0:T(8,128)(2,1)S(1)} %get-tuple-element.72), channel_id=1, source_target_pairs={{0,96},{1,97},{2,98},{3,99},{4,100},{5,101},{6,102},{7,103},{8,104... | collective-permute-start | bytes 393224 | tf_op jit(solution)/shard_map/ppermute | solution.py:32
  62.8 6.4 %collective-permute-start.20 = (bf16[128,512]{1,0:T(8,128)(2,1)S(1)}, bf16[128,512]{1,0:T(8,128)(2,1)S(1)}, u32[]{:S(2)}, u32[]{:S(2)}) collective-permute-start(bf16[128,512]{1,0:T(8,128)(2,1)S(1)} %get-tuple-element.72), channel_id=1, source_target_pairs={{0,64},{1,65},{2,66},{3,67},{4,68},{5,69},{6,70},{7,71},{8,72},{9,... | collective-permute-start | bytes 393224 | tf_op jit(solution)/shard_map/ppermute | solution.py:32
  65.2 6.5 %collective-permute-start.19 = (bf16[128,512]{1,0:T(8,128)(2,1)S(1)}, bf16[128,512]{1,0:T(8,128)(2,1)S(1)}, u32[]{:S(2)}, u32[]{:S(2)}) collective-permute-start(bf16[128,512]{1,0:T(8,128)(2,1)S(1)} %get-tuple-element.72), channel_id=1, source_target_pairs={{0,32},{1,33},{2,34},{3,35},{4,36},{5,37},{6,38},{7,39},{8,40},{9,... | collective-permute-start | bytes 393224 | tf_op jit(solution)/shard_map/ppermute | solution.py:32
  66.1 5.7 %collective-permute-start.22 = (bf16[2,64,512]{2,1,0:T(8,128)(2,1)S(1)}, bf16[2,64,512]{2,1,0:T(8,128)(2,1)S(1)}, u32[]{:S(2)}, u32[]{:S(2)}) collective-permute-start(bf16[2,64,512]{2,1,0:T(8,128)(2,1)S(1)} %slice.14), channel_id=1, source_target_pairs={{0,2},{1,3},{2,4},{3,5},{4,6},{5,7},{6,8},{7,9},{8,10},{9,11},{10,... | collective-permute-start | bytes 393224 | tf_op jit(solution)/shard_map/ppermute | solution.py:32
  66.2 5.6 %collective-permute-start.23 = (bf16[2,64,512]{2,1,0:T(8,128)(2,1)S(1)}, bf16[2,64,512]{2,1,0:T(8,128)(2,1)S(1)}, u32[]{:S(2)}, u32[]{:S(2)}) collective-permute-start(bf16[2,64,512]{2,1,0:T(8,128)(2,1)S(1)} %slice.15), channel_id=1, source_target_pairs={{0,14},{1,15},{2,0},{3,1},{4,2},{5,3},{6,4},{7,5},{8,6},{9,7},{10,... | collective-permute-start | bytes 393224 | tf_op jit(solution)/shard_map/ppermute | solution.py:32
  77.1 7.8 %collective-permute-start.25 = (bf16[128,1024]{1,0:T(8,128)(2,1)S(1)}, bf16[128,1024]{1,0:T(8,128)(2,1)}, u32[]{:S(2)}, u32[]{:S(2)}) collective-permute-start(bf16[128,1024]{1,0:T(8,128)(2,1)S(1)} %get-tuple-element.78), channel_id=1, source_target_pairs={{0,96},{1,97},{2,98},{3,99},{4,100},{5,101},{6,102},{7,103},{8,104... | collective-permute-start | bytes 786440 | tf_op jit(solution)/shard_map/ppermute | solution.py:32
  79.2 8.9 %collective-permute-start.26 = (bf16[128,1024]{1,0:T(8,128)(2,1)S(1)}, bf16[128,1024]{1,0:T(8,128)(2,1)}, u32[]{:S(2)}, u32[]{:S(2)}) collective-permute-start(bf16[128,1024]{1,0:T(8,128)(2,1)S(1)} %get-tuple-element.79), channel_id=1, source_target_pairs={{0,64},{1,65},{2,66},{3,67},{4,68},{5,69},{6,70},{7,71},{8,72},{9,... | collective-permute-start | bytes 786440 | tf_op jit(solution)/shard_map/ppermute | solution.py:32
  79.5 15.1 %collective-permute-start.27 = (bf16[128,1024]{1,0:T(8,128)(2,1)S(1)}, bf16[128,1024]{1,0:T(8,128)(2,1)}, u32[]{:S(2)}, u32[]{:S(2)}) collective-permute-start(bf16[128,1024]{1,0:T(8,128)(2,1)S(1)} %get-tuple-element.80), channel_id=1, source_target_pairs={{0,32},{1,33},{2,34},{3,35},{4,36},{5,37},{6,38},{7,39},{8,40},{9,... | collective-permute-start | bytes 786440 | tf_op jit(solution)/shard_map/ppermute | solution.py:32
  (13 other events, 107.4 us)

commit v5 on v3

--- a/solution.py
+++ b/solution.py
@@ -45,13 +45,16 @@
 
 
 def delta_body(do_ref, o_ref, lse_ref, delta_ref, lse2_ref):
-    ones = jnp.ones((8, HD), F32)
+    ones = jnp.ones((8, 3 * HD), BF16)
     for h in range(16):
         cols = slice(h * HD, (h + 1) * HD)
-        prod = do_ref[:, cols].astype(F32) * o_ref[:, cols].astype(F32)
+        rest = do_ref[:, cols].astype(F32) * o_ref[:, cols].astype(F32)
+        pieces = []
+        for _ in range(3):
+            pieces.append(rest.astype(BF16))
+            rest = rest - pieces[-1].astype(F32)
         row = lax.dot_general(
-            ones, prod, (((1,), (1,)), ((), ())),
-            precision=lax.Precision.HIGHEST, preferred_element_type=F32,
+            ones, jnp.concatenate(pieces, axis=1), (((1,), (1,)), ((), ())), preferred_element_type=F32
         )
         delta_ref[h : h + 1, :] = row[0:1]
     lse2_ref[...] = lse_ref[...] * LOG2E

time: 96.4 us -> 96.2 us (level)
  Pallas kernels: 19 us -> 17.9 us
    pallas_call x1, Pallas kernels: 3.54 us -> 2.47 us  [shards(): pl.pallas_call(delta_body, in_specs=[vmem] * 3, out_specs=[vmem] * 2, out...]
  transfers between devices with their start and end apart: 27 -> 27, of which waited for: 14 -> 14; matrix products, arithmetic and copies ran while one was open for 2% -> 2% of each run, Pallas kernels for 14% -> 13%
where the time goes in v5:
time: 96.2 us; the launch traced here: 96 us
  starting transfers between devices  44.5 us (46%)
  waiting for transfers between devices  29.5 us (31%)
  Pallas kernels  17.9 us (19%)
  local copies, waits for them, and re-layouts  2.72 us (3%)
  between operations  1.12 us (1%)
    ppermute x27, starting transfers between devices, permute(): return lax.ppermute(value, AXES, pairs)  44.5 us
    ppermute x27, waiting for transfers between devices, permute(): return lax.ppermute(value, AXES, pairs)  29.5 us
    pallas_call x4, Pallas kernels, attend(): pl.pallas_call(lambda *refs: attend_body(shift, *refs), in_specs=[pl.Bloc...  9.31 us
    pallas_call x1, Pallas kernels, shards(): pl.pallas_call(delta_body, in_specs=[vmem] * 3, out_specs=[vmem] * 2, out...  2.47 us
    pallas_call x1, Pallas kernels, shards(): pl.pallas_call(gather_body, in_specs=[vmem] * 4, out_specs=pl.BlockSpec(m...  2.18 us
    pallas_call x2, Pallas kernels, dx_parts(): pl.pallas_call(dx_body, in_specs=[vmem] * 10, out_specs=[vmem] * count, o...  2.12 us
  transfers between devices with their start and end apart: 27, of which 14 were waited for; matrix products, arithmetic and copies ran while one was open for 2% of the time, Pallas kernels for 13%

profile of v5, /device:TPU:1, one launch (start us, length us, event | category | flops | bytes accessed | tf_op | source)
XLA Modules:
  0.0 96.0 jit_solution(155134031447374052)
XLA Ops:
  0.6 3.8 %collective-permute-start = (bf16[128,2,256]{2,1,0:T(2,128)(2,1)}, bf16[128,2,256]{2,1,0:T(2,128)(2,1)S(1)}, u32[]{:S(2)}, u32[]{:S(2)}) collective-permute-start(bf16[128,2,256]{2,1,0:T(2,128)(2,1)} %param.13), channel_id=1, source_target_pairs={{0,128},{1,129},{2,130},{3,131},{4,132},{5,133},{6,134},{7,135},{8... | collective-permute-start | bytes 393224 | tf_op jit(solution)/shard_map/ppermute | solution.py:32
  5.5 2.5 %row_sums.1 = (f32[16,128]{1,0:T(8,128)}, f32[16,128]{1,0:T(8,128)}) custom-call(bf16[128,2048]{1,0:T(8,128)(2,1)} %refs_2_.7, bf16[128,2048]{1,0:T(8,128)(2,1)} %o_ref.1, f32[16,128]{1,0:T(8,128)} %lse_ref.1), custom_call_target="tpu_custom_call" | custom-call | flops 1000 | bytes 1000 | tf_op jit(solution)/shard_map/row_sums/pallas_call | solution.py:210
  8.2 2.6 %collective-permute-done.4 = bf16[1,64,512]{2,1,0:T(8,128)(2,1)S(1)} collective-permute-done((bf16[1,64,512]{2,1,0:T(8,128)(2,1)S(1)}, bf16[1,64,512]{2,1,0:T(8,128)(2,1)S(1)}, u32[]{:S(2)}, u32[]{:S(2)}) %collective-permute-start.4) | collective-permute-done | bytes 65568 | tf_op jit(solution)/shard_map/ppermute | solution.py:32
  19.8 4.0 %collective-permute-start.8 = (bf16[4,64,512]{2,1,0:T(8,128)(2,1)S(1)}, bf16[4,64,512]{2,1,0:T(8,128)(2,1)S(1)}, u32[]{:S(2)}, u32[]{:S(2)}) collective-permute-start(bf16[4,64,512]{2,1,0:T(8,128)(2,1)S(1)} %pad_maximum_fusion.1.refs_0_), channel_id=1, source_target_pairs={{0,14},{1,15},{2,0},{3,1},{4,2},{5,3},{6,4},{7,5},{8,6},{9,7},{10,... | collective-permute-start | bytes 786440 | tf_op jit(solution)/shard_map/ppermute | solution.py:32
  23.8 4.9 %collective-permute-done.3.refs_5_.refs_3_ = bf16[2,128,512]{2,1,0:T(8,128)(2,1)S(1)} collective-permute-done((bf16[2,128,512]{2,1,0:T(8,128)(2,1)S(1)}, bf16[2,128,512]{2,1,0:T(8,128)(2,1)S(1)}, u32[]{:S(2)}, u32[]{:S(2)}) %collective-permute-start.3) | collective-permute-done | bytes 262176 | tf_op jit(solution)/shard_map/ppermute | solution.py:32
  28.8 2.3 %attend.4 = (bf16[2,128,512]{2,1,0:T(8,128)(2,1)S(1)}, bf16[256,2048]{1,0:T(8,128)(2,1)S(1)}) custom-call(s32[256]{0:T(256)S(1)} %copy-done.6, bf16[128,2048]{1,0:T(8,128)(2,1)S(1)} %copy-done.1, bf16[128,2048]{1,0:T(8,128)(2,1)S(1)} %copy-done, f32[16,128]{1,0:T(8,128)S(1)} %copy-done.5, f32[16,128]{1,0:T(8,128)S(1)} %copy-done.4, ...), custom_call_target="tpu_custom_call" | custom-call | flops 1000 | bytes 1000 | tf_op jit(solution)/shard_map/attend/pallas_call | solution.py:118
  31.1 2.3 %attend.5 = (bf16[2,128,512]{2,1,0:T(8,128)(2,1)S(1)}, bf16[256,2048]{1,0:T(8,128)(2,1)S(1)}) custom-call(s32[256]{0:T(256)S(1)} %copy-done.6, bf16[128,2048]{1,0:T(8,128)(2,1)S(1)} %copy-done.1, bf16[128,2048]{1,0:T(8,128)(2,1)S(1)} %copy-done, f32[16,128]{1,0:T(8,128)S(1)} %copy-done.5, f32[16,128]{1,0:T(8,128)S(1)} %copy-done.4, ...), custom_call_target="tpu_custom_call" | custom-call | flops 1000 | bytes 1000 | tf_op jit(solution)/shard_map/attend/pallas_call | solution.py:118
  33.4 2.3 %attend.6 = (bf16[2,128,512]{2,1,0:T(8,128)(2,1)S(1)}, bf16[256,2048]{1,0:T(8,128)(2,1)S(1)}) custom-call(s32[256]{0:T(256)S(1)} %copy-done.6, bf16[128,2048]{1,0:T(8,128)(2,1)S(1)} %copy-done.1, bf16[128,2048]{1,0:T(8,128)(2,1)S(1)} %copy-done, f32[16,128]{1,0:T(8,128)S(1)} %copy-done.5, f32[16,128]{1,0:T(8,128)S(1)} %copy-done.4, ...), custom_call_target="tpu_custom_call" | custom-call | flops 1000 | bytes 1000 | tf_op jit(solution)/shard_map/attend/pallas_call | solution.py:118
  38.0 3.9 %collective-permute-start.13 = (bf16[4,64,512]{2,1,0:T(8,128)(2,1)S(1)}, bf16[4,64,512]{2,1,0:T(8,128)(2,1)S(1)}, u32[]{:S(2)}, u32[]{:S(2)}) collective-permute-start(bf16[4,64,512]{2,1,0:T(8,128)(2,1)S(1)} %collective-permute-done.8.refs_7_), channel_id=1, source_target_pairs={{0,14},{1,15},{2,0},{3,1},{4,2},{5,3},{6,4},{7,5},{8,6},{9,7},{10,... | collective-permute-start | bytes 786440 | tf_op jit(solution)/shard_map/ppermute | solution.py:32
  44.6 2.3 %attend.7 = (bf16[2,128,512]{2,1,0:T(8,128)(2,1)S(1)}, bf16[256,2048]{1,0:T(8,128)(2,1)S(1)}) custom-call(s32[256]{0:T(256)S(1)} %copy-done.6, bf16[128,2048]{1,0:T(8,128)(2,1)S(1)} %copy-done.1, bf16[128,2048]{1,0:T(8,128)(2,1)S(1)} %copy-done, f32[16,128]{1,0:T(8,128)S(1)} %copy-done.5, f32[16,128]{1,0:T(8,128)S(1)} %copy-done.4, ...), custom_call_target="tpu_custom_call" | custom-call | flops 1000 | bytes 1000 | tf_op jit(solution)/shard_map/attend/pallas_call | solution.py:118
  47.1 2.7 %collective-permute-start.16 = (bf16[4,64,512]{2,1,0:T(8,128)(2,1)S(1)}, bf16[4,64,512]{2,1,0:T(8,128)(2,1)S(1)}, u32[]{:S(2)}, u32[]{:S(2)}) collective-permute-start(bf16[4,64,512]{2,1,0:T(8,128)(2,1)S(1)} %collective-permute-done.13.refs_6_), channel_id=1, source_target_pairs={{0,14},{1,15},{2,0},{3,1},{4,2},{5,3},{6,4},{7,5},{8,6},{9,7},{10,... | collective-permute-start | bytes 786440 | tf_op jit(solution)/shard_map/ppermute | solution.py:32
  50.0 2.7 %collective-permute-start.14 = (bf16[128,512]{1,0:T(8,128)(2,1)S(1)}, bf16[128,512]{1,0:T(8,128)(2,1)S(1)}, u32[]{:S(2)}, u32[]{:S(2)}) collective-permute-start(bf16[128,512]{1,0:T(8,128)(2,1)S(1)} %get-tuple-element.82), channel_id=1, source_target_pairs={{0,2},{1,3},{2,4},{3,5},{4,6},{5,7},{6,8},{7,9},{8,10},{9,11},{10,... | collective-permute-start | bytes 393224 | tf_op jit(solution)/shard_map/ppermute | solution.py:32
  52.7 3.3 %collective-permute-start.17 = (bf16[128,512]{1,0:T(8,128)(2,1)S(1)}, bf16[128,512]{1,0:T(8,128)(2,1)S(1)}, u32[]{:S(2)}, u32[]{:S(2)}) collective-permute-start(bf16[128,512]{1,0:T(8,128)(2,1)S(1)} %get-tuple-element.81), channel_id=1, source_target_pairs={{0,130},{1,131},{2,132},{3,133},{4,134},{5,135},{6,136},{7,137},{8... | collective-permute-start | bytes 393224 | tf_op jit(solution)/shard_map/ppermute | solution.py:32
  56.0 1.8 %query_grad.1 = f32[128,2048]{1,0:T(8,128)} custom-call(bf16[2,128,512]{2,1,0:T(8,128)(2,1)S(1)} %constant_dynamic-update-slice_fusion.refs_5_.refs_0_, bf16[2,128,512]{2,1,0:T(8,128)(2,1)S(1)} %collective-permute-done.1.refs_5_.refs_1_, bf16[2,128,512]{2,1,0:T(8,128)(2,1)S(1)} %collective-permute-done.2.refs_5_.refs_2_, ...), custom_call_target="tpu_custom_call" | custom-call | flops 1000 | bytes 12000000 | tf_op jit(solution)/shard_map/query_grad/pallas_call | solution.py:246
  57.8 2.7 %collective-permute-done.14 = bf16[128,512]{1,0:T(8,128)(2,1)S(1)} collective-permute-done((bf16[128,512]{1,0:T(8,128)(2,1)S(1)}, bf16[128,512]{1,0:T(8,128)(2,1)S(1)}, u32[]{:S(2)}, u32[]{:S(2)}) %collective-permute-start.14) | collective-permute-done | bytes 131104 | tf_op jit(solution)/shard_map/ppermute | solution.py:32
  60.6 2.1 %collective-permute-done.17 = bf16[128,512]{1,0:T(8,128)(2,1)S(1)} collective-permute-done((bf16[128,512]{1,0:T(8,128)(2,1)S(1)}, bf16[128,512]{1,0:T(8,128)(2,1)S(1)}, u32[]{:S(2)}, u32[]{:S(2)}) %collective-permute-start.17) | collective-permute-done | bytes 131104 | tf_op jit(solution)/shard_map/ppermute | solution.py:32
  63.6 2.0 %collective-permute-start.20 = (bf16[128,512]{1,0:T(8,128)(2,1)S(1)}, bf16[128,512]{1,0:T(8,128)(2,1)S(1)}, u32[]{:S(2)}, u32[]{:S(2)}) collective-permute-start(bf16[128,512]{1,0:T(8,128)(2,1)S(1)} %get-tuple-element.79), channel_id=1, source_target_pairs={{0,64},{1,65},{2,66},{3,67},{4,68},{5,69},{6,70},{7,71},{8,72},{9,... | collective-permute-start | bytes 393224 | tf_op jit(solution)/shard_map/ppermute | solution.py:32
  66.1 2.0 %collective-permute-done.19 = bf16[128,512]{1,0:T(8,128)(2,1)S(1)} collective-permute-done((bf16[128,512]{1,0:T(8,128)(2,1)S(1)}, bf16[128,512]{1,0:T(8,128)(2,1)S(1)}, u32[]{:S(2)}, u32[]{:S(2)}) %collective-permute-start.19) | collective-permute-done | bytes 131104 | tf_op jit(solution)/shard_map/ppermute | solution.py:32
  70.2 3.7 %collective-permute-start.23 = (bf16[3,128,512]{2,1,0:T(8,128)(2,1)S(1)}, bf16[3,128,512]{2,1,0:T(8,128)(2,1)S(1)}, u32[]{:S(2)}, u32[]{:S(2)}) collective-permute-start(bf16[3,128,512]{2,1,0:T(8,128)(2,1)S(1)} %pad_maximum_fusion.own_ref), channel_id=1, source_target_pairs={{0,1},{1,0},{2,3},{3,2},{4,5},{5,4},{6,7},{7,6},{8,9},{9,8},{10,11... | collective-permute-start | bytes 1179656 | tf_op jit(solution)/shard_map/ppermute | solution.py:32
  76.4 2.5 %collective-permute-start.24 = (bf16[128,1024]{1,0:T(8,128)(2,1)S(1)}, bf16[128,1024]{1,0:T(8,128)(2,1)}, u32[]{:S(2)}, u32[]{:S(2)}) collective-permute-start(bf16[128,1024]{1,0:T(8,128)(2,1)S(1)} %get-tuple-element.76), channel_id=1, source_target_pairs={{0,96},{1,97},{2,98},{3,99},{4,100},{5,101},{6,102},{7,103},{8,104... | collective-permute-start | bytes 786440 | tf_op jit(solution)/shard_map/ppermute | solution.py:32
  83.1 1.7 %collective-permute-done.24.p1 = bf16[128,1024]{1,0:T(8,128)(2,1)} collective-permute-done((bf16[128,1024]{1,0:T(8,128)(2,1)S(1)}, bf16[128,1024]{1,0:T(8,128)(2,1)}, u32[]{:S(2)}, u32[]{:S(2)}) %collective-permute-start.24) | collective-permute-done | bytes 262176 | tf_op jit(solution)/shard_map/ppermute | solution.py:32
  84.8 2.9 %collective-permute-done.25.p2 = bf16[128,1024]{1,0:T(8,128)(2,1)} collective-permute-done((bf16[128,1024]{1,0:T(8,128)(2,1)S(1)}, bf16[128,1024]{1,0:T(8,128)(2,1)}, u32[]{:S(2)}, u32[]{:S(2)}) %collective-permute-start.25) | collective-permute-done | bytes 262176 | tf_op jit(solution)/shard_map/ppermute | solution.py:32
  87.7 6.0 %collective-permute-done.26.p3 = bf16[128,1024]{1,0:T(8,128)(2,1)} collective-permute-done((bf16[128,1024]{1,0:T(8,128)(2,1)S(1)}, bf16[128,1024]{1,0:T(8,128)(2,1)}, u32[]{:S(2)}, u32[]{:S(2)}) %collective-permute-start.26) | collective-permute-done | bytes 262176 | tf_op jit(solution)/shard_map/ppermute | solution.py:32
  93.7 2.2 %join_parts.1 = bf16[128,4096]{1,0:T(8,128)(2,1)} custom-call(bf16[128,1024]{1,0:T(8,128)(2,1)} %copy-done.3, bf16[128,1024]{1,0:T(8,128)(2,1)} %collective-permute-done.24.p1, bf16[128,1024]{1,0:T(8,128)(2,1)} %collective-permute-done.25.p2, bf16[128,1024]{1,0:T(8,128)(2,1)} %collective-permute-done.26.p3), custom_call_target="tpu_custom_call" | custom-call | flops 1000 | bytes 1000 | tf_op jit(solution)/shard_map/join_parts/pallas_call | solution.py:272
  (71 shorter events, 25.6 us)
Async XLA Ops:
  0.6 7.4 %collective-permute-start = (bf16[128,2,256]{2,1,0:T(2,128)(2,1)}, bf16[128,2,256]{2,1,0:T(2,128)(2,1)S(1)}, u32[]{:S(2)}, u32[]{:S(2)}) collective-permute-start(bf16[128,2,256]{2,1,0:T(2,128)(2,1)} %param.13), channel_id=1, source_target_pairs={{0,128},{1,129},{2,130},{3,131},{4,132},{5,133},{6,134},{7,135},{8... | collective-permute-start | bytes 393224 | tf_op jit(solution)/shard_map/ppermute | solution.py:32
  5.4 5.5 %collective-permute-start.4 = (bf16[1,64,512]{2,1,0:T(8,128)(2,1)S(1)}, bf16[1,64,512]{2,1,0:T(8,128)(2,1)S(1)}, u32[]{:S(2)}, u32[]{:S(2)}) collective-permute-start(bf16[1,64,512]{2,1,0:T(8,128)(2,1)S(1)} %reshape.20), channel_id=1, source_target_pairs={{0,128},{1,129},{2,130},{3,131},{4,132},{5,133},{6,134},{7,135},{8... | collective-permute-start | bytes 196616 | tf_op jit(solution)/shard_map/ppermute | solution.py:32
  13.2 4.8 %collective-permute-start.6 = (bf16[2,64,512]{2,1,0:T(8,128)(2,1)S(1)}, bf16[2,64,512]{2,1,0:T(8,128)(2,1)S(1)}, u32[]{:S(2)}, u32[]{:S(2)}) collective-permute-start(bf16[2,64,512]{2,1,0:T(8,128)(2,1)S(1)} %pad_maximum_fusion.2), channel_id=1, source_target_pairs={{0,16},{1,17},{2,18},{3,19},{4,20},{5,21},{6,22},{7,23},{8,24},{9,... | collective-permute-start | bytes 393224 | tf_op jit(solution)/shard_map/ppermute | solution.py:32
  13.7 10.1 %collective-permute-start.1 = (bf16[2,128,512]{2,1,0:T(8,128)(2,1)S(1)}, bf16[2,128,512]{2,1,0:T(8,128)(2,1)S(1)}, u32[]{:S(2)}, u32[]{:S(2)}) collective-permute-start(bf16[2,128,512]{2,1,0:T(8,128)(2,1)S(1)} %constant_dynamic-update-slice_fusion.refs_5_.refs_0_), channel_id=1, source_target_pairs={{0,32},{1,33},{2,34},{3,35},{4,36},{5,37},{6,38},{7,39},{8,40},{9,... | collective-permute-start | bytes 786440 | tf_op jit(solution)/shard_map/ppermute | solution.py:32
  14.9 8.9 %collective-permute-start.2 = (bf16[2,128,512]{2,1,0:T(8,128)(2,1)S(1)}, bf16[2,128,512]{2,1,0:T(8,128)(2,1)S(1)}, u32[]{:S(2)}, u32[]{:S(2)}) collective-permute-start(bf16[2,128,512]{2,1,0:T(8,128)(2,1)S(1)} %constant_dynamic-update-slice_fusion.refs_5_.refs_0_), channel_id=1, source_target_pairs={{0,96},{1,97},{2,98},{3,99},{4,100},{5,101},{6,102},{7,103},{8,104... | collective-permute-start | bytes 786440 | tf_op jit(solution)/shard_map/ppermute | solution.py:32
  16.4 12.4 %collective-permute-start.3 = (bf16[2,128,512]{2,1,0:T(8,128)(2,1)S(1)}, bf16[2,128,512]{2,1,0:T(8,128)(2,1)S(1)}, u32[]{:S(2)}, u32[]{:S(2)}) collective-permute-start(bf16[2,128,512]{2,1,0:T(8,128)(2,1)S(1)} %constant_dynamic-update-slice_fusion.refs_5_.refs_0_), channel_id=1, source_target_pairs={{0,64},{1,65},{2,66},{3,67},{4,68},{5,69},{6,70},{7,71},{8,72},{9,... | collective-permute-start | bytes 786440 | tf_op jit(solution)/shard_map/ppermute | solution.py:32
  18.1 15.4 %collective-permute-start.7 = (bf16[4,64,512]{2,1,0:T(8,128)(2,1)S(1)}, bf16[4,64,512]{2,1,0:T(8,128)(2,1)S(1)}, u32[]{:S(2)}, u32[]{:S(2)}) collective-permute-start(bf16[4,64,512]{2,1,0:T(8,128)(2,1)S(1)} %pad_maximum_fusion.1.refs_0_), channel_id=1, source_target_pairs={{0,2},{1,3},{2,4},{3,5},{4,6},{5,7},{6,8},{7,9},{8,10},{9,11},{10,... | collective-permute-start | bytes 786440 | tf_op jit(solution)/shard_map/ppermute | solution.py:32
  19.8 13.7 %collective-permute-start.8 = (bf16[4,64,512]{2,1,0:T(8,128)(2,1)S(1)}, bf16[4,64,512]{2,1,0:T(8,128)(2,1)S(1)}, u32[]{:S(2)}, u32[]{:S(2)}) collective-permute-start(bf16[4,64,512]{2,1,0:T(8,128)(2,1)S(1)} %pad_maximum_fusion.1.refs_0_), channel_id=1, source_target_pairs={{0,14},{1,15},{2,0},{3,1},{4,2},{5,3},{6,4},{7,5},{8,6},{9,7},{10,... | collective-permute-start | bytes 786440 | tf_op jit(solution)/shard_map/ppermute | solution.py:32
  35.8 11.2 %collective-permute-start.11 = (bf16[2,128,512]{2,1,0:T(8,128)(2,1)S(1)}, bf16[2,128,512]{2,1,0:T(8,128)(2,1)S(1)}, u32[]{:S(2)}, u32[]{:S(2)}) collective-permute-start(bf16[2,128,512]{2,1,0:T(8,128)(2,1)S(1)} %get-tuple-element.60), channel_id=1, source_target_pairs={{0,64},{1,65},{2,66},{3,67},{4,68},{5,69},{6,70},{7,71},{8,72},{9,... | collective-permute-start | bytes 786440 | tf_op jit(solution)/shard_map/ppermute | solution.py:32
  36.4 10.6 %collective-permute-start.12 = (bf16[4,64,512]{2,1,0:T(8,128)(2,1)S(1)}, bf16[4,64,512]{2,1,0:T(8,128)(2,1)S(1)}, u32[]{:S(2)}, u32[]{:S(2)}) collective-permute-start(bf16[4,64,512]{2,1,0:T(8,128)(2,1)S(1)} %collective-permute-done.7.refs_1_), channel_id=1, source_target_pairs={{0,2},{1,3},{2,4},{3,5},{4,6},{5,7},{6,8},{7,9},{8,10},{9,11},{10,... | collective-permute-start | bytes 786440 | tf_op jit(solution)/shard_map/ppermute | solution.py:32
  38.0 9.0 %collective-permute-start.13 = (bf16[4,64,512]{2,1,0:T(8,128)(2,1)S(1)}, bf16[4,64,512]{2,1,0:T(8,128)(2,1)S(1)}, u32[]{:S(2)}, u32[]{:S(2)}) collective-permute-start(bf16[4,64,512]{2,1,0:T(8,128)(2,1)S(1)} %collective-permute-done.8.refs_7_), channel_id=1, source_target_pairs={{0,14},{1,15},{2,0},{3,1},{4,2},{5,3},{6,4},{7,5},{8,6},{9,7},{10,... | collective-permute-start | bytes 786440 | tf_op jit(solution)/shard_map/ppermute | solution.py:32
  42.0 7.8 %collective-permute-start.10 = (bf16[2,128,512]{2,1,0:T(8,128)(2,1)S(1)}, bf16[2,128,512]{2,1,0:T(8,128)(2,1)S(1)}, u32[]{:S(2)}, u32[]{:S(2)}) collective-permute-start(bf16[2,128,512]{2,1,0:T(8,128)(2,1)S(1)} %get-tuple-element.59), channel_id=1, source_target_pairs={{0,32},{1,33},{2,34},{3,35},{4,36},{5,37},{6,38},{7,39},{8,40},{9,... | collective-permute-start | bytes 786440 | tf_op jit(solution)/shard_map/ppermute | solution.py:32
  43.2 6.6 %collective-permute-start.9 = (bf16[2,128,512]{2,1,0:T(8,128)(2,1)S(1)}, bf16[2,128,512]{2,1,0:T(8,128)(2,1)S(1)}, u32[]{:S(2)}, u32[]{:S(2)}) collective-permute-start(bf16[2,128,512]{2,1,0:T(8,128)(2,1)S(1)} %get-tuple-element.58), channel_id=1, source_target_pairs={{0,96},{1,97},{2,98},{3,99},{4,100},{5,101},{6,102},{7,103},{8,104... | collective-permute-start | bytes 786440 | tf_op jit(solution)/shard_map/ppermute | solution.py:32
  47.0 13.5 %collective-permute-start.15 = (bf16[4,64,512]{2,1,0:T(8,128)(2,1)S(1)}, bf16[4,64,512]{2,1,0:T(8,128)(2,1)S(1)}, u32[]{:S(2)}, u32[]{:S(2)}) collective-permute-start(bf16[4,64,512]{2,1,0:T(8,128)(2,1)S(1)} %collective-permute-done.12.refs_2_), channel_id=1, source_target_pairs={{0,2},{1,3},{2,4},{3,5},{4,6},{5,7},{6,8},{7,9},{8,10},{9,11},{10,... | collective-permute-start | bytes 786440 | tf_op jit(solution)/shard_map/ppermute | solution.py:32
  47.1 13.4 %collective-permute-start.16 = (bf16[4,64,512]{2,1,0:T(8,128)(2,1)S(1)}, bf16[4,64,512]{2,1,0:T(8,128)(2,1)S(1)}, u32[]{:S(2)}, u32[]{:S(2)}) collective-permute-start(bf16[4,64,512]{2,1,0:T(8,128)(2,1)S(1)} %collective-permute-done.13.refs_6_), channel_id=1, source_target_pairs={{0,14},{1,15},{2,0},{3,1},{4,2},{5,3},{6,4},{7,5},{8,6},{9,7},{10,... | collective-permute-start | bytes 786440 | tf_op jit(solution)/shard_map/ppermute | solution.py:32
  50.0 10.6 %collective-permute-start.14 = (bf16[128,512]{1,0:T(8,128)(2,1)S(1)}, bf16[128,512]{1,0:T(8,128)(2,1)S(1)}, u32[]{:S(2)}, u32[]{:S(2)}) collective-permute-start(bf16[128,512]{1,0:T(8,128)(2,1)S(1)} %get-tuple-element.82), channel_id=1, source_target_pairs={{0,2},{1,3},{2,4},{3,5},{4,6},{5,7},{6,8},{7,9},{8,10},{9,11},{10,... | collective-permute-start | bytes 393224 | tf_op jit(solution)/shard_map/ppermute | solution.py:32
  52.7 10.0 %collective-permute-start.17 = (bf16[128,512]{1,0:T(8,128)(2,1)S(1)}, bf16[128,512]{1,0:T(8,128)(2,1)S(1)}, u32[]{:S(2)}, u32[]{:S(2)}) collective-permute-start(bf16[128,512]{1,0:T(8,128)(2,1)S(1)} %get-tuple-element.81), channel_id=1, source_target_pairs={{0,130},{1,131},{2,132},{3,133},{4,134},{5,135},{6,136},{7,137},{8... | collective-permute-start | bytes 393224 | tf_op jit(solution)/shard_map/ppermute | solution.py:32
  60.5 9.6 %collective-permute-start.22 = (bf16[4,64,512]{2,1,0:T(8,128)(2,1)S(1)}, bf16[4,64,512]{2,1,0:T(8,128)(2,1)S(1)}, u32[]{:S(2)}, u32[]{:S(2)}) collective-permute-start(bf16[4,64,512]{2,1,0:T(8,128)(2,1)S(1)} %collective-permute-done.15.refs_3_), channel_id=1, source_target_pairs={{0,2},{1,3},{2,4},{3,5},{4,6},{5,7},{6,8},{7,9},{8,10},{9,11},{10,... | collective-permute-start | bytes 786440 | tf_op jit(solution)/shard_map/ppermute | solution.py:32
  62.7 5.4 %collective-permute-start.19 = (bf16[128,512]{1,0:T(8,128)(2,1)S(1)}, bf16[128,512]{1,0:T(8,128)(2,1)S(1)}, u32[]{:S(2)}, u32[]{:S(2)}) collective-permute-start(bf16[128,512]{1,0:T(8,128)(2,1)S(1)} %get-tuple-element.79), channel_id=1, source_target_pairs={{0,32},{1,33},{2,34},{3,35},{4,36},{5,37},{6,38},{7,39},{8,40},{9,... | collective-permute-start | bytes 393224 | tf_op jit(solution)/shard_map/ppermute | solution.py:32
  63.6 5.7 %collective-permute-start.20 = (bf16[128,512]{1,0:T(8,128)(2,1)S(1)}, bf16[128,512]{1,0:T(8,128)(2,1)S(1)}, u32[]{:S(2)}, u32[]{:S(2)}) collective-permute-start(bf16[128,512]{1,0:T(8,128)(2,1)S(1)} %get-tuple-element.79), channel_id=1, source_target_pairs={{0,64},{1,65},{2,66},{3,67},{4,68},{5,69},{6,70},{7,71},{8,72},{9,... | collective-permute-start | bytes 393224 | tf_op jit(solution)/shard_map/ppermute | solution.py:32
  70.2 5.1 %collective-permute-start.23 = (bf16[3,128,512]{2,1,0:T(8,128)(2,1)S(1)}, bf16[3,128,512]{2,1,0:T(8,128)(2,1)S(1)}, u32[]{:S(2)}, u32[]{:S(2)}) collective-permute-start(bf16[3,128,512]{2,1,0:T(8,128)(2,1)S(1)} %pad_maximum_fusion.own_ref), channel_id=1, source_target_pairs={{0,1},{1,0},{2,3},{3,2},{4,5},{5,4},{6,7},{7,6},{8,9},{9,8},{10,11... | collective-permute-start | bytes 1179656 | tf_op jit(solution)/shard_map/ppermute | solution.py:32
  76.4 8.5 %collective-permute-start.24 = (bf16[128,1024]{1,0:T(8,128)(2,1)S(1)}, bf16[128,1024]{1,0:T(8,128)(2,1)}, u32[]{:S(2)}, u32[]{:S(2)}) collective-permute-start(bf16[128,1024]{1,0:T(8,128)(2,1)S(1)} %get-tuple-element.76), channel_id=1, source_target_pairs={{0,96},{1,97},{2,98},{3,99},{4,100},{5,101},{6,102},{7,103},{8,104... | collective-permute-start | bytes 786440 | tf_op jit(solution)/shard_map/ppermute | solution.py:32
  78.8 8.9 %collective-permute-start.25 = (bf16[128,1024]{1,0:T(8,128)(2,1)S(1)}, bf16[128,1024]{1,0:T(8,128)(2,1)}, u32[]{:S(2)}, u32[]{:S(2)}) collective-permute-start(bf16[128,1024]{1,0:T(8,128)(2,1)S(1)} %get-tuple-element.77), channel_id=1, source_target_pairs={{0,64},{1,65},{2,66},{3,67},{4,68},{5,69},{6,70},{7,71},{8,72},{9,... | collective-permute-start | bytes 786440 | tf_op jit(solution)/shard_map/ppermute | solution.py:32
  78.8 14.8 %collective-permute-start.26 = (bf16[128,1024]{1,0:T(8,128)(2,1)S(1)}, bf16[128,1024]{1,0:T(8,128)(2,1)}, u32[]{:S(2)}, u32[]{:S(2)}) collective-permute-start(bf16[128,1024]{1,0:T(8,128)(2,1)S(1)} %get-tuple-element.78), channel_id=1, source_target_pairs={{0,32},{1,33},{2,34},{3,35},{4,36},{5,37},{6,38},{7,39},{8,40},{9,... | collective-permute-start | bytes 786440 | tf_op jit(solution)/shard_map/ppermute | solution.py:32
  (12 other events, 122.0 us)

commit v6 on v5

--- a/solution.py
+++ b/solution.py
@@ -228,17 +228,17 @@
     w = jnp.concatenate([kept, permute(sent, lambda a, x, b, z, h: (a, x, b, z, 1 - h))], axis=0)
     w = jnp.concatenate([w, permute(w, lambda a, x, b, z, h: (a, x, 1 - b, z, h))], axis=0)
     f1, g1 = step(w, 1), step(w, -1)
-    pairs[1], pairs[3], pairs[2] = lax.optimization_barrier((pairs[1], pairs[3], pairs[2]))
+    pairs[1], pairs[3] = lax.optimization_barrier((pairs[1], pairs[3]))
     t1, ds1 = run(1, pairs[1])
     back1 = permute(t1, along_x(-1))
     ds1, pairs[3] = lax.optimization_barrier((ds1, pairs[3]))
     t3, ds3 = run(3, pairs[3])
     back3 = permute(t3, along_x(-3))
-    ds3, pairs[2], f1, g1 = lax.optimization_barrier((ds3, pairs[2], f1, g1))
+    ds3, pairs[2] = lax.optimization_barrier((ds3, pairs[2]))
     t2, ds2 = run(2, pairs[2])
     back2 = permute(t2, along_x(-2))
+    ds2, own_pair, f1, g1 = lax.optimization_barrier((ds2, pair, f1, g1))
     f2, g2 = step(f1, 1), step(g1, -1)
-    ds2, own_pair = lax.optimization_barrier((ds2, pair))
     t0, ds0 = run(0, own_pair)
     back2, f2, g2 = lax.optimization_barrier((back2, f2, g2))
     f3, g3 = step(f2, 1), step(g2, -1)

time: 96.2 us -> 96.9 us (level)
  starting transfers between devices: 44.5 us -> 46.2 us
  waiting for transfers between devices: 29.5 us -> 28.4 us
    ppermute x27, starting transfers between devices: 44.5 us -> 46.2 us  [permute(): return lax.ppermute(value, AXES, pairs)]
    ppermute x27, waiting for transfers between devices: 29.5 us -> 28.4 us  [permute(): return lax.ppermute(value, AXES, pairs)]
  transfers between devices with their start and end apart: 27 -> 27, of which waited for: 14 -> 16; matrix products, arithmetic and copies ran while one was open for 2% -> 2% of each run, Pallas kernels for 13% -> 15%
where the time goes in v6:
time: 96.9 us; the launch traced here: 96.7 us
  starting transfers between devices  46.2 us (48%)
  waiting for transfers between devices  28.4 us (29%)
  Pallas kernels  17.9 us (18%)
  local copies, waits for them, and re-layouts  2.72 us (3%)
  between operations  1.13 us (1%)
    ppermute x27, starting transfers between devices, permute(): return lax.ppermute(value, AXES, pairs)  46.2 us
    ppermute x27, waiting for transfers between devices, permute(): return lax.ppermute(value, AXES, pairs)  28.4 us
    pallas_call x4, Pallas kernels, attend(): pl.pallas_call(lambda *refs: attend_body(shift, *refs), in_specs=[pl.Bloc...  9.29 us
    pallas_call x1, Pallas kernels, shards(): pl.pallas_call(delta_body, in_specs=[vmem] * 3, out_specs=[vmem] * 2, out...  2.47 us
    pallas_call x1, Pallas kernels, shards(): pl.pallas_call(gather_body, in_specs=[vmem] * 4, out_specs=pl.BlockSpec(m...  2.18 us
    pallas_call x2, Pallas kernels, dx_parts(): pl.pallas_call(dx_body, in_specs=[vmem] * 10, out_specs=[vmem] * count, o...  2.13 us
  transfers between devices with their start and end apart: 27, of which 16 were waited for; matrix products, arithmetic and copies ran while one was open for 2% of the time, Pallas kernels for 15%

profile of v6, /device:TPU:1, one launch (start us, length us, event | category | flops | bytes accessed | tf_op | source)
XLA Modules:
  0.0 96.7 jit_solution(2477345994572273955)
XLA Ops:
  0.6 3.8 %collective-permute-start = (bf16[128,2,256]{2,1,0:T(2,128)(2,1)}, bf16[128,2,256]{2,1,0:T(2,128)(2,1)S(1)}, u32[]{:S(2)}, u32[]{:S(2)}) collective-permute-start(bf16[128,2,256]{2,1,0:T(2,128)(2,1)} %param.13), channel_id=1, source_target_pairs={{0,128},{1,129},{2,130},{3,131},{4,132},{5,133},{6,134},{7,135},{8... | collective-permute-start | bytes 393224 | tf_op jit(solution)/shard_map/ppermute | solution.py:32
  5.5 2.5 %row_sums.1 = (f32[16,128]{1,0:T(8,128)}, f32[16,128]{1,0:T(8,128)}) custom-call(bf16[128,2048]{1,0:T(8,128)(2,1)} %refs_2_.7, bf16[128,2048]{1,0:T(8,128)(2,1)} %o_ref.1, f32[16,128]{1,0:T(8,128)} %lse_ref.1), custom_call_target="tpu_custom_call" | custom-call | flops 1000 | bytes 1000 | tf_op jit(solution)/shard_map/row_sums/pallas_call | solution.py:210
  8.2 2.6 %collective-permute-done.4 = bf16[1,64,512]{2,1,0:T(8,128)(2,1)S(1)} collective-permute-done((bf16[1,64,512]{2,1,0:T(8,128)(2,1)S(1)}, bf16[1,64,512]{2,1,0:T(8,128)(2,1)S(1)}, u32[]{:S(2)}, u32[]{:S(2)}) %collective-permute-start.4) | collective-permute-done | bytes 65568 | tf_op jit(solution)/shard_map/ppermute | solution.py:32
  16.4 1.5 %collective-permute-start.3 = (bf16[2,128,512]{2,1,0:T(8,128)(2,1)S(1)}, bf16[2,128,512]{2,1,0:T(8,128)(2,1)S(1)}, u32[]{:S(2)}, u32[]{:S(2)}) collective-permute-start(bf16[2,128,512]{2,1,0:T(8,128)(2,1)S(1)} %constant_dynamic-update-slice_fusion.refs_5_.refs_0_), channel_id=1, source_target_pairs={{0,64},{1,65},{2,66},{3,67},{4,68},{5,69},{6,70},{7,71},{8,72},{9,... | collective-permute-start | bytes 786440 | tf_op jit(solution)/shard_map/ppermute | solution.py:32
  18.1 1.7 %collective-permute-start.7 = (bf16[4,64,512]{2,1,0:T(8,128)(2,1)S(1)}, bf16[4,64,512]{2,1,0:T(8,128)(2,1)S(1)}, u32[]{:S(2)}, u32[]{:S(2)}) collective-permute-start(bf16[4,64,512]{2,1,0:T(8,128)(2,1)S(1)} %pad_maximum_fusion.1.refs_0_), channel_id=1, source_target_pairs={{0,2},{1,3},{2,4},{3,5},{4,6},{5,7},{6,8},{7,9},{8,10},{9,11},{10,... | collective-permute-start | bytes 786440 | tf_op jit(solution)/shard_map/ppermute | solution.py:32
  19.8 4.0 %collective-permute-start.8 = (bf16[4,64,512]{2,1,0:T(8,128)(2,1)S(1)}, bf16[4,64,512]{2,1,0:T(8,128)(2,1)S(1)}, u32[]{:S(2)}, u32[]{:S(2)}) collective-permute-start(bf16[4,64,512]{2,1,0:T(8,128)(2,1)S(1)} %pad_maximum_fusion.1.refs_0_), channel_id=1, source_target_pairs={{0,14},{1,15},{2,0},{3,1},{4,2},{5,3},{6,4},{7,5},{8,6},{9,7},{10,... | collective-permute-start | bytes 786440 | tf_op jit(solution)/shard_map/ppermute | solution.py:32
  23.8 2.3 %attend.4 = (bf16[2,128,512]{2,1,0:T(8,128)(2,1)S(1)}, bf16[256,2048]{1,0:T(8,128)(2,1)S(1)}) custom-call(s32[256]{0:T(256)S(1)} %copy-done.6, bf16[128,2048]{1,0:T(8,128)(2,1)S(1)} %copy-done.1, bf16[128,2048]{1,0:T(8,128)(2,1)S(1)} %copy-done, f32[16,128]{1,0:T(8,128)S(1)} %copy-done.5, f32[16,128]{1,0:T(8,128)S(1)} %copy-done.4, ...), custom_call_target="tpu_custom_call" | custom-call | flops 1000 | bytes 1000 | tf_op jit(solution)/shard_map/attend/pallas_call | solution.py:118
  26.2 2.3 %attend.5 = (bf16[2,128,512]{2,1,0:T(8,128)(2,1)S(1)}, bf16[256,2048]{1,0:T(8,128)(2,1)S(1)}) custom-call(s32[256]{0:T(256)S(1)} %copy-done.6, bf16[128,2048]{1,0:T(8,128)(2,1)S(1)} %copy-done.1, bf16[128,2048]{1,0:T(8,128)(2,1)S(1)} %copy-done, f32[16,128]{1,0:T(8,128)S(1)} %copy-done.5, f32[16,128]{1,0:T(8,128)S(1)} %copy-done.4, ...), custom_call_target="tpu_custom_call" | custom-call | flops 1000 | bytes 1000 | tf_op jit(solution)/shard_map/attend/pallas_call | solution.py:118
  28.7 2.3 %attend.6 = (bf16[2,128,512]{2,1,0:T(8,128)(2,1)S(1)}, bf16[256,2048]{1,0:T(8,128)(2,1)S(1)}) custom-call(s32[256]{0:T(256)S(1)} %copy-done.6, bf16[128,2048]{1,0:T(8,128)(2,1)S(1)} %copy-done.1, bf16[128,2048]{1,0:T(8,128)(2,1)S(1)} %copy-done, f32[16,128]{1,0:T(8,128)S(1)} %copy-done.5, f32[16,128]{1,0:T(8,128)S(1)} %copy-done.4, ...), custom_call_target="tpu_custom_call" | custom-call | flops 1000 | bytes 1000 | tf_op jit(solution)/shard_map/attend/pallas_call | solution.py:118
  31.1 2.6 %collective-permute-start.11 = (bf16[2,128,512]{2,1,0:T(8,128)(2,1)S(1)}, bf16[2,128,512]{2,1,0:T(8,128)(2,1)S(1)}, u32[]{:S(2)}, u32[]{:S(2)}) collective-permute-start(bf16[2,128,512]{2,1,0:T(8,128)(2,1)S(1)} %get-tuple-element.58), channel_id=1, source_target_pairs={{0,64},{1,65},{2,66},{3,67},{4,68},{5,69},{6,70},{7,71},{8,72},{9,... | collective-permute-start | bytes 786440 | tf_op jit(solution)/shard_map/ppermute | solution.py:32
  33.7 3.6 %collective-permute-start.13 = (bf16[4,64,512]{2,1,0:T(8,128)(2,1)S(1)}, bf16[4,64,512]{2,1,0:T(8,128)(2,1)S(1)}, u32[]{:S(2)}, u32[]{:S(2)}) collective-permute-start(bf16[4,64,512]{2,1,0:T(8,128)(2,1)S(1)} %collective-permute-done.8.refs_7_), channel_id=1, source_target_pairs={{0,14},{1,15},{2,0},{3,1},{4,2},{5,3},{6,4},{7,5},{8,6},{9,7},{10,... | collective-permute-start | bytes 786440 | tf_op jit(solution)/shard_map/ppermute | solution.py:32
  40.0 2.3 %attend.7 = (bf16[2,128,512]{2,1,0:T(8,128)(2,1)S(1)}, bf16[256,2048]{1,0:T(8,128)(2,1)S(1)}) custom-call(s32[256]{0:T(256)S(1)} %copy-done.6, bf16[128,2048]{1,0:T(8,128)(2,1)S(1)} %copy-done.1, bf16[128,2048]{1,0:T(8,128)(2,1)S(1)} %copy-done, f32[16,128]{1,0:T(8,128)S(1)} %copy-done.5, f32[16,128]{1,0:T(8,128)S(1)} %copy-done.4, ...), custom_call_target="tpu_custom_call" | custom-call | flops 1000 | bytes 1000 | tf_op jit(solution)/shard_map/attend/pallas_call | solution.py:118
  42.5 2.7 %collective-permute-start.16 = (bf16[4,64,512]{2,1,0:T(8,128)(2,1)S(1)}, bf16[4,64,512]{2,1,0:T(8,128)(2,1)S(1)}, u32[]{:S(2)}, u32[]{:S(2)}) collective-permute-start(bf16[4,64,512]{2,1,0:T(8,128)(2,1)S(1)} %collective-permute-done.13.refs_6_), channel_id=1, source_target_pairs={{0,14},{1,15},{2,0},{3,1},{4,2},{5,3},{6,4},{7,5},{8,6},{9,7},{10,... | collective-permute-start | bytes 786440 | tf_op jit(solution)/shard_map/ppermute | solution.py:32
  48.1 1.9 %query_grad.1 = f32[128,2048]{1,0:T(8,128)} custom-call(bf16[2,128,512]{2,1,0:T(8,128)(2,1)S(1)} %constant_dynamic-update-slice_fusion.refs_5_.refs_0_, bf16[2,128,512]{2,1,0:T(8,128)(2,1)S(1)} %collective-permute-done.1.refs_5_.refs_1_, bf16[2,128,512]{2,1,0:T(8,128)(2,1)S(1)} %collective-permute-done.2.refs_5_.refs_2_, ...), custom_call_target="tpu_custom_call" | custom-call | flops 1000 | bytes 12000000 | tf_op jit(solution)/shard_map/query_grad/pallas_call | solution.py:246
  50.0 3.0 %collective-permute-done.14 = bf16[128,512]{1,0:T(8,128)(2,1)S(1)} collective-permute-done((bf16[128,512]{1,0:T(8,128)(2,1)S(1)}, bf16[128,512]{1,0:T(8,128)(2,1)S(1)}, u32[]{:S(2)}, u32[]{:S(2)}) %collective-permute-start.14) | collective-permute-done | bytes 131104 | tf_op jit(solution)/shard_map/ppermute | solution.py:32
  53.0 3.6 %collective-permute-done.17 = bf16[128,512]{1,0:T(8,128)(2,1)S(1)} collective-permute-done((bf16[128,512]{1,0:T(8,128)(2,1)S(1)}, bf16[128,512]{1,0:T(8,128)(2,1)S(1)}, u32[]{:S(2)}, u32[]{:S(2)}) %collective-permute-start.17) | collective-permute-done | bytes 131104 | tf_op jit(solution)/shard_map/ppermute | solution.py:32
  56.7 3.5 %collective-permute-start.20 = (bf16[128,512]{1,0:T(8,128)(2,1)S(1)}, bf16[128,512]{1,0:T(8,128)(2,1)S(1)}, u32[]{:S(2)}, u32[]{:S(2)}) collective-permute-start(bf16[128,512]{1,0:T(8,128)(2,1)S(1)} %get-tuple-element.77), channel_id=1, source_target_pairs={{0,64},{1,65},{2,66},{3,67},{4,68},{5,69},{6,70},{7,71},{8,72},{9,... | collective-permute-start | bytes 393224 | tf_op jit(solution)/shard_map/ppermute | solution.py:32
  60.2 1.8 %collective-permute-done.19 = bf16[128,512]{1,0:T(8,128)(2,1)S(1)} collective-permute-done((bf16[128,512]{1,0:T(8,128)(2,1)S(1)}, bf16[128,512]{1,0:T(8,128)(2,1)S(1)}, u32[]{:S(2)}, u32[]{:S(2)}) %collective-permute-start.19) | collective-permute-done | bytes 131104 | tf_op jit(solution)/shard_map/ppermute | solution.py:32
  62.0 2.0 %collective-permute-done.20 = bf16[128,512]{1,0:T(8,128)(2,1)S(1)} collective-permute-done((bf16[128,512]{1,0:T(8,128)(2,1)S(1)}, bf16[128,512]{1,0:T(8,128)(2,1)S(1)}, u32[]{:S(2)}, u32[]{:S(2)}) %collective-permute-start.20) | collective-permute-done | bytes 131104 | tf_op jit(solution)/shard_map/ppermute | solution.py:32
  64.1 10.0 %collective-permute-start.23 = (bf16[3,128,512]{2,1,0:T(8,128)(2,1)S(1)}, bf16[3,128,512]{2,1,0:T(8,128)(2,1)S(1)}, u32[]{:S(2)}, u32[]{:S(2)}) collective-permute-start(bf16[3,128,512]{2,1,0:T(8,128)(2,1)S(1)} %pad_maximum_fusion.own_ref), channel_id=1, source_target_pairs={{0,1},{1,0},{2,3},{3,2},{4,5},{5,4},{6,7},{7,6},{8,9},{9,8},{10,11... | collective-permute-start | bytes 1179656 | tf_op jit(solution)/shard_map/ppermute | solution.py:32
  76.6 2.3 %collective-permute-start.24 = (bf16[128,1024]{1,0:T(8,128)(2,1)S(1)}, bf16[128,1024]{1,0:T(8,128)(2,1)}, u32[]{:S(2)}, u32[]{:S(2)}) collective-permute-start(bf16[128,1024]{1,0:T(8,128)(2,1)S(1)} %get-tuple-element.74), channel_id=1, source_target_pairs={{0,96},{1,97},{2,98},{3,99},{4,100},{5,101},{6,102},{7,103},{8,104... | collective-permute-start | bytes 786440 | tf_op jit(solution)/shard_map/ppermute | solution.py:32
  84.7 3.0 %collective-permute-done.25.p2 = bf16[128,1024]{1,0:T(8,128)(2,1)} collective-permute-done((bf16[128,1024]{1,0:T(8,128)(2,1)S(1)}, bf16[128,1024]{1,0:T(8,128)(2,1)}, u32[]{:S(2)}, u32[]{:S(2)}) %collective-permute-start.25) | collective-permute-done | bytes 262176 | tf_op jit(solution)/shard_map/ppermute | solution.py:32
  87.7 6.6 %collective-permute-done.26.p3 = bf16[128,1024]{1,0:T(8,128)(2,1)} collective-permute-done((bf16[128,1024]{1,0:T(8,128)(2,1)S(1)}, bf16[128,1024]{1,0:T(8,128)(2,1)}, u32[]{:S(2)}, u32[]{:S(2)}) %collective-permute-start.26) | collective-permute-done | bytes 262176 | tf_op jit(solution)/shard_map/ppermute | solution.py:32
  94.3 2.2 %join_parts.1 = bf16[128,4096]{1,0:T(8,128)(2,1)} custom-call(bf16[128,1024]{1,0:T(8,128)(2,1)} %copy-done.3, bf16[128,1024]{1,0:T(8,128)(2,1)} %collective-permute-done.24.p1, bf16[128,1024]{1,0:T(8,128)(2,1)} %collective-permute-done.25.p2, bf16[128,1024]{1,0:T(8,128)(2,1)} %collective-permute-done.26.p3), custom_call_target="tpu_custom_call" | custom-call | flops 1000 | bytes 1000 | tf_op jit(solution)/shard_map/join_parts/pallas_call | solution.py:272
  (71 shorter events, 21.4 us)
Async XLA Ops:
  0.6 7.4 %collective-permute-start = (bf16[128,2,256]{2,1,0:T(2,128)(2,1)}, bf16[128,2,256]{2,1,0:T(2,128)(2,1)S(1)}, u32[]{:S(2)}, u32[]{:S(2)}) collective-permute-start(bf16[128,2,256]{2,1,0:T(2,128)(2,1)} %param.13), channel_id=1, source_target_pairs={{0,128},{1,129},{2,130},{3,131},{4,132},{5,133},{6,134},{7,135},{8... | collective-permute-start | bytes 393224 | tf_op jit(solution)/shard_map/ppermute | solution.py:32
  5.4 5.5 %collective-permute-start.4 = (bf16[1,64,512]{2,1,0:T(8,128)(2,1)S(1)}, bf16[1,64,512]{2,1,0:T(8,128)(2,1)S(1)}, u32[]{:S(2)}, u32[]{:S(2)}) collective-permute-start(bf16[1,64,512]{2,1,0:T(8,128)(2,1)S(1)} %reshape.20), channel_id=1, source_target_pairs={{0,128},{1,129},{2,130},{3,131},{4,132},{5,133},{6,134},{7,135},{8... | collective-permute-start | bytes 196616 | tf_op jit(solution)/shard_map/ppermute | solution.py:32
  13.2 4.8 %collective-permute-start.6 = (bf16[2,64,512]{2,1,0:T(8,128)(2,1)S(1)}, bf16[2,64,512]{2,1,0:T(8,128)(2,1)S(1)}, u32[]{:S(2)}, u32[]{:S(2)}) collective-permute-start(bf16[2,64,512]{2,1,0:T(8,128)(2,1)S(1)} %pad_maximum_fusion.2), channel_id=1, source_target_pairs={{0,16},{1,17},{2,18},{3,19},{4,20},{5,21},{6,22},{7,23},{8,24},{9,... | collective-permute-start | bytes 393224 | tf_op jit(solution)/shard_map/ppermute | solution.py:32
  13.7 10.1 %collective-permute-start.1 = (bf16[2,128,512]{2,1,0:T(8,128)(2,1)S(1)}, bf16[2,128,512]{2,1,0:T(8,128)(2,1)S(1)}, u32[]{:S(2)}, u32[]{:S(2)}) collective-permute-start(bf16[2,128,512]{2,1,0:T(8,128)(2,1)S(1)} %constant_dynamic-update-slice_fusion.refs_5_.refs_0_), channel_id=1, source_target_pairs={{0,32},{1,33},{2,34},{3,35},{4,36},{5,37},{6,38},{7,39},{8,40},{9,... | collective-permute-start | bytes 786440 | tf_op jit(solution)/shard_map/ppermute | solution.py:32
  14.9 8.9 %collective-permute-start.2 = (bf16[2,128,512]{2,1,0:T(8,128)(2,1)S(1)}, bf16[2,128,512]{2,1,0:T(8,128)(2,1)S(1)}, u32[]{:S(2)}, u32[]{:S(2)}) collective-permute-start(bf16[2,128,512]{2,1,0:T(8,128)(2,1)S(1)} %constant_dynamic-update-slice_fusion.refs_5_.refs_0_), channel_id=1, source_target_pairs={{0,96},{1,97},{2,98},{3,99},{4,100},{5,101},{6,102},{7,103},{8,104... | collective-permute-start | bytes 786440 | tf_op jit(solution)/shard_map/ppermute | solution.py:32
  16.4 12.4 %collective-permute-start.3 = (bf16[2,128,512]{2,1,0:T(8,128)(2,1)S(1)}, bf16[2,128,512]{2,1,0:T(8,128)(2,1)S(1)}, u32[]{:S(2)}, u32[]{:S(2)}) collective-permute-start(bf16[2,128,512]{2,1,0:T(8,128)(2,1)S(1)} %constant_dynamic-update-slice_fusion.refs_5_.refs_0_), channel_id=1, source_target_pairs={{0,64},{1,65},{2,66},{3,67},{4,68},{5,69},{6,70},{7,71},{8,72},{9,... | collective-permute-start | bytes 786440 | tf_op jit(solution)/shard_map/ppermute | solution.py:32
  18.1 15.6 %collective-permute-start.7 = (bf16[4,64,512]{2,1,0:T(8,128)(2,1)S(1)}, bf16[4,64,512]{2,1,0:T(8,128)(2,1)S(1)}, u32[]{:S(2)}, u32[]{:S(2)}) collective-permute-start(bf16[4,64,512]{2,1,0:T(8,128)(2,1)S(1)} %pad_maximum_fusion.1.refs_0_), channel_id=1, source_target_pairs={{0,2},{1,3},{2,4},{3,5},{4,6},{5,7},{6,8},{7,9},{8,10},{9,11},{10,... | collective-permute-start | bytes 786440 | tf_op jit(solution)/shard_map/ppermute | solution.py:32
  19.8 13.9 %collective-permute-start.8 = (bf16[4,64,512]{2,1,0:T(8,128)(2,1)S(1)}, bf16[4,64,512]{2,1,0:T(8,128)(2,1)S(1)}, u32[]{:S(2)}, u32[]{:S(2)}) collective-permute-start(bf16[4,64,512]{2,1,0:T(8,128)(2,1)S(1)} %pad_maximum_fusion.1.refs_0_), channel_id=1, source_target_pairs={{0,14},{1,15},{2,0},{3,1},{4,2},{5,3},{6,4},{7,5},{8,6},{9,7},{10,... | collective-permute-start | bytes 786440 | tf_op jit(solution)/shard_map/ppermute | solution.py:32
  31.1 11.3 %collective-permute-start.11 = (bf16[2,128,512]{2,1,0:T(8,128)(2,1)S(1)}, bf16[2,128,512]{2,1,0:T(8,128)(2,1)S(1)}, u32[]{:S(2)}, u32[]{:S(2)}) collective-permute-start(bf16[2,128,512]{2,1,0:T(8,128)(2,1)S(1)} %get-tuple-element.58), channel_id=1, source_target_pairs={{0,64},{1,65},{2,66},{3,67},{4,68},{5,69},{6,70},{7,71},{8,72},{9,... | collective-permute-start | bytes 786440 | tf_op jit(solution)/shard_map/ppermute | solution.py:32
  33.7 8.7 %collective-permute-start.12 = (bf16[4,64,512]{2,1,0:T(8,128)(2,1)S(1)}, bf16[4,64,512]{2,1,0:T(8,128)(2,1)S(1)}, u32[]{:S(2)}, u32[]{:S(2)}) collective-permute-start(bf16[4,64,512]{2,1,0:T(8,128)(2,1)S(1)} %collective-permute-done.7.refs_1_), channel_id=1, source_target_pairs={{0,2},{1,3},{2,4},{3,5},{4,6},{5,7},{6,8},{7,9},{8,10},{9,11},{10,... | collective-permute-start | bytes 786440 | tf_op jit(solution)/shard_map/ppermute | solution.py:32
  33.7 8.7 %collective-permute-start.13 = (bf16[4,64,512]{2,1,0:T(8,128)(2,1)S(1)}, bf16[4,64,512]{2,1,0:T(8,128)(2,1)S(1)}, u32[]{:S(2)}, u32[]{:S(2)}) collective-permute-start(bf16[4,64,512]{2,1,0:T(8,128)(2,1)S(1)} %collective-permute-done.8.refs_7_), channel_id=1, source_target_pairs={{0,14},{1,15},{2,0},{3,1},{4,2},{5,3},{6,4},{7,5},{8,6},{9,7},{10,... | collective-permute-start | bytes 786440 | tf_op jit(solution)/shard_map/ppermute | solution.py:32
  37.3 8.4 %collective-permute-start.10 = (bf16[2,128,512]{2,1,0:T(8,128)(2,1)S(1)}, bf16[2,128,512]{2,1,0:T(8,128)(2,1)S(1)}, u32[]{:S(2)}, u32[]{:S(2)}) collective-permute-start(bf16[2,128,512]{2,1,0:T(8,128)(2,1)S(1)} %get-tuple-element.57), channel_id=1, source_target_pairs={{0,32},{1,33},{2,34},{3,35},{4,36},{5,37},{6,38},{7,39},{8,40},{9,... | collective-permute-start | bytes 786440 | tf_op jit(solution)/shard_map/ppermute | solution.py:32
  38.5 8.2 %collective-permute-start.9 = (bf16[2,128,512]{2,1,0:T(8,128)(2,1)S(1)}, bf16[2,128,512]{2,1,0:T(8,128)(2,1)S(1)}, u32[]{:S(2)}, u32[]{:S(2)}) collective-permute-start(bf16[2,128,512]{2,1,0:T(8,128)(2,1)S(1)} %get-tuple-element.56), channel_id=1, source_target_pairs={{0,96},{1,97},{2,98},{3,99},{4,100},{5,101},{6,102},{7,103},{8,104... | collective-permute-start | bytes 786440 | tf_op jit(solution)/shard_map/ppermute | solution.py:32
  42.4 10.6 %collective-permute-start.15 = (bf16[4,64,512]{2,1,0:T(8,128)(2,1)S(1)}, bf16[4,64,512]{2,1,0:T(8,128)(2,1)S(1)}, u32[]{:S(2)}, u32[]{:S(2)}) collective-permute-start(bf16[4,64,512]{2,1,0:T(8,128)(2,1)S(1)} %collective-permute-done.12.refs_2_), channel_id=1, source_target_pairs={{0,2},{1,3},{2,4},{3,5},{4,6},{5,7},{6,8},{7,9},{8,10},{9,11},{10,... | collective-permute-start | bytes 786440 | tf_op jit(solution)/shard_map/ppermute | solution.py:32
  42.5 10.5 %collective-permute-start.16 = (bf16[4,64,512]{2,1,0:T(8,128)(2,1)S(1)}, bf16[4,64,512]{2,1,0:T(8,128)(2,1)S(1)}, u32[]{:S(2)}, u32[]{:S(2)}) collective-permute-start(bf16[4,64,512]{2,1,0:T(8,128)(2,1)S(1)} %collective-permute-done.13.refs_6_), channel_id=1, source_target_pairs={{0,14},{1,15},{2,0},{3,1},{4,2},{5,3},{6,4},{7,5},{8,6},{9,7},{10,... | collective-permute-start | bytes 786440 | tf_op jit(solution)/shard_map/ppermute | solution.py:32
  47.0 6.0 %collective-permute-start.14 = (bf16[128,512]{1,0:T(8,128)(2,1)S(1)}, bf16[128,512]{1,0:T(8,128)(2,1)S(1)}, u32[]{:S(2)}, u32[]{:S(2)}) collective-permute-start(bf16[128,512]{1,0:T(8,128)(2,1)S(1)} %get-tuple-element.80), channel_id=1, source_target_pairs={{0,2},{1,3},{2,4},{3,5},{4,6},{5,7},{6,8},{7,9},{8,10},{9,11},{10,... | collective-permute-start | bytes 393224 | tf_op jit(solution)/shard_map/ppermute | solution.py:32
  47.0 9.5 %collective-permute-start.17 = (bf16[128,512]{1,0:T(8,128)(2,1)S(1)}, bf16[128,512]{1,0:T(8,128)(2,1)S(1)}, u32[]{:S(2)}, u32[]{:S(2)}) collective-permute-start(bf16[128,512]{1,0:T(8,128)(2,1)S(1)} %get-tuple-element.79), channel_id=1, source_target_pairs={{0,130},{1,131},{2,132},{3,133},{4,134},{5,135},{6,136},{7,137},{8... | collective-permute-start | bytes 393224 | tf_op jit(solution)/shard_map/ppermute | solution.py:32
  53.0 11.1 %collective-permute-start.22 = (bf16[4,64,512]{2,1,0:T(8,128)(2,1)S(1)}, bf16[4,64,512]{2,1,0:T(8,128)(2,1)S(1)}, u32[]{:S(2)}, u32[]{:S(2)}) collective-permute-start(bf16[4,64,512]{2,1,0:T(8,128)(2,1)S(1)} %collective-permute-done.15.refs_3_), channel_id=1, source_target_pairs={{0,2},{1,3},{2,4},{3,5},{4,6},{5,7},{6,8},{7,9},{8,10},{9,11},{10,... | collective-permute-start | bytes 786440 | tf_op jit(solution)/shard_map/ppermute | solution.py:32
  56.6 5.4 %collective-permute-start.19 = (bf16[128,512]{1,0:T(8,128)(2,1)S(1)}, bf16[128,512]{1,0:T(8,128)(2,1)S(1)}, u32[]{:S(2)}, u32[]{:S(2)}) collective-permute-start(bf16[128,512]{1,0:T(8,128)(2,1)S(1)} %get-tuple-element.77), channel_id=1, source_target_pairs={{0,32},{1,33},{2,34},{3,35},{4,36},{5,37},{6,38},{7,39},{8,40},{9,... | collective-permute-start | bytes 393224 | tf_op jit(solution)/shard_map/ppermute | solution.py:32
  56.7 7.3 %collective-permute-start.20 = (bf16[128,512]{1,0:T(8,128)(2,1)S(1)}, bf16[128,512]{1,0:T(8,128)(2,1)S(1)}, u32[]{:S(2)}, u32[]{:S(2)}) collective-permute-start(bf16[128,512]{1,0:T(8,128)(2,1)S(1)} %get-tuple-element.77), channel_id=1, source_target_pairs={{0,64},{1,65},{2,66},{3,67},{4,68},{5,69},{6,70},{7,71},{8,72},{9,... | collective-permute-start | bytes 393224 | tf_op jit(solution)/shard_map/ppermute | solution.py:32
  64.1 11.4 %collective-permute-start.23 = (bf16[3,128,512]{2,1,0:T(8,128)(2,1)S(1)}, bf16[3,128,512]{2,1,0:T(8,128)(2,1)S(1)}, u32[]{:S(2)}, u32[]{:S(2)}) collective-permute-start(bf16[3,128,512]{2,1,0:T(8,128)(2,1)S(1)} %pad_maximum_fusion.own_ref), channel_id=1, source_target_pairs={{0,1},{1,0},{2,3},{3,2},{4,5},{5,4},{6,7},{7,6},{8,9},{9,8},{10,11... | collective-permute-start | bytes 1179656 | tf_op jit(solution)/shard_map/ppermute | solution.py:32
  76.6 8.1 %collective-permute-start.24 = (bf16[128,1024]{1,0:T(8,128)(2,1)S(1)}, bf16[128,1024]{1,0:T(8,128)(2,1)}, u32[]{:S(2)}, u32[]{:S(2)}) collective-permute-start(bf16[128,1024]{1,0:T(8,128)(2,1)S(1)} %get-tuple-element.74), channel_id=1, source_target_pairs={{0,96},{1,97},{2,98},{3,99},{4,100},{5,101},{6,102},{7,103},{8,104... | collective-permute-start | bytes 786440 | tf_op jit(solution)/shard_map/ppermute | solution.py:32
  78.9 8.9 %collective-permute-start.25 = (bf16[128,1024]{1,0:T(8,128)(2,1)S(1)}, bf16[128,1024]{1,0:T(8,128)(2,1)}, u32[]{:S(2)}, u32[]{:S(2)}) collective-permute-start(bf16[128,1024]{1,0:T(8,128)(2,1)S(1)} %get-tuple-element.75), channel_id=1, source_target_pairs={{0,64},{1,65},{2,66},{3,67},{4,68},{5,69},{6,70},{7,71},{8,72},{9,... | collective-permute-start | bytes 786440 | tf_op jit(solution)/shard_map/ppermute | solution.py:32
  79.6 14.8 %collective-permute-start.26 = (bf16[128,1024]{1,0:T(8,128)(2,1)S(1)}, bf16[128,1024]{1,0:T(8,128)(2,1)}, u32[]{:S(2)}, u32[]{:S(2)}) collective-permute-start(bf16[128,1024]{1,0:T(8,128)(2,1)S(1)} %get-tuple-element.76), channel_id=1, source_target_pairs={{0,32},{1,33},{2,34},{3,35},{4,36},{5,37},{6,38},{7,39},{8,40},{9,... | collective-permute-start | bytes 786440 | tf_op jit(solution)/shard_map/ppermute | solution.py:32
  (12 other events, 87.1 us)
